TPU v7x, 256 devices: a whole 4x4x8 slice. The times are simulated.
256 devices in a mesh: dp: 8 (over z), expert: 32 (over y, x, core).
Axes of the slice: x: 4, y: 4, z: 8, core: 2. Of those that a mesh axis runs over, the one named last changes fastest.
Arguments:
- tokens: bfloat16 [32768, 3584], P(('dp', 'expert')), may hold values from -6 to 6
- cotangent: bfloat16 [32768, 3584], P(('dp', 'expert')), may hold values from -6 to 6
- routes: int32 [32768, 1], P(('dp', 'expert')), may hold values from 0 to 7; in each aligned block of 128 rows (0 to 127, 128 to 255, ...) at most 20 rows name the same one
- gates: float32 [32768, 1], P(('dp', 'expert')), may hold values from 0.1 to 1
- w_gate_up: bfloat16 [2, 3584, 8192], P(None, 'dp', 'expert'), may hold values from -0.09375 to 0.09375
- w_down: bfloat16 [8192, 3584], P('expert', 'dp'), may hold values from -0.1875 to 0.1875
- m_gate_up: float32 [2, 3584, 8192], P(None, 'dp', 'expert'), may hold values from -2 to 2
- v_gate_up: float32 [2, 3584, 8192], P(None, 'dp', 'expert'), may hold values from 0.01 to 1
- m_down: float32 [8192, 3584], P('expert', 'dp'), may hold values from -2 to 2
- v_down: float32 [8192, 3584], P('expert', 'dp'), may hold values from 0.01 to 1
Outputs:
- outputs: bfloat16 [32768, 3584], P(('dp', 'expert'))
- input_grads: bfloat16 [32768, 3584], P(('dp', 'expert'))
- new_w_gate_up: bfloat16 [2, 3584, 8192], P(None, 'dp', 'expert')
- new_m_gate_up: float32 [2, 3584, 8192], P(None, 'dp', 'expert')
- new_v_gate_up: float32 [2, 3584, 8192], P(None, 'dp', 'expert')
- new_w_down: bfloat16 [8192, 3584], P('expert', 'dp')
- new_m_down: float32 [8192, 3584], P('expert', 'dp')
- new_v_down: float32 [8192, 3584], P('expert', 'dp')
Inputs may be any that keep to these rules, and one draw needn't show every extreme that they name: `routes`: among the rows of one device, no expert is named more than 20 times, and one expert is named exactly 20 times in some devices' rows.
All inputs are finite; a program needn't handle non-finite values.
Results may differ from a plain program's by a relative error of at most 0.014.
Values may be sent and summed in bfloat16 or wider, within the bound.
No kernel may reach another device: no remote copies, remote signals or barrier semaphores. Data moves between devices by JAX's collectives and lax.ppermute only.
A program may use at most 128 MiB of HBM per device.

v0:
```python
import jax
import jax.numpy as jnp
from jax import lax
from jax.sharding import PartitionSpec as P

EXPERTS = 8
CAPACITY = 20


first_decay = 0.9
second_decay = 0.95
first_correction = 1.0 - 0.9**50 * 0.9**50
second_correction = 1.0 - 0.95**50 * 0.95**50
learn_rate = 0.01
adam_epsilon = 1e-08


def slot_positions(flat_routes):
    experts_iota = jnp.arange(EXPERTS, dtype=jnp.int32)
    onehot = (flat_routes[:, None] == experts_iota[None, :]).astype(jnp.int32)
    before = jnp.cumsum(onehot, axis=0) - onehot
    slots = jnp.sum(before * onehot, axis=1)
    return flat_routes * CAPACITY + slots


def adam_update(weight, moment, second, grad_sum, scale):
    grad = grad_sum * scale
    moment_new = first_decay * moment + (1.0 - first_decay) * grad
    second_new = second_decay * second + (1.0 - second_decay) * grad * grad
    update = (
        moment_new / first_correction / (jnp.sqrt(second_new / second_correction) + adam_epsilon)
    )
    weight_new = (weight.astype(jnp.float32) - learn_rate * update).astype(jnp.bfloat16)
    return (weight_new, moment_new, second_new)


def shards(
    tokens, cotangent, routes, gates, w_gate_up, w_down, m_gate_up, v_gate_up, m_down, v_down
):
    n_expert = lax.axis_size("expert")
    n_data = lax.axis_size("dp")
    group = n_expert // EXPERTS
    tok_rows, width = tokens.shape
    topk = routes.shape[1]
    places = slot_positions(routes.reshape(-1))
    gate_flat = gates.reshape(-1)
    token_rows = jnp.repeat(tokens, topk, axis=0)
    cot_rows = (
        gate_flat[:, None] * jnp.repeat(cotangent, topk, axis=0).astype(jnp.float32)
    ).astype(jnp.bfloat16)

    def pack(rows):
        buffer = jnp.zeros((EXPERTS * CAPACITY, width), jnp.bfloat16).at[places].set(rows)
        return jnp.repeat(buffer.reshape(EXPERTS, CAPACITY, width), group, axis=0)

    def unpack(received):
        summed = received.astype(jnp.float32).reshape(EXPERTS, group, CAPACITY, width).sum(axis=1)
        return summed.reshape(EXPERTS * CAPACITY, width)[places].reshape(tok_rows, topk, width)

    weights_up, weights_down = (
        lax.all_gather(w_gate_up, "dp", axis=1, tiled=True),
        lax.all_gather(w_down, "dp", axis=1, tiled=True),
    )
    got_x = lax.all_to_all(pack(token_rows), "expert", split_axis=0, concat_axis=0, tiled=True)
    inputs = got_x.reshape(n_expert * CAPACITY, width)
    pre = jnp.einsum("rc,gcf->grf", inputs, weights_up, preferred_element_type=jnp.float32)
    act_in = pre[0]
    linear = pre[1]
    sig = jax.nn.sigmoid(act_in)
    hidden = (act_in * sig * linear).astype(jnp.bfloat16)
    out_part = jnp.dot(hidden, weights_down, preferred_element_type=jnp.float32).astype(
        jnp.bfloat16
    )
    out_part = out_part.reshape(n_expert, CAPACITY, width)
    back_out = lax.all_to_all(out_part, "expert", split_axis=0, concat_axis=0, tiled=True)
    outputs = jnp.sum(gates[:, :, None] * unpack(back_out), axis=1).astype(jnp.bfloat16)
    got_y = lax.all_to_all(pack(cot_rows), "expert", split_axis=0, concat_axis=0, tiled=True)
    grads_in = got_y.reshape(n_expert * CAPACITY, width)
    d_hidden = lax.dot_general(
        grads_in, weights_down, (((1,), (1,)), ((), ())), preferred_element_type=jnp.float32
    )
    d_act = (d_hidden * linear * sig * (1.0 + act_in * (1.0 - sig))).astype(jnp.bfloat16)
    d_lin = (d_hidden * act_in * sig).astype(jnp.bfloat16)
    d_pre = jnp.stack([d_act, d_lin])
    in_part = jnp.einsum(
        "grf,gcf->rc", d_pre, weights_up, preferred_element_type=jnp.float32
    ).astype(jnp.bfloat16)
    in_part = in_part.reshape(n_expert, CAPACITY, width)
    grad_up = jnp.einsum("rc,grf->gcf", inputs, d_pre, preferred_element_type=jnp.float32)
    grad_down = lax.dot_general(
        hidden, grads_in, (((0,), (0,)), ((), ())), preferred_element_type=jnp.float32
    )
    owned_up, owned_down = (
        lax.psum_scatter(
            grad_up.astype(jnp.bfloat16), "dp", scatter_dimension=1, tiled=True
        ).astype(jnp.float32),
        lax.psum_scatter(
            grad_down.astype(jnp.bfloat16), "dp", scatter_dimension=1, tiled=True
        ).astype(jnp.float32),
    )
    back_in = lax.all_to_all(in_part, "expert", split_axis=0, concat_axis=0, tiled=True)
    input_grads = jnp.sum(unpack(back_in), axis=1).astype(jnp.bfloat16)
    scale = (tok_rows * n_data * n_expert * topk / EXPERTS) ** (-0.5)
    new_wu, new_mu, new_vu = adam_update(w_gate_up, m_gate_up, v_gate_up, owned_up, scale)
    new_wd, new_md, new_vd = adam_update(w_down, m_down, v_down, owned_down, scale)
    return (outputs, input_grads, new_wu, new_mu, new_vu, new_wd, new_md, new_vd)


def solution(mesh):
    placed = (
        P(("dp", "expert"), None),
        P(("dp", "expert"), None),
        P(("dp", "expert"), None),
        P(("dp", "expert"), None),
        P(None, "dp", "expert"),
        P("expert", "dp"),
        P(None, "dp", "expert"),
        P(None, "dp", "expert"),
        P("expert", "dp"),
        P("expert", "dp"),
    )
    return jax.shard_map(
        shards,
        mesh=mesh,
        in_specs=placed,
        out_specs=(
            P(("dp", "expert"), None),
            P(("dp", "expert"), None),
            P(None, "dp", "expert"),
            P(None, "dp", "expert"),
            P(None, "dp", "expert"),
            P("expert", "dp"),
            P("expert", "dp"),
            P("expert", "dp"),
        ),
        check_vma=False,
    )
```

profile of v0, /device:TPU:1, one launch (start us, length us, event | category | flops | bytes accessed | tf_op | source)
XLA Modules:
  0.0 390.5 jit_solution(8428602322410248086)
XLA Ops:
  7.2 0.7 fusion.27
  7.9 0.2 reduce_window_sum.11
  8.1 0.8 select_reduce_fusion
  8.9 0.7 fusion.28
  9.6 2.8 scatter_custom_fusion
  12.4 0.3 reshape.77
  12.7 2.9 broadcast_in_dim.4
  15.6 8.8 %all-to-all-start = ((bf16[32,20,3584]{2,1,0:T(8,128)(2,1)}), bf16[32,20,3584]{2,1,0:T(8,128)(2,1)}, u32[]{:S(2)}, u32[]{:S(2)}) async-start(bf16[32,20,3584]{2,1,0:T(8,128)(2,1)} %bitcast.84), calls=%async_computation | async-start | bytes 11010048 | tf_op jit(solution)/shard_map/all_to_all | solution.py:64
  24.4 0.0 all-gather.3.cloned.1.call-start
  24.4 0.7 all-gather.3.cloned.1.call-update
  25.1 0.0 copy-done.2
  25.1 0.0 copy-done.6
  25.1 2.3 scatter_custom_fusion.1
  27.4 0.3 reshape.84
  27.7 61.0 %all-to-all-done = bf16[32,20,3584]{2,1,0:T(8,128)(2,1)} async-done(((bf16[32,20,3584]{2,1,0:T(8,128)(2,1)}), bf16[32,20,3584]{2,1,0:T(8,128)(2,1)}, u32[]{:S(2)}, u32[]{:S(2)}) %all-to-all-start) | async-done | bytes 4587552 | tf_op jit(solution)/shard_map/all_to_all | solution.py:64
  88.7 2.8 broadcast_in_dim.5
  91.5 9.1 %all-to-all-start.2 = ((bf16[32,20,3584]{2,1,0:T(8,128)(2,1)}), bf16[32,20,3584]{2,1,0:T(8,128)(2,1)}, u32[]{:S(2)}, u32[]{:S(2)}) async-start(bf16[32,20,3584]{2,1,0:T(8,128)(2,1)} %bitcast.85), calls=%async_computation.2 | async-start | bytes 11010048 | tf_op jit(solution)/shard_map/all_to_all | solution.py:77
  100.6 0.0 all-gather.5.cloned.1.call-start
  100.7 0.7 all-gather.5.cloned.1.call-update
  101.4 7.3 %reshape.127 = bf16[640,3584,1]{1,0,2:T(8,128)(2,1)} reshape(bf16[32,20,3584]{2,1,0:T(8,128)(2,1)} %all-to-all-done) | data formatting | bytes 9175040 | tf_op jit(solution)/shard_map/reshape | solution.py:65
  108.7 56.4 %all-to-all-done.2 = bf16[32,20,3584]{2,1,0:T(8,128)(2,1)} async-done(((bf16[32,20,3584]{2,1,0:T(8,128)(2,1)}), bf16[32,20,3584]{2,1,0:T(8,128)(2,1)}, u32[]{:S(2)}, u32[]{:S(2)}) %all-to-all-start.2) | async-done | bytes 4587552 | tf_op jit(solution)/shard_map/all_to_all | solution.py:77
  165.0 7.3 %reshape.86 = bf16[640,3584]{1,0:T(8,128)(2,1)} reshape(bf16[32,20,3584]{2,1,0:T(8,128)(2,1)} %all-to-all-done.2) | data formatting | bytes 9175040 | tf_op jit(solution)/shard_map/reshape | solution.py:78
  172.3 6.0 %convolution_bitcast_fusion = f32[2,640,256]{2,1,0:T(8,128)S(1)} fusion(bf16[640,3584,1]{1,0,2:T(8,128)(2,1)} %reshape.127, bf16[2,3584,256]{2,1,0:T(8,128)(2,1)} %all-gather.3.cloned.1.call-done), kind=kOutput, calls=%fused_computation.13 | convolution fusion | flops 2348810240 | bytes 9568256 | tf_op jit(solution)/shard_map/rc,gcf->grf/dot_general | solution.py:66
  178.3 0.0 all-gather.5.cloned.1.call-done
  178.3 0.0 copy-start.7
  178.3 4.5 %fusion.26 = (bf16[1,640,256]{2,1,0:T(8,128)(2,1)S(1)}, bf16[1,640,256]{2,1,0:T(8,128)(2,1)S(1)}) fusion(f32[2,640,256]{2,1,0:T(8,128)S(1)} %convolution_bitcast_fusion, bf16[640,3584]{1,0:T(8,128)(2,1)} %reshape.86, bf16[256,3584]{0,1:T(8,128)(2,1)} %all-gather.5.cloned.1.call-done), kind=kOutput, calls=%fused_computation.54 | convolution fusion | flops 1176535040 | bytes 8388608 | tf_op jit(solution)/shard_map/dot_general | solution.py:79
  182.8 0.0 copy-done.7
  182.8 4.7 %bitcast_convert_fusion = bf16[640,3584]{1,0:T(8,128)(2,1)} fusion(bf16[2,3584,256]{2,1,0:T(8,128)(2,1)S(1)} %copy-done.7, bf16[1,640,256]{2,1,0:T(8,128)(2,1)S(1)} %get-tuple-element.39, bf16[1,640,256]{2,1,0:T(8,128)(2,1)S(1)} %get-tuple-element.38), kind=kOutput, calls=%fused_computation.6 | convolution fusion | flops 2351431680 | bytes 8912896 | tf_op jit(solution)/shard_map/grf,gcf->rc/dot_general | solution.py:85
  187.5 7.2 %reshape.87 = bf16[32,20,3584]{2,1,0:T(8,128)(2,1)} reshape(bf16[640,3584]{1,0:T(8,128)(2,1)} %bitcast_convert_fusion) | data formatting | bytes 9175040 | tf_op jit(solution)/shard_map/reshape | solution.py:88
  194.7 9.2 %all-to-all-start.3 = ((bf16[32,20,3584]{2,1,0:T(8,128)(2,1)}), bf16[32,20,3584]{2,1,0:T(8,128)(2,1)}, u32[]{:S(2)}, u32[]{:S(2)}) async-start(bf16[32,20,3584]{2,1,0:T(8,128)(2,1)} %reshape.87), calls=%async_computation.3 | async-start | bytes 11010048 | tf_op jit(solution)/shard_map/all_to_all | solution.py:101
  203.9 0.2 all-reduce.3.cloned.1.call-start
  204.1 6.8 %fusion = bf16[2,3584,256]{1,2,0:T(8,128)(2,1)} fusion(bf16[640,3584,1]{1,0,2:T(8,128)(2,1)} %reshape.127, bf16[1,640,256]{2,1,0:T(8,128)(2,1)S(1)} %get-tuple-element.39, bf16[1,640,256]{2,1,0:T(8,128)(2,1)S(1)} %get-tuple-element.38), kind=kOutput, calls=%fused_computation.9 | convolution fusion | flops 2350972928 | bytes 8912896 | tf_op jit(solution)/shard_map/rc,grf->gcf/dot_general | solution.py:89
  211.0 9.9 %copy.41 = bf16[2,3584,256]{2,0,1:T(2,128)(2,1)} copy(bf16[2,3584,256]{1,2,0:T(8,128)(2,1)} %fusion) | data formatting | bytes 7340032 | tf_op jit(solution)/shard_map/convert_element_type | solution.py:95
  220.9 0.0 all-reduce.3.cloned.1.call-update
  220.9 0.0 copy-start.8
  220.9 0.0 reduce-scatter.2.cloned.1.call-start
  220.9 5.7 %convolution_convert_fusion.2 = bf16[256,3584]{0,1:T(8,128)(2,1)} fusion(bf16[640,3584]{1,0:T(8,128)(2,1)} %reshape.86, f32[2,640,256]{2,1,0:T(8,128)S(1)} %convolution_bitcast_fusion), kind=kOutput, calls=%fused_computation.10 | convolution fusion | flops 1176305664 | bytes 7733248 | tf_op jit(solution)/shard_map/dot_general | solution.py:90
  226.6 0.0 reduce-scatter.2.cloned.1.call-update
  226.6 0.0 copy-done.8
  226.7 3.5 convolution_convert_fusion
  230.1 7.3 %reshape.80 = bf16[32,20,3584]{2,1,0:T(8,128)(2,1)} reshape(bf16[640,3584]{1,0:T(8,128)(2,1)} %convolution_convert_fusion) | data formatting | bytes 9175040 | tf_op jit(solution)/shard_map/reshape | solution.py:74
  237.5 30.8 %all-to-all-done.3 = bf16[32,20,3584]{2,1,0:T(8,128)(2,1)} async-done(((bf16[32,20,3584]{2,1,0:T(8,128)(2,1)}), bf16[32,20,3584]{2,1,0:T(8,128)(2,1)}, u32[]{:S(2)}, u32[]{:S(2)}) %all-to-all-start.3) | async-done | bytes 4587552 | tf_op jit(solution)/shard_map/all_to_all | solution.py:101
  268.3 9.2 %all-to-all-start.1 = ((bf16[32,20,3584]{2,1,0:T(8,128)(2,1)}), bf16[32,20,3584]{2,1,0:T(8,128)(2,1)}, u32[]{:S(2)}, u32[]{:S(2)}) async-start(bf16[32,20,3584]{2,1,0:T(8,128)(2,1)} %reshape.80), calls=%async_computation.1 | async-start | bytes 11010048 | tf_op jit(solution)/shard_map/all_to_all | solution.py:75
  277.5 0.0 copy-start
  277.5 0.0 copy-start.3
  277.5 0.0 copy-start.4
  277.6 0.0 copy-done.9
  277.6 0.6 dynamic-slice
  278.9 44.3 %all-reduce.3.cloned.1.call-done = bf16[2,3584,256]{2,0,1:T(2,128)(2,1)} async-done(((bf16[2,3584,256]{2,0,1:T(2,128)(2,1)}), bf16[2,3584,256]{2,0,1:T(2,128)(2,1)}) %all-reduce.3.cloned.1.call-update) | async-done | bytes 3670032
  323.2 1.3 constant_dynamic-slice_fusion
  324.6 37.1 %reduce-scatter.2.cloned.1.call-done = bf16[256,448]{0,1:T(8,128)(2,1)} async-done(((bf16[256,3584]{0,1:T(8,128)(2,1)}), bf16[256,448]{0,1:T(8,128)(2,1)}) %reduce-scatter.2.cloned.1.call-update) | async-done | bytes 229392 | tf_op jit(solution)/shard_map/reduce_scatter | solution.py:97
  361.7 0.0 copy-done.1
  361.7 0.0 copy-done.5
  361.7 2.4 subtract_convert_fusion.1
  364.1 0.0 copy-done
  364.1 1.9 subtract_convert_fusion
  366.0 3.4 convert_reduce_fusion
  369.4 0.3 reshape.90
  369.7 0.0 all-to-all-done.1
  369.7 5.3 %convert_reduce_fusion.1 = f32[8,20,3584]{2,1,0:T(8,128)} fusion(bf16[32,20,3584]{2,1,0:T(8,128)(2,1)} %all-to-all-done.1), kind=kLoop, calls=%fused_computation.5 | loop fusion | flops 4014080 | bytes 6881280 | tf_op jit(solution)/shard_map/reduce_sum | solution.py:57
  375.0 1.9 reshape.83
  376.9 2.0 gather_fusion.1
  378.9 2.4 gather_fusion
  381.4 2.6 multiply_convert_fusion.1
  (9 shorter events, 0.0 us)
Async XLA Ops:
  15.6 9.5 %copy-start.2 = (bf16[128,3584]{1,0:T(8,128)(2,1)S(1)}, bf16[128,3584]{1,0:T(8,128)(2,1)}, u32[]{:S(2)}) copy-start(bf16[128,3584]{1,0:T(8,128)(2,1)} %param.11) | copy-start | bytes 2752516
  15.6 9.5 %copy-start.6 = (f32[128,1]{0,1:T(1,128)S(1)}, f32[128,1]{0,1:T(1,128)}, u32[]{:S(2)}) copy-start(f32[128,1]{0,1:T(1,128)} %param.13) | copy-start | bytes 1540
  15.6 73.1 %all-to-all-start = ((bf16[32,20,3584]{2,1,0:T(8,128)(2,1)}), bf16[32,20,3584]{2,1,0:T(8,128)(2,1)}, u32[]{:S(2)}, u32[]{:S(2)}) async-start(bf16[32,20,3584]{2,1,0:T(8,128)(2,1)} %bitcast.84), calls=%async_computation | async-start | bytes 11010048 | tf_op jit(solution)/shard_map/all_to_all | solution.py:64
  24.4 148.0 %all-gather.3.cloned.1.call-start = ((), (), s32[]{:S(2)}) async-start(), calls=%async_computation.5 | async-start | bytes 4128768 | tf_op jit(solution)/shard_map/all_gather | solution.py:61
  91.5 73.5 %all-to-all-start.2 = ((bf16[32,20,3584]{2,1,0:T(8,128)(2,1)}), bf16[32,20,3584]{2,1,0:T(8,128)(2,1)}, u32[]{:S(2)}, u32[]{:S(2)}) async-start(bf16[32,20,3584]{2,1,0:T(8,128)(2,1)} %bitcast.85), calls=%async_computation.2 | async-start | bytes 11010048 | tf_op jit(solution)/shard_map/all_to_all | solution.py:77
  100.6 77.7 %all-gather.5.cloned.1.call-start = ((), (), s32[]{:S(2)}) async-start(), calls=%async_computation.6 | async-start | bytes 2064384 | tf_op jit(solution)/shard_map/all_gather | solution.py:62
  178.3 4.5 %copy-start.7 = (bf16[2,3584,256]{2,1,0:T(8,128)(2,1)S(1)}, bf16[2,3584,256]{2,1,0:T(8,128)(2,1)}, u32[]{:S(2)}) copy-start(bf16[2,3584,256]{2,1,0:T(8,128)(2,1)} %all-gather.3.cloned.1.call-done) | copy-start | bytes 11010052
  194.7 73.6 %all-to-all-start.3 = ((bf16[32,20,3584]{2,1,0:T(8,128)(2,1)}), bf16[32,20,3584]{2,1,0:T(8,128)(2,1)}, u32[]{:S(2)}, u32[]{:S(2)}) async-start(bf16[32,20,3584]{2,1,0:T(8,128)(2,1)} %reshape.87), calls=%async_computation.3 | async-start | bytes 11010048 | tf_op jit(solution)/shard_map/all_to_all | solution.py:101
  203.9 119.3 %all-reduce.3.cloned.1.call-start = ((), (), s32[]{:S(2)}) async-start(), calls=%async_computation.8 | async-start | bytes 7340032
  220.9 5.8 %copy-start.8 = (bf16[256,3584]{0,1:T(8,128)(2,1)S(1)}, bf16[256,3584]{0,1:T(8,128)(2,1)}, u32[]{:S(2)}) copy-start(bf16[256,3584]{0,1:T(8,128)(2,1)} %all-gather.5.cloned.1.call-done) | copy-start | bytes 5505028
  220.9 140.8 %reduce-scatter.2.cloned.1.call-start = ((), (), s32[]{:S(2)}) async-start(), calls=%async_computation.7 | async-start | bytes 2064384 | tf_op jit(solution)/shard_map/reduce_scatter | solution.py:97
  237.5 40.1 %copy-start.9 = (u32[256]{0:T(256)S(1)}, u32[256]{0:T(256)}, u32[]{:S(2)}) copy-start(u32[256]{0:T(256)} %constant.58) | copy-start | bytes 3076
  237.5 124.2 %copy-start.1 = (bf16[256,448]{0,1:T(8,128)(2,1)S(1)}, bf16[256,448]{0,1:T(8,128)(2,1)}, u32[]{:S(2)}) copy-start(bf16[256,448]{0,1:T(8,128)(2,1)} %param.15) | copy-start | bytes 688132
  237.5 124.2 %copy-start.5 = (f32[256,448]{0,1:T(8,128)S(1)}, f32[256,448]{0,1:T(8,128)}, u32[]{:S(2)}) copy-start(f32[256,448]{0,1:T(8,128)} %param.18) | copy-start | bytes 1376260
  268.3 101.4 %all-to-all-start.1 = ((bf16[32,20,3584]{2,1,0:T(8,128)(2,1)}), bf16[32,20,3584]{2,1,0:T(8,128)(2,1)}, u32[]{:S(2)}, u32[]{:S(2)}) async-start(bf16[32,20,3584]{2,1,0:T(8,128)(2,1)} %reshape.80), calls=%async_computation.1 | async-start | bytes 11010048 | tf_op jit(solution)/shard_map/all_to_all | solution.py:75
  277.5 86.6 %copy-start = (bf16[2,448,256]{2,1,0:T(8,128)(2,1)S(1)}, bf16[2,448,256]{2,1,0:T(8,128)(2,1)}, u32[]{:S(2)}) copy-start(bf16[2,448,256]{2,1,0:T(8,128)(2,1)} %param.14) | copy-start | bytes 1376260
  277.5 86.5 %copy-start.3 = (f32[2,448,256]{2,1,0:T(8,128)S(1)}, f32[2,448,256]{2,1,0:T(8,128)}, u32[]{:S(2)}) copy-start(f32[2,448,256]{2,1,0:T(8,128)} %param.16) | copy-start | bytes 2752516
  277.5 86.5 %copy-start.4 = (f32[2,448,256]{2,1,0:T(8,128)S(1)}, f32[2,448,256]{2,1,0:T(8,128)}, u32[]{:S(2)}) copy-start(f32[2,448,256]{2,1,0:T(8,128)} %param.17) | copy-start | bytes 2752516
Sparse Core Ops, SparseCore 0:
  27.0 52.4 all-gather.2
  103.3 39.6 all-gather.4
  221.0 102.1 all-reduce.2
  325.6 36.0 reduce-scatter.1
where the time goes:
time: 395 us; the launch traced here: 390 us
  waiting for transfers between devices  231 us (58%)
  local copies, waits for them, and re-layouts  56.7 us (14%)
  starting transfers between devices  36.7 us (9%)
  matrix products  31.1 us (8%)
  other arithmetic  20.2 us (5%)
  between operations  14.7 us (4%)
    all_to_all x1, waiting for transfers between devices, shards(): lax.all_to_all(pack(token_rows), 'expert', split_axis=0, concat_axis=0, t...  61 us
    all_to_all x1, waiting for transfers between devices, shards(): lax.all_to_all(pack(cot_rows), 'expert', split_axis=0, concat_axis=0, til...  56.4 us
    unnamed x5, waiting for transfers between devices  45.7 us
    reduce_scatter x1, waiting for transfers between devices, shards(): lax.psum_scatter(grad_down.astype(jnp.bfloat16), 'dp', scatter_dimension=...  37.1 us
    all_to_all x1, waiting for transfers between devices, shards(): lax.all_to_all(in_part, 'expert', split_axis=0, concat_axis=0, tiled=True)  30.8 us
    convert_element_type x1, local copies, waits for them, and re-layouts, shards(): grad_up.astype(jnp.bfloat16)  9.87 us
    all_to_all x1, starting transfers between devices, shards(): lax.all_to_all(out_part, 'expert', split_axis=0, concat_axis=0, tiled=True)  9.2 us
    all_to_all x1, starting transfers between devices, shards(): lax.all_to_all(in_part, 'expert', split_axis=0, concat_axis=0, tiled=True)  9.2 us
  transfers between devices with their start and end apart: 8, of which 5 were waited for; matrix products, arithmetic and copies ran while one was open for 18% of the time, Pallas kernels for 0%

commit v1 on v0

v1 whole, which is shorter than its diff:
```python
import jax
import jax.numpy as jnp
from jax import lax
from jax.sharding import Mesh, PartitionSpec as P

EXPERTS = 8
CAPACITY = 20


first_decay = 0.9
second_decay = 0.95
first_correction = 1.0 - 0.9**50 * 0.9**50
second_correction = 1.0 - 0.95**50 * 0.95**50
learn_rate = 0.01
adam_epsilon = 1e-08

SWAP = [(0, 1), (1, 0)]


def slots_of(flat_routes):
    n = flat_routes.shape[0]
    onehot = (flat_routes[:, None] == jnp.arange(EXPERTS, dtype=jnp.int32)[None, :]).astype(jnp.bfloat16)
    earlier = (jnp.arange(n)[:, None] > jnp.arange(n)[None, :]).astype(jnp.bfloat16)
    before = jnp.dot(earlier, onehot, preferred_element_type=jnp.float32)
    return jnp.sum(before * onehot.astype(jnp.float32), axis=1).astype(jnp.int32)


def adam_update(weight, moment, second, grad_sum, scale):
    grad = grad_sum * scale
    moment_new = first_decay * moment + (1.0 - first_decay) * grad
    second_new = second_decay * second + (1.0 - second_decay) * grad * grad
    update = (
        moment_new / first_correction / (jnp.sqrt(second_new / second_correction) + adam_epsilon)
    )
    weight_new = (weight.astype(jnp.float32) - learn_rate * update).astype(jnp.bfloat16)
    return (weight_new, moment_new, second_new)


def dot(a, b, dims=((1,), (0,))):
    return lax.dot_general(a, b, (dims, ((), ())), preferred_element_type=jnp.float32)


def shards(
    tokens, cotangent, routes, gates, w_gate_up, w_down, m_gate_up, v_gate_up, m_down, v_down
):
    n_data, n_chip, n_core = (lax.axis_size(a) for a in ("z", "p", "c"))
    pair = n_chip // EXPERTS
    tok_rows, width = tokens.shape
    half = width // n_core
    block = n_core * CAPACITY
    hid = w_down.shape[0]
    c = lax.axis_index("c")
    orders = [
        [((z + k * n_data // n_core) % n_data) * n_core + k for z in range(n_data)]
        for k in range(n_core)
    ]

    owned = jnp.concatenate([w_gate_up[0], w_gate_up[1], w_down.T], axis=1)
    weights = lax.all_gather(owned, ("z", "c"), axis=0, tiled=True, axis_index_groups=orders)
    w_m, w_o = weights[:half], weights[half:]

    flat = routes.reshape(-1)
    place = flat * block + c * CAPACITY + slots_of(flat)
    info = jnp.concatenate([place.astype(jnp.float32)[:, None], gates], axis=1)
    info2 = jnp.concatenate([info, lax.ppermute(info, "c", SWAP)], axis=0)
    place2 = info2[:, 0].astype(jnp.int32)
    gate2 = info2[:, 1:2]
    cot = (gates * cotangent.astype(jnp.float32)).astype(jnp.bfloat16)

    def half_of(array, k):
        return lax.dynamic_slice_in_dim(array, k * half, half, axis=1)

    def both_of(k):
        return jnp.concatenate([half_of(tokens, k), half_of(cot, k)], axis=1)

    rows2 = jnp.concatenate([both_of(c), lax.ppermute(both_of(1 - c), "c", SWAP)], axis=0)
    row_id = lax.broadcasted_iota(jnp.int32, (EXPERTS, pair, block), 0) * block + (
        lax.broadcasted_iota(jnp.int32, (EXPERTS, pair, block), 2)
    )
    row_id = row_id.reshape(-1)
    pick = (row_id[:, None] == place2[None, :]).astype(jnp.bfloat16)
    packed = dot(pick, rows2).astype(jnp.bfloat16).reshape(n_chip, block, width)
    got = lax.all_to_all(packed, "p", split_axis=0, concat_axis=0, tiled=True)
    mine = got.reshape(n_chip * block, width)
    other = lax.ppermute(mine, "c", SWAP)
    x_m, y_m = mine[:, :half], mine[:, half:]
    x_o, y_o = other[:, :half], other[:, half:]

    pre = dot(x_m, w_m[:, : 2 * hid]) + dot(x_o, w_o[:, : 2 * hid])
    d_hidden = dot(y_m, w_m[:, 2 * hid :]) + dot(y_o, w_o[:, 2 * hid :])
    act_in, linear = pre[:, :hid], pre[:, hid:]
    sig = jax.nn.sigmoid(act_in)
    hidden = (act_in * sig * linear).astype(jnp.bfloat16)
    d_act = (d_hidden * linear * sig * (1.0 + act_in * (1.0 - sig))).astype(jnp.bfloat16)
    d_lin = (d_hidden * act_in * sig).astype(jnp.bfloat16)
    d_pre = jnp.concatenate([d_act, d_lin], axis=1)

    def parts(w):
        out = dot(hidden, w[:, 2 * hid :], ((1,), (1,)))
        inp = dot(d_pre, w[:, : 2 * hid], ((1,), (1,)))
        return jnp.concatenate([out.astype(jnp.bfloat16), inp.astype(jnp.bfloat16)], axis=1)

    from_other = lax.ppermute(parts(w_o), "c", SWAP)
    back = (parts(w_m).astype(jnp.float32) + from_other.astype(jnp.float32)).astype(jnp.bfloat16)

    def grads(x, y):
        up = dot(x, d_pre, ((0,), (0,))).astype(jnp.bfloat16)
        down = dot(y, hidden, ((0,), (0,))).astype(jnp.bfloat16)
        return jnp.concatenate([up, down], axis=1)

    grad = jnp.concatenate([grads(x_m, y_m), grads(x_o, y_o)], axis=0)
    grad = lax.psum_scatter(
        grad, ("z", "c"), scatter_dimension=0, tiled=True, axis_index_groups=orders
    ).astype(jnp.float32)

    back = lax.all_to_all(
        back.reshape(n_chip, block, width), "p", split_axis=0, concat_axis=0, tiled=True
    ).reshape(n_chip * block, width)
    unpick = (place2[:, None] == row_id[None, :]).astype(jnp.bfloat16)
    summed = dot(unpick, back)
    result = jnp.concatenate([summed[:, :half] * gate2, summed[:, half:]], axis=1).astype(jnp.bfloat16)
    near = result[:tok_rows]
    far = lax.ppermute(result[tok_rows:], "c", SWAP)

    def joined(cols):
        a, b = near[:, cols], far[:, cols]
        first = jnp.where(c == 0, a, b)
        second = jnp.where(c == 0, b, a)
        return jnp.concatenate([first, second], axis=1)

    outputs, input_grads = joined(slice(0, half)), joined(slice(half, width))
    scale = (tok_rows * n_data * n_chip * n_core * routes.shape[1] / EXPERTS) ** (-0.5)
    grad_up = jnp.stack([grad[:, :hid], grad[:, hid : 2 * hid]])
    new_wu, new_mu, new_vu = adam_update(w_gate_up, m_gate_up, v_gate_up, grad_up, scale)
    new_wd, new_md, new_vd = adam_update(w_down, m_down, v_down, grad[:, 2 * hid :].T, scale)
    return (outputs, input_grads, new_wu, new_mu, new_vu, new_wd, new_md, new_vd)


def solution(mesh):
    n_data, n_expert = (mesh.shape[a] for a in ("dp", "expert"))
    cores = Mesh(mesh.devices.reshape(n_data, n_expert // 2, 2), ("z", "p", "c"))
    rows = P(("z", "p", "c"), None)
    up, down = P(None, "z", ("p", "c")), P(("p", "c"), "z")
    return jax.shard_map(
        shards,
        mesh=cores,
        in_specs=(rows, rows, rows, rows, up, down, up, up, down, down),
        out_specs=(rows, rows, up, up, up, down, down, down),
        check_vma=False,
    )
```

time: 395 us -> 254 us (0.64)
  waiting for transfers between devices: 231 us -> 2.9 us
  blocking collectives: 0 us -> 121 us
  starting transfers between devices: 36.7 us -> 7.44 us
  local copies, waits for them, and re-layouts: 56.7 us -> 31.3 us
  other arithmetic: 20.2 us -> 40 us
  matrix products: 31.1 us -> 36 us
    all_to_all x4 -> x0, waiting for transfers between devices: 148 us -> none  [the longest x1 61 us: shards(): lax.all_to_all(pack(token_rows), 'expert', split_axis=0, concat_axis=0, t...]
    all_to_all x0 -> x2, blocking collectives: none -> 121 us  [the longest x1 61.3 us: shards(): lax.all_to_all(back.reshape(n_chip, block, width), 'p', split_axis=0, con...]
    unnamed x5 -> x3, waiting for transfers between devices: 45.7 us -> 0.03 us
    reduce_scatter x1 -> x0, waiting for transfers between devices: 37.1 us -> none  [shards(): lax.psum_scatter(grad_down.astype(jnp.bfloat16), 'dp', scatter_dimension=...]
    all_to_all x4 -> x0, starting transfers between devices: 36.3 us -> none  [the longest x1 9.2 us: shards(): lax.all_to_all(out_part, 'expert', split_axis=0, concat_axis=0, tiled=True)]
    reshape x8 -> x0, local copies, waits for them, and re-layouts: 31.9 us -> none  [the longest x1 7.35 us: shards(): out_part = out_part.reshape(n_expert, CAPACITY, width)]
    concatenate x0 -> x9, other arithmetic: none -> 31.5 us  [the longest x1 24.3 us: shards(): grad = jnp.concatenate([grads(x_m, y_m), grads(x_o, y_o)], axis=0)]
    unnamed x22 -> x32, local copies, waits for them, and re-layouts: 1.96 us -> 29.7 us
  transfers between devices with their start and end apart: 8 -> 7, of which waited for: 5 -> 3; matrix products, arithmetic and copies ran while one was open for 18% -> 31% of each run, Pallas kernels for 0% -> 0%
where the time goes in v1:
time: 254 us; the launch traced here: 253 us
  blocking collectives  121 us (48%)
  other arithmetic  40 us (16%)
  matrix products  36 us (14%)
  local copies, waits for them, and re-layouts  31.3 us (12%)
  between operations  14.4 us (6%)
  starting transfers between devices  7.44 us (3%)
  waiting for transfers between devices  2.9 us (1%)
    all_to_all x1, blocking collectives, shards(): lax.all_to_all(back.reshape(n_chip, block, width), 'p', split_axis=0, con...  61.3 us
    all_to_all x1, blocking collectives, shards(): got = lax.all_to_all(packed, 'p', split_axis=0, concat_axis=0, tiled=True)  59.4 us
    dot_general x14, matrix products, dot(): lax.dot_general(a, b, (dims, ((), ())), preferred_element_type=jnp.float32)  35.9 us
    unnamed x32, local copies, waits for them, and re-layouts  29.7 us
    concatenate x1, other arithmetic, shards(): grad = jnp.concatenate([grads(x_m, y_m), grads(x_o, y_o)], axis=0)  24.3 us
  transfers between devices with their start and end apart: 7, of which 3 were waited for; matrix products, arithmetic and copies ran while one was open for 31% of the time, Pallas kernels for 0%

profile of v1, /device:TPU:1, one launch (start us, length us, event | category | flops | bytes accessed | tf_op | source)
XLA Modules:
  0.0 252.7 jit_solution(15040216984263756690)
XLA Ops:
  7.2 0.0 all-gather.2.cloned.1.call-start
  7.2 1.2 slice_bitcast_fusion.3
  8.4 1.8 pad_maximum_fusion.6
  10.3 0.0 all-gather.2.cloned.1.call-update
  10.3 0.0 reduce-scatter.4.cloned.1.call-start
  10.4 0.2 multiply_convert_fusion
  10.6 0.1 constant_dynamic-slice_fusion.2
  10.8 0.1 pad_maximum_fusion.3
  10.8 3.3 %collective-permute-start.1 = (bf16[128,3584]{1,0:T(8,128)(2,1)S(1)}, bf16[128,3584]{1,0:T(8,128)(2,1)}, u32[]{:S(2)}, u32[]{:S(2)}) collective-permute-start(bf16[128,3584]{1,0:T(8,128)(2,1)S(1)} %pad_maximum_fusion.3), channel_id=1, source_target_pairs={{0,1},{1,0},{2,3},{3,2},{4,5},{5,4},{6,7},{7,6},{8,9},{9,8},{10,11... | collective-permute-start | bytes 2752520 | tf_op jit(solution)/shard_map/ppermute | solution.py:76
  14.2 0.1 fusion.30
  14.4 0.4 collective-permute-start
  14.8 0.1 iota_add_fusion
  14.9 0.1 add.82
  15.0 1.3 collective-permute-done
  16.3 0.1 collective-permute-done.1
  16.4 2.6 %convolution_convert_fusion = bf16[640,3584]{1,0:T(8,128)(2,1)S(1)} fusion(bf16[128,3584]{1,0:T(8,128)(2,1)} %collective-permute-done.1, bf16[128,1792]{1,0:T(8,128)(2,1)S(1)} %get-tuple-element.43, bf16[128,1792]{1,0:T(8,128)(2,1)S(1)} %get-tuple-element.52, s32[256]{0:T(256)S(1)} %bitcast.41, s32[640]{0:T(1024)S(1)} %add.82), kind=kOutput, calls=%fused_computation.1 | convolution fusion | flops 1182367744 | bytes 6426112 | tf_op jit(solution)/shard_map/dot_general | solution.py:40
  19.0 59.4 %all_to_all.10 = bf16[16,40,3584]{2,1,0:T(8,128)(2,1)} all-to-all(bf16[16,40,3584]{2,1,0:T(8,128)(2,1)S(1)} %bitcast.35), channel_id=1, replica_groups=mesh['z'=8,'p'=16,'c'=2] {'p'}, dimensions={0} | all-to-all | bytes 9175040 | tf_op jit(solution)/shard_map/all_to_all | solution.py:83
  78.4 1.5 collective-permute-start.2
  79.9 1.5 all-gather.2.cloned.1.call-done
  81.4 2.9 %fusion.4 = f32[640,256]{0,1:T(8,128)S(1)} fusion(bf16[640,3584]{1,0:T(8,128)(2,1)} %bitcast.5, bf16[3584,768]{1,0:T(8,128)(2,1)} %all-gather.2.cloned.1.call-done), kind=kOutput, calls=%fused_computation.16 | convolution fusion | flops 587202560 | bytes 3866624 | tf_op jit(solution)/shard_map/dot_general | solution.py:40
  84.3 3.9 %fusion.10 = f32[640,512]{0,1:T(8,128)S(1)} fusion(bf16[640,3584]{1,0:T(8,128)(2,1)} %bitcast.5, bf16[3584,768]{1,0:T(8,128)(2,1)} %all-gather.2.cloned.1.call-done), kind=kOutput, calls=%fused_computation.22 | convolution fusion | flops 1174405120 | bytes 5439488 | tf_op jit(solution)/shard_map/dot_general | solution.py:40
  88.3 3.3 %fusion.22 = f32[640,512]{0,1:T(8,128)S(1)} fusion(f32[640,512]{0,1:T(8,128)S(1)} %fusion.10, bf16[3584,768]{1,0:T(8,128)(2,1)S(1)} %bitcast.38, bf16[640,3584]{1,0:T(8,128)(2,1)} %collective-permute-done.2), kind=kOutput, calls=%fused_computation.36 | convolution fusion | flops 1174732800 | bytes 6750208 | tf_op jit(solution)/shard_map/dot_general | solution.py:40
  91.6 2.8 %multiply_convert_fusion.2 = (bf16[640,256]{0,1:T(8,128)(2,1)S(1)}, bf16[640,256]{0,1:T(8,128)(2,1)S(1)}, bf16[640,256]{0,1:T(8,128)(2,1)S(1)}) fusion(f32[640,512]{0,1:T(8,128)S(1)} %fusion.22, f32[640,256]{0,1:T(8,128)S(1)} %fusion.4, bf16[3584,768]{1,0:T(8,128)(2,1)S(1)} %bitcast.38, bf16[640,3584]{1,0:T(8,128)(2,1)} %collective-permute-done.2), kind=kOutput, calls=%fused_computation.55 | convolution fusion | flops 589987840 | bytes 6160384 | tf_op jit(solution)/shard_map/dot_general | solution.py:40
  94.4 0.8 convolution_convert_fusion.3
  95.3 1.4 convolution_convert_fusion.1
  96.7 2.4 pad_maximum_fusion
  99.1 0.7 collective-permute-start.3
  99.8 2.5 %convolution_convert_fusion.8 = bf16[1792,256]{0,1:T(8,128)(2,1)S(1)} fusion(bf16[640,256]{0,1:T(8,128)(2,1)S(1)} %get-tuple-element.38, bf16[640,3584]{1,0:T(8,128)(2,1)} %bitcast.5), kind=kOutput, calls=%fused_computation.11 | convolution fusion | flops 587661312 | bytes 3538944 | tf_op jit(solution)/shard_map/dot_general | solution.py:40
  102.3 2.5 %convolution_convert_fusion.7 = bf16[1792,256]{0,1:T(8,128)(2,1)S(1)} fusion(bf16[640,256]{0,1:T(8,128)(2,1)S(1)} %get-tuple-element.38, bf16[640,3584]{1,0:T(8,128)(2,1)} %collective-permute-done.2), kind=kOutput, calls=%fused_computation.10 | convolution fusion | flops 587661312 | bytes 3538944 | tf_op jit(solution)/shard_map/dot_general | solution.py:40
  104.8 3.2 %convolution_convert_fusion.6 = bf16[1792,512]{0,1:T(8,128)(2,1)S(1)} fusion(bf16[640,3584]{1,0:T(8,128)(2,1)} %bitcast.5, bf16[640,256]{0,1:T(8,128)(2,1)S(1)} %get-tuple-element.33, bf16[640,256]{0,1:T(8,128)(2,1)S(1)} %get-tuple-element.32), kind=kOutput, calls=%fused_computation.9 | convolution fusion | flops 1176633344 | bytes 4784128 | tf_op jit(solution)/shard_map/dot_general | solution.py:40
  108.1 3.2 %convolution_convert_fusion.5 = bf16[1792,512]{0,1:T(8,128)(2,1)S(1)} fusion(bf16[640,3584]{1,0:T(8,128)(2,1)} %collective-permute-done.2, bf16[640,256]{0,1:T(8,128)(2,1)S(1)} %get-tuple-element.33, bf16[640,256]{0,1:T(8,128)(2,1)S(1)} %get-tuple-element.32), kind=kOutput, calls=%fused_computation.8 | convolution fusion | flops 1176633344 | bytes 4784128 | tf_op jit(solution)/shard_map/dot_general | solution.py:40
  111.4 24.3 %maximum_maximum_fusion = bf16[3584,768]{0,1:T(8,128)(2,1)} fusion(bf16[1792,256]{0,1:T(8,128)(2,1)S(1)} %convolution_convert_fusion.7, bf16[1792,512]{0,1:T(8,128)(2,1)S(1)} %convolution_convert_fusion.5, bf16[1792,256]{0,1:T(8,128)(2,1)S(1)} %convolution_convert_fusion.8, bf16[1792,512]{0,1:T(8,128)(2,1)S(1)} %convolution_convert_fusion.6), kind=kLoop, calls=%fused_computation.2 | loop fusion | flops 22020096 | bytes 11010048 | tf_op jit(solution)/shard_map/concatenate | solution.py:111
  135.6 8.3 %copy.42 = bf16[3584,768]{1,0:T(8,128)(2,1)} copy(bf16[3584,768]{0,1:T(8,128)(2,1)} %maximum_maximum_fusion) | data formatting | bytes 11010048
  143.9 2.0 convolution_convert_fusion.4
  145.9 2.9 %convolution_convert_fusion.2 = bf16[640,1792]{1,0:T(8,128)(2,1)S(1)} fusion(bf16[3584,768]{1,0:T(8,128)(2,1)} %all-gather.2.cloned.1.call-done, bf16[640,256]{0,1:T(8,128)(2,1)S(1)} %get-tuple-element.33, bf16[640,256]{0,1:T(8,128)(2,1)S(1)} %get-tuple-element.32), kind=kOutput, calls=%fused_computation.5 | convolution fusion | flops 1176862720 | bytes 4784128 | tf_op jit(solution)/shard_map/dot_general | solution.py:40
  148.8 2.9 %add_convert_fusion = bf16[640,3584]{1,0:T(8,128)(2,1)S(1)} fusion(bf16[640,3584]{1,0:T(8,128)(2,1)} %collective-permute-done.3, bf16[640,1792]{1,0:T(8,128)(2,1)S(1)} %convolution_convert_fusion.2, bf16[640,1792]{1,0:T(8,128)(2,1)S(1)} %convolution_convert_fusion.4), kind=kLoop, calls=%fused_computation | loop fusion | flops 16056320 | bytes 13762560 | tf_op jit(solution)/shard_map/convert_element_type | solution.py:104
  151.7 61.3 %all_to_all.11 = bf16[16,40,3584]{2,1,0:T(8,128)(2,1)S(1)} all-to-all(bf16[16,40,3584]{2,1,0:T(8,128)(2,1)S(1)} %bitcast.34), channel_id=1, replica_groups=mesh['z'=8,'p'=16,'c'=2] {'p'}, dimensions={0} | all-to-all | bytes 9175040 | tf_op jit(solution)/shard_map/all_to_all | solution.py:116
  213.0 1.6 fusion.47
  214.7 0.1 slice.127
  214.7 0.2 fusion.12
  214.9 1.0 pad_maximum_fusion.2
  215.9 1.4 collective-permute-start.4
  217.3 1.2 copy.30
  218.5 1.1 copy.33
  219.6 2.5 copy.31
  222.1 2.5 copy.32
  224.6 2.0 copy.34
  226.6 2.0 copy.35
  228.6 1.3 broadcast_select_fusion.1
  229.9 1.0 pad_maximum_fusion.5
  230.9 1.0 pad_maximum_fusion.4
  231.9 1.4 copy.43
  233.3 0.2 convert_element_type.126
  233.5 0.1 slice_bitcast_fusion.1
  233.6 0.9 copy-done
  234.5 0.3 copy-done.1
  234.8 2.0 subtract_convert_fusion
  236.8 2.5 copy.37
  239.3 1.2 copy.38
  240.6 1.0 copy.36
  241.6 1.6 subtract_convert_fusion.1
  243.2 1.0 copy.40
  244.1 1.0 copy.41
  245.1 0.8 copy.39
  (27 shorter events, 0.1 us)
Async XLA Ops:
  7.2 3.2 %copy-start.5 = (f32[128,1]{0,1:T(1,128)S(1)}, f32[128,1]{0,1:T(1,128)}, u32[]{:S(2)}) copy-start(f32[128,1]{0,1:T(1,128)} %param.13) | copy-start | bytes 1540
  7.2 3.2 %copy-start.3 = (bf16[128,3584]{1,0:T(8,128)(2,1)S(1)}, bf16[128,3584]{1,0:T(8,128)(2,1)}, u32[]{:S(2)}) copy-start(bf16[128,3584]{1,0:T(8,128)(2,1)} %param.11) | copy-start | bytes 2752516
  7.2 3.4 %copy-start.4 = (bf16[128,3584]{1,0:T(8,128)(2,1)S(1)}, bf16[128,3584]{1,0:T(8,128)(2,1)}, u32[]{:S(2)}) copy-start(bf16[128,3584]{1,0:T(8,128)(2,1)} %param.10) | copy-start | bytes 2752516
  7.2 74.2 %all-gather.2.cloned.1.call-start = ((), (), s32[]{:S(2)}) async-start(), calls=%async_computation.3 | async-start | bytes 6193152 | tf_op jit(solution)/shard_map/all_gather | solution.py:59
  10.3 221.6 %reduce-scatter.4.cloned.1.call-start = ((), (), s32[]{:S(2)}) async-start(), calls=%async_computation.4 | async-start | bytes 6193152
  10.6 3.5 %copy-start.6 = (s32[128,1]{0,1:T(1,128)S(1)}, s32[128,1]{0,1:T(1,128)}, u32[]{:S(2)}) copy-start(s32[128,1]{0,1:T(1,128)} %param.12) | copy-start | bytes 1540
  10.8 5.6 %collective-permute-start.1 = (bf16[128,3584]{1,0:T(8,128)(2,1)S(1)}, bf16[128,3584]{1,0:T(8,128)(2,1)}, u32[]{:S(2)}, u32[]{:S(2)}) collective-permute-start(bf16[128,3584]{1,0:T(8,128)(2,1)S(1)} %pad_maximum_fusion.3), channel_id=1, source_target_pairs={{0,1},{1,0},{2,3},{3,2},{4,5},{5,4},{6,7},{7,6},{8,9},{9,8},{10,11... | collective-permute-start | bytes 2752520 | tf_op jit(solution)/shard_map/ppermute | solution.py:76
  14.4 1.9 collective-permute-start
  78.4 9.9 %collective-permute-start.2 = (bf16[640,3584]{1,0:T(8,128)(2,1)}, bf16[640,3584]{1,0:T(8,128)(2,1)}, u32[]{:S(2)}, u32[]{:S(2)}) collective-permute-start(bf16[640,3584]{1,0:T(8,128)(2,1)} %bitcast.5), channel_id=1, source_target_pairs={{0,1},{1,0},{2,3},{3,2},{4,5},{5,4},{6,7},{7,6},{8,9},{9,8},{10,11... | collective-permute-start | bytes 13762568 | tf_op jit(solution)/shard_map/ppermute | solution.py:85
  81.4 6.9 %slice-start = ((s8[5505024]{0:T(1024)(128)(4,1)}), s8[4194304]{0:T(1024)(128)(4,1)S(1)}, s32[]{:S(2)}) async-start(s8[5505024]{0:T(1024)(128)(4,1)} %bitcast.37), calls=%async_computation.5 | async-start | bytes 8388608
  84.3 4.0 %slice-start.1 = ((s8[5505024]{0:T(1024)(128)(4,1)}), s8[1310720]{0:T(1024)(128)(4,1)S(1)}, s32[]{:S(2)}) async-start(s8[5505024]{0:T(1024)(128)(4,1)} %bitcast.37), calls=%async_computation.6 | async-start | bytes 2621440
  99.1 49.7 %collective-permute-start.3 = (bf16[640,3584]{1,0:T(8,128)(2,1)}, bf16[640,3584]{1,0:T(8,128)(2,1)}, u32[]{:S(2)}, u32[]{:S(2)}) collective-permute-start(bf16[640,3584]{1,0:T(8,128)(2,1)} %pad_maximum_fusion), channel_id=1, source_target_pairs={{0,1},{1,0},{2,3},{3,2},{4,5},{5,4},{6,7},{7,6},{8,9},{9,8},{10,11... | collective-permute-start | bytes 13762568 | tf_op jit(solution)/shard_map/ppermute | solution.py:103
  215.9 12.7 %collective-permute-start.4 = (bf16[128,3584]{1,0:T(8,128)(2,1)}, bf16[128,3584]{1,0:T(8,128)(2,1)}, u32[]{:S(2)}, u32[]{:S(2)}) collective-permute-start(bf16[128,3584]{1,0:T(8,128)(2,1)} %pad_maximum_fusion.2), channel_id=1, source_target_pairs={{0,1},{1,0},{2,3},{3,2},{4,5},{5,4},{6,7},{7,6},{8,9},{9,8},{10,11... | collective-permute-start | bytes 2752520 | tf_op jit(solution)/shard_map/ppermute | solution.py:123
  233.3 1.2 copy-start
  233.3 1.5 copy-start.1
  236.8 3.8 %copy-start.2 = (bf16[2,448,256]{1,2,0:T(8,128)(2,1)S(1)}, bf16[2,448,256]{1,2,0:T(8,128)(2,1)}, u32[]{:S(2)}) copy-start(bf16[2,448,256]{1,2,0:T(8,128)(2,1)} %get-tuple-element.27) | copy-start | bytes 1376260
Sparse Core Ops, SparseCore 0:
  10.4 70.8 all-gather.1
  144.0 65.8 reduce-scatter.3

commit v2 on v1

--- a/solution.py
+++ b/solution.py
@@ -1,6 +1,10 @@
+import functools
+
 import jax
 import jax.numpy as jnp
 from jax import lax
+from jax.experimental import pallas as pl
+from jax.experimental.pallas import tpu as pltpu
 from jax.sharding import Mesh, PartitionSpec as P
 
 EXPERTS = 8
@@ -15,6 +19,7 @@
 adam_epsilon = 1e-08
 
 SWAP = [(0, 1), (1, 0)]
+BLOCKS = 2
 
 
 def slots_of(flat_routes):
@@ -38,6 +43,178 @@
 
 def dot(a, b, dims=((1,), (0,))):
     return lax.dot_general(a, b, (dims, ((), ())), preferred_element_type=jnp.float32)
+
+
+MIB = 1 << 20
+
+
+def call(body, grid, in_specs, out_specs, out_shape, flops, scratch=(), vmem=40):
+    return pl.pallas_call(
+        body,
+        grid=(grid,),
+        in_specs=in_specs,
+        out_specs=out_specs,
+        out_shape=out_shape,
+        scratch_shapes=list(scratch),
+        compiler_params=pltpu.CompilerParams(vmem_limit_bytes=vmem * MIB),
+        cost_estimate=pl.CostEstimate(flops=flops, bytes_accessed=12 * MIB, transcendentals=0),
+    )
+
+
+def pre_body(hid, x_ref, y_ref, w_ref, acc_ref):
+    @pl.when(pl.program_id(0) == 0)
+    def _():
+        acc_ref[...] = jnp.zeros_like(acc_ref)
+
+    acc_ref[:, : 2 * hid] += dot(x_ref[...], w_ref[:, : 2 * hid])
+    acc_ref[:, 2 * hid :] += dot(y_ref[...], w_ref[:, 2 * hid :])
+
+
+def first_half(rows, weights, hid, blocks):
+    n, width = rows.shape
+    cols = width // 2 // blocks
+    return call(
+        functools.partial(pre_body, hid),
+        blocks,
+        [
+            pl.BlockSpec((n, cols), lambda i: (0, i)),
+            pl.BlockSpec((n, cols), lambda i: (0, blocks + i)),
+            pl.BlockSpec((cols, 3 * hid), lambda i: (i, 0)),
+        ],
+        pl.BlockSpec((n, 3 * hid), lambda i: (0, 0)),
+        jax.ShapeDtypeStruct((n, 3 * hid), jnp.float32),
+        flops=3 * n * width * hid,
+    )(rows, rows, weights)
+
+
+def mid_body(hid, blocks, pre_ref, x_ref, y_ref, w_ref, part_ref, deriv_ref, acc_ref):
+    step = pl.program_id(0)
+
+    @pl.when(step == 0)
+    def _():
+        acc_ref[...] = pre_ref[...]
+
+    @pl.when(step < blocks)
+    def _():
+        acc_ref[:, : 2 * hid] += dot(x_ref[...], w_ref[:, : 2 * hid])
+        acc_ref[:, 2 * hid :] += dot(y_ref[...], w_ref[:, 2 * hid :])
+
+    @pl.when(step == blocks - 1)
+    def _():
+        act, linear, d_hidden = (acc_ref[:, k * hid : (k + 1) * hid] for k in range(3))
+        sig = jax.nn.sigmoid(act)
+        gated = act * sig
+        deriv_ref[:, :hid] = (d_hidden * linear * sig * (1.0 + act * (1.0 - sig))).astype(jnp.bfloat16)
+        deriv_ref[:, hid : 2 * hid] = (d_hidden * gated).astype(jnp.bfloat16)
+        deriv_ref[:, 2 * hid :] = (gated * linear).astype(jnp.bfloat16)
+
+    @pl.when((step >= blocks) & (step < 2 * blocks))
+    def _():
+        part_ref[...] = dot(deriv_ref[:, 2 * hid :], w_ref[:, 2 * hid :], ((1,), (1,))).astype(jnp.bfloat16)
+
+    @pl.when(step >= 2 * blocks)
+    def _():
+        part_ref[...] = dot(deriv_ref[:, : 2 * hid], w_ref[:, : 2 * hid], ((1,), (1,))).astype(jnp.bfloat16)
+
+
+def second_half(pre, rows, weights, hid, blocks):
+    n, width = rows.shape
+    cols = width // 2 // blocks
+    start = weights.shape[0] // cols - blocks
+
+    def reading(i):
+        return jnp.minimum(i, blocks - 1)
+
+    return call(
+        functools.partial(mid_body, hid, blocks),
+        3 * blocks,
+        [
+            pl.BlockSpec((n, 3 * hid), lambda i: (0, 0)),
+            pl.BlockSpec((n, cols), lambda i: (0, reading(i))),
+            pl.BlockSpec((n, cols), lambda i: (0, blocks + reading(i))),
+            pl.BlockSpec((cols, 3 * hid), lambda i: (start + lax.rem(i, blocks), 0)),
+        ],
+        [
+            pl.BlockSpec((n, cols), lambda i: (0, jnp.maximum(i - blocks, 0))),
+            pl.BlockSpec((n, 3 * hid), lambda i: (0, 0)),
+        ],
+        [
+            jax.ShapeDtypeStruct((n, width), jnp.bfloat16),
+            jax.ShapeDtypeStruct((n, 3 * hid), jnp.bfloat16),
+        ],
+        flops=6 * n * width * hid,
+        scratch=[pltpu.VMEM((n, 3 * hid), jnp.float32)],
+    )(pre, rows, rows, weights)
+
+
+def grad_body(hid, blocks, xm_ref, ym_ref, xo_ref, yo_ref, deriv_ref, grad_ref):
+    def write(x, y):
+        grad_ref[:, : 2 * hid] = dot(x, deriv_ref[:, : 2 * hid], ((0,), (0,))).astype(jnp.bfloat16)
+        grad_ref[:, 2 * hid :] = dot(y, deriv_ref[:, 2 * hid :], ((0,), (0,))).astype(jnp.bfloat16)
+
+    @pl.when(pl.program_id(0) < blocks)
+    def _():
+        write(xm_ref[...], ym_ref[...])
+
+    @pl.when(pl.program_id(0) >= blocks)
+    def _():
+        write(xo_ref[...], yo_ref[...])
+
+
+def weight_grads(mine, other, deriv, hid, blocks):
+    n, width = mine.shape
+    cols = width // 2 // blocks
+
+    def early(i):
+        return jnp.minimum(i, blocks - 1)
+
+    def late(i):
+        return jnp.maximum(i - blocks, 0)
+
+    return call(
+        functools.partial(grad_body, hid, blocks),
+        2 * blocks,
+        [
+            pl.BlockSpec((n, cols), lambda i: (0, early(i))),
+            pl.BlockSpec((n, cols), lambda i: (0, blocks + early(i))),
+            pl.BlockSpec((n, cols), lambda i: (0, late(i))),
+            pl.BlockSpec((n, cols), lambda i: (0, blocks + late(i))),
+            pl.BlockSpec((n, 3 * hid), lambda i: (0, 0)),
+        ],
+        pl.BlockSpec((cols, 3 * hid), lambda i: (i, 0)),
+        jax.ShapeDtypeStruct((width, 3 * hid), jnp.bfloat16),
+        flops=6 * n * width * hid,
+    )(mine, mine, other, other, deriv)
+
+
+def back_body(hid, blocks, deriv_ref, w_ref, other_ref, back_ref):
+    def write(part):
+        back_ref[...] = (part + other_ref[...].astype(jnp.float32)).astype(jnp.bfloat16)
+
+    @pl.when(pl.program_id(0) < blocks)
+    def _():
+        write(dot(deriv_ref[:, 2 * hid :], w_ref[:, 2 * hid :], ((1,), (1,))))
+
+    @pl.when(pl.program_id(0) >= blocks)
+    def _():
+        write(dot(deriv_ref[:, : 2 * hid], w_ref[:, : 2 * hid], ((1,), (1,))))
+
+
+def sent_back(deriv, weights, from_other, hid, blocks):
+    n, width = from_other.shape
+    cols = width // 2 // blocks
+    return call(
+        functools.partial(back_body, hid, blocks),
+        2 * blocks,
+        [
+            pl.BlockSpec((n, 3 * hid), lambda i: (0, 0)),
+            pl.BlockSpec((cols, 3 * hid), lambda i: (lax.rem(i, blocks), 0)),
+            pl.BlockSpec((n, cols), lambda i: (0, i)),
+        ],
+        pl.BlockSpec((n, cols), lambda i: (0, i)),
+        jax.ShapeDtypeStruct((n, width), jnp.bfloat16),
+        flops=3 * n * width * hid,
+    )(deriv, weights, from_other)
 
 
 def shards(
@@ -57,7 +234,6 @@
 
     owned = jnp.concatenate([w_gate_up[0], w_gate_up[1], w_down.T], axis=1)
     weights = lax.all_gather(owned, ("z", "c"), axis=0, tiled=True, axis_index_groups=orders)
-    w_m, w_o = weights[:half], weights[half:]
 
     flat = routes.reshape(-1)
     place = flat * block + c * CAPACITY + slots_of(flat)
@@ -83,36 +259,16 @@
     got = lax.all_to_all(packed, "p", split_axis=0, concat_axis=0, tiled=True)
     mine = got.reshape(n_chip * block, width)
     other = lax.ppermute(mine, "c", SWAP)
-    x_m, y_m = mine[:, :half], mine[:, half:]
-    x_o, y_o = other[:, :half], other[:, half:]
-
-    pre = dot(x_m, w_m[:, : 2 * hid]) + dot(x_o, w_o[:, : 2 * hid])
-    d_hidden = dot(y_m, w_m[:, 2 * hid :]) + dot(y_o, w_o[:, 2 * hid :])
-    act_in, linear = pre[:, :hid], pre[:, hid:]
-    sig = jax.nn.sigmoid(act_in)
-    hidden = (act_in * sig * linear).astype(jnp.bfloat16)
-    d_act = (d_hidden * linear * sig * (1.0 + act_in * (1.0 - sig))).astype(jnp.bfloat16)
-    d_lin = (d_hidden * act_in * sig).astype(jnp.bfloat16)
-    d_pre = jnp.concatenate([d_act, d_lin], axis=1)
-
-    def parts(w):
-        out = dot(hidden, w[:, 2 * hid :], ((1,), (1,)))
-        inp = dot(d_pre, w[:, : 2 * hid], ((1,), (1,)))
-        return jnp.concatenate([out.astype(jnp.bfloat16), inp.astype(jnp.bfloat16)], axis=1)
-
-    from_other = lax.ppermute(parts(w_o), "c", SWAP)
-    back = (parts(w_m).astype(jnp.float32) + from_other.astype(jnp.float32)).astype(jnp.bfloat16)
-
-    def grads(x, y):
-        up = dot(x, d_pre, ((0,), (0,))).astype(jnp.bfloat16)
-        down = dot(y, hidden, ((0,), (0,))).astype(jnp.bfloat16)
-        return jnp.concatenate([up, down], axis=1)
-
-    grad = jnp.concatenate([grads(x_m, y_m), grads(x_o, y_o)], axis=0)
+
+    pre = first_half(mine, weights, hid, BLOCKS)
+    parts_o, deriv = second_half(pre, other, weights, hid, BLOCKS)
+    from_other = lax.ppermute(parts_o, "c", SWAP)
+    grad = weight_grads(mine, other, deriv, hid, BLOCKS)
     grad = lax.psum_scatter(
         grad, ("z", "c"), scatter_dimension=0, tiled=True, axis_index_groups=orders
     ).astype(jnp.float32)
 
+    back = sent_back(deriv, weights, from_other, hid, BLOCKS)
     back = lax.all_to_all(
         back.reshape(n_chip, block, width), "p", split_axis=0, concat_axis=0, tiled=True
     ).reshape(n_chip * block, width)

time: 254 us -> 199 us (0.78)
  matrix products: 36 us -> 4.35 us
  Pallas kernels: 0 us -> 30.3 us
  other arithmetic: 40 us -> 11.3 us
  local copies, waits for them, and re-layouts: 31.3 us -> 3.6 us
  waiting for transfers between devices: 2.9 us -> 6.71 us
    dot_general x14 -> x2, matrix products: 35.9 us -> 4.2 us  [dot(): lax.dot_general(a, b, (dims, ((), ())), preferred_element_type=jnp.float32)]
    pallas_call x0 -> x4, Pallas kernels: none -> 30.3 us  [the longest x1 10.7 us: second_half(): call(functools.partial(mid_body, hid, blocks), 3 * blocks, [pl.BlockSpec(...]
    concatenate x2 -> x0, other arithmetic: 26.7 us -> none  [the longest x1 24.3 us: shards(): grad = jnp.concatenate([grads(x_m, y_m), grads(x_o, y_o)], axis=0)]
    unnamed x32 -> x20, local copies, waits for them, and re-layouts: 29.7 us -> 3.23 us
    convert_element_type x1 -> x0, other arithmetic: 2.92 us -> none  [shards(): (parts(w_m).astype(jnp.float32) + from_other.astype(jnp.float32)).astype(...]
  transfers between devices with their start and end apart: 7 -> 7, of which waited for: 3 -> 4; matrix products, arithmetic and copies ran while one was open for 31% -> 5% of each run, Pallas kernels for 0% -> 10%
where the time goes in v2:
time: 199 us
  blocking collectives  121 us (61%)
  Pallas kernels  30.3 us (15%)
  between operations  14.3 us (7%)
  other arithmetic  11.3 us (6%)
  starting transfers between devices  7.58 us (4%)
  waiting for transfers between devices  6.71 us (3%)
  matrix products  4.35 us (2%)
  local copies, waits for them, and re-layouts  3.6 us (2%)
    all_to_all x1, blocking collectives, shards(): lax.all_to_all(back.reshape(n_chip, block, width), 'p', split_axis=0, con...  61.2 us
    all_to_all x1, blocking collectives, shards(): got = lax.all_to_all(packed, 'p', split_axis=0, concat_axis=0, tiled=True)  59.4 us
    pallas_call x1, Pallas kernels, second_half(): call(functools.partial(mid_body, hid, blocks), 3 * blocks, [pl.BlockSpec(...  10.7 us
    pallas_call x1, Pallas kernels, weight_grads(): call(functools.partial(grad_body, hid, blocks), 2 * blocks, [pl.BlockSpec...  9.43 us
    pallas_call x1, Pallas kernels, sent_back(): call(functools.partial(back_body, hid, blocks), 2 * blocks, [pl.BlockSpec...  6.04 us
    dot_general x2, matrix products, dot(): lax.dot_general(a, b, (dims, ((), ())), preferred_element_type=jnp.float32)  4.2 us
    pallas_call x1, Pallas kernels, first_half(): call(functools.partial(pre_body, hid), blocks, [pl.BlockSpec((n, cols), l...  4.15 us
  transfers between devices with their start and end apart: 7, of which 4 were waited for; matrix products, arithmetic and copies ran while one was open for 5% of the time, Pallas kernels for 10%

profile of v2, /device:TPU:1, one launch (start us, length us, event | category | flops | bytes accessed | tf_op | source)
XLA Modules:
  0.0 198.8 jit_solution(5316638669176435012)
XLA Ops:
  7.2 0.0 copy-start.2
  7.2 0.0 all-gather.2.cloned.1.call-start
  7.2 1.5 multiply_convert_fusion
  8.7 0.0 copy-done.2
  8.7 0.1 constant_dynamic-slice_fusion.2
  8.8 0.0 copy-start.9
  8.9 0.0 copy-start.8
  8.9 0.0 copy-start.1
  8.9 0.0 copy-start.5
  8.9 0.1 pad_maximum_fusion.1
  9.0 3.3 %collective-permute-start.1 = (bf16[128,3584]{1,0:T(8,128)(2,1)S(1)}, bf16[128,3584]{1,0:T(8,128)(2,1)}, u32[]{:S(2)}, u32[]{:S(2)}) collective-permute-start(bf16[128,3584]{1,0:T(8,128)(2,1)S(1)} %pad_maximum_fusion.1), channel_id=1, source_target_pairs={{0,1},{1,0},{2,3},{3,2},{4,5},{5,4},{6,7},{7,6},{8,9},{9,8},{10,11... | collective-permute-start | bytes 2752520 | tf_op jit(solution)/shard_map/ppermute | solution.py:252
  12.3 0.0 copy-done.9
  12.3 0.1 fusion.6
  12.5 0.0 copy-done.8
  12.5 0.5 collective-permute-start
  13.0 0.0 copy-done.1
  13.1 0.0 copy-done.5
  13.1 0.9 pad_maximum_fusion.5
  14.0 0.0 all-gather.2.cloned.1.call-update
  14.0 0.0 reduce-scatter.2.cloned.1.call-start
  14.1 0.1 iota_add_fusion
  14.1 0.1 add.67
  14.2 0.2 collective-permute-done
  14.4 0.1 collective-permute-done.1
  14.5 2.6 %convolution_convert_fusion = bf16[640,3584]{1,0:T(8,128)(2,1)S(1)} fusion(bf16[128,3584]{1,0:T(8,128)(2,1)} %collective-permute-done.1, bf16[128,1792]{1,0:T(8,128)(2,1)S(1)} %get-tuple-element.28, bf16[128,1792]{1,0:T(8,128)(2,1)S(1)} %get-tuple-element.37, s32[256]{0:T(256)S(1)} %bitcast.34, s32[640]{0:T(1024)S(1)} %add.67), kind=kOutput, calls=%fused_computation | convolution fusion | flops 1182367744 | bytes 6426112 | tf_op jit(solution)/shard_map/dot_general | solution.py:45
  17.1 59.4 %all_to_all.10 = bf16[16,40,3584]{2,1,0:T(8,128)(2,1)} all-to-all(bf16[16,40,3584]{2,1,0:T(8,128)(2,1)S(1)} %bitcast.30), channel_id=1, replica_groups=mesh['z'=8,'p'=16,'c'=2] {'p'}, dimensions={0} | all-to-all | bytes 9175040 | tf_op jit(solution)/shard_map/all_to_all | solution.py:259
  76.5 1.5 collective-permute-start.2
  78.0 3.9 %all-gather.2.cloned.1.call-done.w_ref = bf16[3584,768]{1,0:T(8,128)(2,1)} async-done(((bf16[448,768]{1,0:T(8,128)(2,1)}), bf16[3584,768]{1,0:T(8,128)(2,1)}) %all-gather.2.cloned.1.call-update) | async-done | bytes 5505040 | tf_op jit(solution)/shard_map/all_gather | solution.py:236
  82.0 0.0 copy-start
  82.0 2.6 %copy-done = bf16[3584,768]{1,0:T(8,128)(2,1)S(1)} copy-done((bf16[3584,768]{1,0:T(8,128)(2,1)S(1)}, bf16[3584,768]{1,0:T(8,128)(2,1)}, u32[]{:S(2)}) %copy-start) | copy-done | bytes 5505048
  84.6 4.2 %shard_map.161.pre_ref = f32[640,768]{1,0:T(8,128)S(1)} custom-call(bf16[640,3584]{1,0:T(8,128)(2,1)} %bitcast.5.x_ref.y_ref.xm_ref.ym_ref, bf16[640,3584]{1,0:T(8,128)(2,1)} %bitcast.5.x_ref.y_ref.xm_ref.ym_ref, bf16[3584,768]{1,0:T(8,128)(2,1)S(1)} %copy-done), custom_call_target="tpu_custom_call" | custom-call | flops 1761607680 | bytes 12582912 | tf_op jit(solution)/shard_map/pallas_call | solution.py:76
  88.7 0.0 collective-permute-done.2.x_ref.y_ref.xo_ref.yo_ref
  88.7 10.7 %shard_map.162 = (bf16[640,3584]{1,0:T(8,128)(2,1)}, bf16[640,768]{1,0:T(8,128)(2,1)S(1)}) custom-call(f32[640,768]{1,0:T(8,128)S(1)} %shard_map.161.pre_ref, bf16[640,3584]{1,0:T(8,128)(2,1)} %collective-permute-done.2.x_ref.y_ref.xo_ref.yo_ref, bf16[640,3584]{1,0:T(8,128)(2,1)} %collective-permute-done.2.x_ref.y_ref.xo_ref.yo_ref, ...), custom_call_target="tpu_custom_call" | custom-call | flops 3523215360 | bytes 12582912 | tf_op jit(solution)/shard_map/pallas_call | solution.py:128
  99.4 0.7 collective-permute-start.3
  100.1 9.4 %shard_map.164 = bf16[3584,768]{1,0:T(8,128)(2,1)} custom-call(bf16[640,3584]{1,0:T(8,128)(2,1)} %bitcast.5.x_ref.y_ref.xm_ref.ym_ref, bf16[640,3584]{1,0:T(8,128)(2,1)} %bitcast.5.x_ref.y_ref.xm_ref.ym_ref, bf16[640,3584]{1,0:T(8,128)(2,1)} %collective-permute-done.2.x_ref.y_ref.xo_ref.yo_ref, ...), custom_call_target="tpu_custom_call" | custom-call | flops 3523215360 | bytes 12582912 | tf_op jit(solution)/shard_map/pallas_call | solution.py:174
  109.5 0.0 reduce-scatter.2.cloned.1.call-update
  109.5 0.0 collective-permute-done.3.other_ref
  109.5 6.0 %shard_map.163 = bf16[640,3584]{1,0:T(8,128)(2,1)S(1)} custom-call(bf16[640,768]{1,0:T(8,128)(2,1)S(1)} %get-tuple-element.10.deriv_ref, bf16[3584,768]{1,0:T(8,128)(2,1)} %all-gather.2.cloned.1.call-done.w_ref, bf16[640,3584]{1,0:T(8,128)(2,1)} %collective-permute-done.3.other_ref), custom_call_target="tpu_custom_call" | custom-call | flops 1761607680 | bytes 12582912 | tf_op jit(solution)/shard_map/pallas_call | solution.py:206
  115.6 61.2 %all_to_all.11 = bf16[16,40,3584]{2,1,0:T(8,128)(2,1)S(1)} all-to-all(bf16[16,40,3584]{2,1,0:T(8,128)(2,1)S(1)} %bitcast.28), channel_id=1, replica_groups=mesh['z'=8,'p'=16,'c'=2] {'p'}, dimensions={0} | all-to-all | bytes 9175040 | tf_op jit(solution)/shard_map/all_to_all | solution.py:272
  176.8 1.6 fusion.19
  178.4 0.1 slice.67
  178.5 0.2 fusion
  178.7 1.0 pad_maximum_fusion
  179.7 1.4 collective-permute-start.4
  181.1 2.4 %collective-permute-done.4 = bf16[128,3584]{1,0:T(8,128)(2,1)} collective-permute-done((bf16[128,3584]{1,0:T(8,128)(2,1)}, bf16[128,3584]{1,0:T(8,128)(2,1)}, u32[]{:S(2)}, u32[]{:S(2)}) %collective-permute-start.4) | collective-permute-done | bytes 917536 | tf_op jit(solution)/shard_map/ppermute | solution.py:279
  183.5 1.3 broadcast_select_fusion.1
  184.8 1.0 pad_maximum_fusion.2
  185.8 1.0 pad_maximum_fusion.3
  186.8 0.0 copy-start.6
  186.8 0.0 copy-start.7
  186.8 0.0 reduce-scatter.2.cloned.1.call-done
  186.8 1.3 convert_element_type.70
  188.1 0.1 slice_bitcast_fusion.1
  188.1 0.0 copy-done.6
  188.1 0.0 copy-done.7
  188.2 0.0 copy-start.3
  188.2 0.0 copy-start.4
  188.2 1.2 subtract_convert_fusion.1
  189.4 0.1 copy-done.3
  189.5 0.5 copy-done.4
  190.0 1.9 subtract_convert_fusion
  (6 shorter events, 0.1 us)
Async XLA Ops:
  7.2 1.5 copy-start.2
  7.2 74.8 %all-gather.2.cloned.1.call-start = ((), (), s32[]{:S(2)}) async-start(), calls=%async_computation.3 | async-start | bytes 6193152 | tf_op jit(solution)/shard_map/all_gather | solution.py:236
  8.8 3.4 %copy-start.9 = (s32[128,1]{0,1:T(1,128)S(1)}, s32[128,1]{0,1:T(1,128)}, u32[]{:S(2)}) copy-start(s32[128,1]{0,1:T(1,128)} %param.12) | copy-start | bytes 1540
  8.9 3.6 %copy-start.8 = (f32[128,1]{0,1:T(1,128)S(1)}, f32[128,1]{0,1:T(1,128)}, u32[]{:S(2)}) copy-start(f32[128,1]{0,1:T(1,128)} %param.13) | copy-start | bytes 1540
  8.9 4.2 %copy-start.1 = (bf16[2,448,256]{2,1,0:T(8,128)(2,1)S(1)}, bf16[2,448,256]{2,1,0:T(8,128)(2,1)}, u32[]{:S(2)}) copy-start(bf16[2,448,256]{2,1,0:T(8,128)(2,1)} %param.14) | copy-start | bytes 1376260
  8.9 4.2 %copy-start.5 = (bf16[256,448]{0,1:T(8,128)(2,1)S(1)}, bf16[256,448]{0,1:T(8,128)(2,1)}, u32[]{:S(2)}) copy-start(bf16[256,448]{0,1:T(8,128)(2,1)} %param.15) | copy-start | bytes 688132
  9.0 5.6 %collective-permute-start.1 = (bf16[128,3584]{1,0:T(8,128)(2,1)S(1)}, bf16[128,3584]{1,0:T(8,128)(2,1)}, u32[]{:S(2)}, u32[]{:S(2)}) collective-permute-start(bf16[128,3584]{1,0:T(8,128)(2,1)S(1)} %pad_maximum_fusion.1), channel_id=1, source_target_pairs={{0,1},{1,0},{2,3},{3,2},{4,5},{5,4},{6,7},{7,6},{8,9},{9,8},{10,11... | collective-permute-start | bytes 2752520 | tf_op jit(solution)/shard_map/ppermute | solution.py:252
  12.5 1.9 collective-permute-start
  14.0 172.8 %reduce-scatter.2.cloned.1.call-start = ((), (), s32[]{:S(2)}) async-start(), calls=%async_computation.4 | async-start | bytes 6193152 | tf_op jit(solution)/shard_map/reduce_scatter | solution.py:267
  76.5 12.2 %collective-permute-start.2 = (bf16[640,3584]{1,0:T(8,128)(2,1)}, bf16[640,3584]{1,0:T(8,128)(2,1)}, u32[]{:S(2)}, u32[]{:S(2)}) collective-permute-start(bf16[640,3584]{1,0:T(8,128)(2,1)} %bitcast.5.x_ref.y_ref.xm_ref.ym_ref), channel_id=1, source_target_pairs={{0,1},{1,0},{2,3},{3,2},{4,5},{5,4},{6,7},{7,6},{8,9},{9,8},{10,11... | collective-permute-start | bytes 13762568 | tf_op jit(solution)/shard_map/ppermute | solution.py:261
  82.0 2.6 %copy-start = (bf16[3584,768]{1,0:T(8,128)(2,1)S(1)}, bf16[3584,768]{1,0:T(8,128)(2,1)}, u32[]{:S(2)}) copy-start(bf16[3584,768]{1,0:T(8,128)(2,1)} %all-gather.2.cloned.1.call-done.w_ref) | copy-start | bytes 16515076
  99.4 10.1 %collective-permute-start.3 = (bf16[640,3584]{1,0:T(8,128)(2,1)}, bf16[640,3584]{1,0:T(8,128)(2,1)}, u32[]{:S(2)}, u32[]{:S(2)}) collective-permute-start(bf16[640,3584]{1,0:T(8,128)(2,1)} %get-tuple-element.11), channel_id=1, source_target_pairs={{0,1},{1,0},{2,3},{3,2},{4,5},{5,4},{6,7},{7,6},{8,9},{9,8},{10,11... | collective-permute-start | bytes 13762568 | tf_op jit(solution)/shard_map/ppermute | solution.py:265
  179.7 3.9 %collective-permute-start.4 = (bf16[128,3584]{1,0:T(8,128)(2,1)}, bf16[128,3584]{1,0:T(8,128)(2,1)}, u32[]{:S(2)}, u32[]{:S(2)}) collective-permute-start(bf16[128,3584]{1,0:T(8,128)(2,1)} %pad_maximum_fusion), channel_id=1, source_target_pairs={{0,1},{1,0},{2,3},{3,2},{4,5},{5,4},{6,7},{7,6},{8,9},{9,8},{10,11... | collective-permute-start | bytes 2752520 | tf_op jit(solution)/shard_map/ppermute | solution.py:279
  186.8 1.4 copy-start.6
  186.8 1.4 copy-start.7
  188.2 1.4 copy-start.3
  188.2 1.9 copy-start.4
Sparse Core Ops, SparseCore 0:
  14.1 67.8 all-gather.1
  109.6 65.8 reduce-scatter.1

commit v3 on v2

--- a/solution.py
+++ b/solution.py
@@ -46,9 +46,10 @@
 
 
 MIB = 1 << 20
-
-
-def call(body, grid, in_specs, out_specs, out_shape, flops, scratch=(), vmem=40):
+VMEM = 57
+
+
+def call(body, grid, in_specs, out_specs, out_shape, flops, scratch=(), vmem=VMEM):
     return pl.pallas_call(
         body,
         grid=(grid,),
@@ -87,17 +88,15 @@
     )(rows, rows, weights)
 
 
-def mid_body(hid, blocks, pre_ref, x_ref, y_ref, w_ref, part_ref, deriv_ref, acc_ref):
+def mid_body(hid, blocks, pre_ref, x_ref, y_ref, w_ref, deriv_ref, acc_ref):
     step = pl.program_id(0)
 
     @pl.when(step == 0)
     def _():
         acc_ref[...] = pre_ref[...]
 
-    @pl.when(step < blocks)
-    def _():
-        acc_ref[:, : 2 * hid] += dot(x_ref[...], w_ref[:, : 2 * hid])
-        acc_ref[:, 2 * hid :] += dot(y_ref[...], w_ref[:, 2 * hid :])
+    acc_ref[:, : 2 * hid] += dot(x_ref[...], w_ref[:, : 2 * hid])
+    acc_ref[:, 2 * hid :] += dot(y_ref[...], w_ref[:, 2 * hid :])
 
     @pl.when(step == blocks - 1)
     def _():
@@ -108,41 +107,22 @@
         deriv_ref[:, hid : 2 * hid] = (d_hidden * gated).astype(jnp.bfloat16)
         deriv_ref[:, 2 * hid :] = (gated * linear).astype(jnp.bfloat16)
 
-    @pl.when((step >= blocks) & (step < 2 * blocks))
-    def _():
-        part_ref[...] = dot(deriv_ref[:, 2 * hid :], w_ref[:, 2 * hid :], ((1,), (1,))).astype(jnp.bfloat16)
-
-    @pl.when(step >= 2 * blocks)
-    def _():
-        part_ref[...] = dot(deriv_ref[:, : 2 * hid], w_ref[:, : 2 * hid], ((1,), (1,))).astype(jnp.bfloat16)
-
 
 def second_half(pre, rows, weights, hid, blocks):
     n, width = rows.shape
     cols = width // 2 // blocks
-    start = weights.shape[0] // cols - blocks
-
-    def reading(i):
-        return jnp.minimum(i, blocks - 1)
-
     return call(
         functools.partial(mid_body, hid, blocks),
-        3 * blocks,
+        blocks,
         [
             pl.BlockSpec((n, 3 * hid), lambda i: (0, 0)),
-            pl.BlockSpec((n, cols), lambda i: (0, reading(i))),
-            pl.BlockSpec((n, cols), lambda i: (0, blocks + reading(i))),
-            pl.BlockSpec((cols, 3 * hid), lambda i: (start + lax.rem(i, blocks), 0)),
+            pl.BlockSpec((n, cols), lambda i: (0, i)),
+            pl.BlockSpec((n, cols), lambda i: (0, blocks + i)),
+            pl.BlockSpec((cols, 3 * hid), lambda i: (blocks + i, 0)),
         ],
-        [
-            pl.BlockSpec((n, cols), lambda i: (0, jnp.maximum(i - blocks, 0))),
-            pl.BlockSpec((n, 3 * hid), lambda i: (0, 0)),
-        ],
-        [
-            jax.ShapeDtypeStruct((n, width), jnp.bfloat16),
-            jax.ShapeDtypeStruct((n, 3 * hid), jnp.bfloat16),
-        ],
-        flops=6 * n * width * hid,
+        pl.BlockSpec((n, 3 * hid), lambda i: (0, 0)),
+        jax.ShapeDtypeStruct((n, 3 * hid), jnp.bfloat16),
+        flops=3 * n * width * hid,
         scratch=[pltpu.VMEM((n, 3 * hid), jnp.float32)],
     )(pre, rows, rows, weights)
 
@@ -187,34 +167,83 @@
     )(mine, mine, other, other, deriv)
 
 
-def back_body(hid, blocks, deriv_ref, w_ref, other_ref, back_ref):
-    def write(part):
-        back_ref[...] = (part + other_ref[...].astype(jnp.float32)).astype(jnp.bfloat16)
+def back_body(hid, blocks, deriv_m_ref, deriv_o_ref, w_m_ref, w_o_ref, back_ref):
+    def write(cols):
+        mine = dot(deriv_m_ref[:, cols], w_m_ref[:, cols], ((1,), (1,)))
+        other = dot(deriv_o_ref[:, cols], w_o_ref[:, cols], ((1,), (1,)))
+        back_ref[...] = (mine + other).astype(jnp.bfloat16)
 
     @pl.when(pl.program_id(0) < blocks)
     def _():
-        write(dot(deriv_ref[:, 2 * hid :], w_ref[:, 2 * hid :], ((1,), (1,))))
+        write(slice(2 * hid, 3 * hid))
 
     @pl.when(pl.program_id(0) >= blocks)
     def _():
-        write(dot(deriv_ref[:, : 2 * hid], w_ref[:, : 2 * hid], ((1,), (1,))))
-
-
-def sent_back(deriv, weights, from_other, hid, blocks):
-    n, width = from_other.shape
-    cols = width // 2 // blocks
+        write(slice(0, 2 * hid))
+
+
+def sent_back(deriv_m, deriv_o, w_m, w_o, hid, blocks):
+    n = deriv_m.shape[0]
+    cols = w_o.shape[0] // blocks
+    deriv = pl.BlockSpec((n, 3 * hid), lambda i: (0, 0))
+    weight = pl.BlockSpec((cols, 3 * hid), lambda i: (lax.rem(i, blocks), 0))
     return call(
         functools.partial(back_body, hid, blocks),
         2 * blocks,
+        [deriv, deriv, weight, weight],
+        pl.BlockSpec((n, cols), lambda i: (0, i)),
+        jax.ShapeDtypeStruct((n, 2 * w_o.shape[0]), jnp.bfloat16),
+        flops=12 * n * w_o.shape[0] * hid,
+    )(deriv_m, deriv_o, w_m, w_o)
+
+
+def unpack_body(pick_ref, gate_ref, back_ref, near_ref, far_ref):
+    n = near_ref.shape[0]
+    picked = dot(pick_ref[...], back_ref[...])
+    picked = picked * jnp.where(pl.program_id(0) == 0, gate_ref[...], 1.0)
+    near_ref[...] = picked[:n].astype(jnp.bfloat16)
+    far_ref[...] = picked[n:].astype(jnp.bfloat16)
+
+
+def unpacked(pick, gate, back):
+    tokens, rows = pick.shape
+    half = back.shape[1] // 2
+    result = pl.BlockSpec((tokens // 2, half), lambda i: (0, i))
+    shape = jax.ShapeDtypeStruct((tokens // 2, 2 * half), jnp.bfloat16)
+    return call(
+        unpack_body,
+        2,
         [
-            pl.BlockSpec((n, 3 * hid), lambda i: (0, 0)),
-            pl.BlockSpec((cols, 3 * hid), lambda i: (lax.rem(i, blocks), 0)),
-            pl.BlockSpec((n, cols), lambda i: (0, i)),
+            pl.BlockSpec((tokens, rows), lambda i: (0, 0)),
+            pl.BlockSpec((tokens, 1), lambda i: (0, 0)),
+            pl.BlockSpec((rows, half), lambda i: (0, i)),
         ],
-        pl.BlockSpec((n, cols), lambda i: (0, i)),
-        jax.ShapeDtypeStruct((n, width), jnp.bfloat16),
-        flops=3 * n * width * hid,
-    )(deriv, weights, from_other)
+        [result, result],
+        [shape, shape],
+        flops=4 * tokens * rows * half,
+    )(pick, gate, back)
+
+
+def join_body(core_ref, near_ref, far_ref, out_ref, grad_ref):
+    half = near_ref.shape[1] // 2
+    first = core_ref[0] == 0
+    for ref, cols in ((out_ref, slice(0, half)), (grad_ref, slice(half, 2 * half))):
+        near, far = near_ref[:, cols], far_ref[:, cols]
+        ref[:, :half] = jnp.where(first, near, far)
+        ref[:, half:] = jnp.where(first, far, near)
+
+
+def joined(core, near, far):
+    whole = pl.BlockSpec(near.shape, lambda i: (0, 0))
+    shape = jax.ShapeDtypeStruct(near.shape, jnp.bfloat16)
+    return call(
+        join_body,
+        1,
+        [pl.BlockSpec(memory_space=pltpu.SMEM), whole, whole],
+        [whole, whole],
+        [shape, shape],
+        flops=near.size,
+    )(core.reshape(1), near, far)
 
 
 def shards(
@@ -260,35 +289,30 @@
     mine = got.reshape(n_chip * block, width)
     other = lax.ppermute(mine, "c", SWAP)
 
+    weights_o = lax.ppermute(weights[half:], "c", SWAP)
     pre = first_half(mine, weights, hid, BLOCKS)
-    parts_o, deriv = second_half(pre, other, weights, hid, BLOCKS)
-    from_other = lax.ppermute(parts_o, "c", SWAP)
+    deriv = second_half(pre, other, weights, hid, BLOCKS)
+    deriv, weights_o = lax.optimization_barrier((deriv, weights_o))
+    deriv_o = lax.ppermute(deriv, "c", SWAP)
     grad = weight_grads(mine, other, deriv, hid, BLOCKS)
+    grad, deriv_o = lax.optimization_barrier((grad, deriv_o))
     grad = lax.psum_scatter(
         grad, ("z", "c"), scatter_dimension=0, tiled=True, axis_index_groups=orders
     ).astype(jnp.float32)
 
-    back = sent_back(deriv, weights, from_other, hid, BLOCKS)
+    back = sent_back(deriv, deriv_o, weights, weights_o, hid, BLOCKS)
     back = lax.all_to_all(
         back.reshape(n_chip, block, width), "p", split_axis=0, concat_axis=0, tiled=True
     ).reshape(n_chip * block, width)
     unpick = (place2[:, None] == row_id[None, :]).astype(jnp.bfloat16)
-    summed = dot(unpick, back)
-    result = jnp.concatenate([summed[:, :half] * gate2, summed[:, half:]], axis=1).astype(jnp.bfloat16)
-    near = result[:tok_rows]
-    far = lax.ppermute(result[tok_rows:], "c", SWAP)
-
-    def joined(cols):
-        a, b = near[:, cols], far[:, cols]
-        first = jnp.where(c == 0, a, b)
-        second = jnp.where(c == 0, b, a)
-        return jnp.concatenate([first, second], axis=1)
-
-    outputs, input_grads = joined(slice(0, half)), joined(slice(half, width))
+    near, far = unpacked(unpick, gate2, back)
+    far = lax.ppermute(far, "c", SWAP)
     scale = (tok_rows * n_data * n_chip * n_core * routes.shape[1] / EXPERTS) ** (-0.5)
     grad_up = jnp.stack([grad[:, :hid], grad[:, hid : 2 * hid]])
     new_wu, new_mu, new_vu = adam_update(w_gate_up, m_gate_up, v_gate_up, grad_up, scale)
     new_wd, new_md, new_vd = adam_update(w_down, m_down, v_down, grad[:, 2 * hid :].T, scale)
+    far, new_mu = lax.optimization_barrier((far, new_mu))
+    outputs, input_grads = joined(c, near, far)
     return (outputs, input_grads, new_wu, new_mu, new_vu, new_wd, new_md, new_vd)
 
 

time: 199 us -> 214 us (1.075)
  waiting for transfers between devices: 6.71 us -> 70.6 us
  blocking collectives: 121 us -> 59.4 us
  Pallas kernels: 30.3 us -> 40.8 us
  starting transfers between devices: 7.58 us -> 14.1 us
  other arithmetic: 11.3 us -> 7.56 us
    all_to_all x0 -> x1, waiting for transfers between devices: none -> 67.9 us  [shards(): lax.all_to_all(back.reshape(n_chip, block, width), 'p', split_axis=0, con...]
    all_to_all x1 -> x0, blocking collectives: 61.2 us -> none  [shards(): lax.all_to_all(back.reshape(n_chip, block, width), 'p', split_axis=0, con...]
    pallas_call x2 -> x4, Pallas kernels: 16.7 us -> 24 us  [the longest x1 10 us: sent_back(): call(functools.partial(back_body, hid, blocks), 2 * blocks, [deriv, deriv...]
    all_to_all x0 -> x1, starting transfers between devices: none -> 6.58 us  [shards(): lax.all_to_all(back.reshape(n_chip, block, width), 'p', split_axis=0, con...]
    concatenate x3 -> x0, other arithmetic: 2.95 us -> none  [the longest x2 1.96 us: joined(): return jnp.concatenate([first, second], axis=1)]
    all_gather x1, waiting for transfers between devices: 3.95 us -> 1.45 us  [shards(): lax.all_gather(owned, ('z', 'c'), axis=0, tiled=True, axis_index_groups=o...]
    ppermute x2 -> x3, waiting for transfers between devices: 2.44 us -> 0.01 us  [the longest x1 0.01 us: shards(): weights_o = lax.ppermute(weights[half:], 'c', SWAP)]
    unnamed x20 -> x25, local copies, waits for them, and re-layouts: 3.23 us -> 0.86 us
  transfers between devices with their start and end apart: 7 -> 9, of which waited for: 4 -> 4; matrix products, arithmetic and copies ran while one was open for 5% -> 5% of each run, Pallas kernels for 10% -> 18%
where the time goes in v3:
time: 214 us
  waiting for transfers between devices  70.6 us (33%)
  blocking collectives  59.4 us (28%)
  Pallas kernels  40.8 us (19%)
  between operations  14.3 us (7%)
  starting transfers between devices  14.1 us (7%)
  other arithmetic  7.56 us (4%)
  local copies, waits for them, and re-layouts  4.25 us (2%)
  matrix products  2.73 us (1%)
    all_to_all x1, waiting for transfers between devices, shards(): lax.all_to_all(back.reshape(n_chip, block, width), 'p', split_axis=0, con...  67.9 us
    all_to_all x1, blocking collectives, shards(): got = lax.all_to_all(packed, 'p', split_axis=0, concat_axis=0, tiled=True)  59.4 us
    pallas_call x1, Pallas kernels, weight_grads(): call(functools.partial(grad_body, hid, blocks), 2 * blocks, [pl.BlockSpec...  11 us
    pallas_call x1, Pallas kernels, sent_back(): call(functools.partial(back_body, hid, blocks), 2 * blocks, [deriv, deriv...  10 us
    pallas_call x1, Pallas kernels, second_half(): call(functools.partial(mid_body, hid, blocks), blocks, [pl.BlockSpec((n,...  6.89 us
    all_to_all x1, starting transfers between devices, shards(): lax.all_to_all(back.reshape(n_chip, block, width), 'p', split_axis=0, con...  6.58 us
    pallas_call x1, Pallas kernels, first_half(): call(functools.partial(pre_body, hid), blocks, [pl.BlockSpec((n, cols), l...  5.84 us
    pallas_call x1, Pallas kernels, unpacked(): call(unpack_body, 2, [pl.BlockSpec((tokens, rows), lambda i: (0, 0)), pl....  4.4 us
  transfers between devices with their start and end apart: 9, of which 4 were waited for; matrix products, arithmetic and copies ran while one was open for 5% of the time, Pallas kernels for 18%

profile of v3, /device:TPU:1, one launch (start us, length us, event | category | flops | bytes accessed | tf_op | source)
XLA Modules:
  0.0 213.8 jit_solution(15788387065781013308)
XLA Ops:
  7.2 0.0 copy-start.10
  7.2 0.0 copy-start.2
  7.2 0.0 all-gather.2.cloned.1.call-start
  7.2 1.2 slice_bitcast_fusion.3
  8.4 0.0 copy-start.4
  8.4 1.9 pad_maximum_fusion.2
  10.3 0.0 all-gather.2.cloned.1.call-update
  10.3 0.0 reduce-scatter.2.cloned.1.call-start
  10.4 0.0 copy-done.10
  10.4 0.0 copy-done.2
  10.4 0.2 multiply_convert_fusion
  10.6 0.0 copy-done.4
  10.6 0.1 constant_dynamic-slice_fusion.2
  10.8 0.0 copy-start.11
  10.8 0.1 pad_maximum_fusion
  10.9 3.3 %collective-permute-start.1 = (bf16[128,3584]{1,0:T(8,128)(2,1)S(1)}, bf16[128,3584]{1,0:T(8,128)(2,1)}, u32[]{:S(2)}, u32[]{:S(2)}) collective-permute-start(bf16[128,3584]{1,0:T(8,128)(2,1)S(1)} %pad_maximum_fusion), channel_id=1, source_target_pairs={{0,1},{1,0},{2,3},{3,2},{4,5},{5,4},{6,7},{7,6},{8,9},{9,8},{10,11... | collective-permute-start | bytes 2752520 | tf_op jit(solution)/shard_map/ppermute | solution.py:281
  14.2 0.0 copy-done.11
  14.2 0.1 fusion.5
  14.4 0.6 collective-permute-start
  15.0 0.1 iota_add_fusion
  15.0 0.1 add.67
  15.1 1.2 collective-permute-done
  16.3 0.1 collective-permute-done.1
  16.4 2.6 %convolution_convert_fusion = bf16[640,3584]{1,0:T(8,128)(2,1)S(1)} fusion(bf16[128,3584]{1,0:T(8,128)(2,1)} %collective-permute-done.1, bf16[128,1792]{1,0:T(8,128)(2,1)S(1)} %get-tuple-element.38, bf16[128,1792]{1,0:T(8,128)(2,1)S(1)} %get-tuple-element.45, s32[256]{0:T(256)S(1)} %bitcast.31, s32[640]{0:T(1024)S(1)} %add.67), kind=kOutput, calls=%fused_computation | convolution fusion | flops 1182367744 | bytes 6426112 | tf_op jit(solution)/shard_map/dot_general | solution.py:45
  19.0 59.4 %all_to_all.10 = bf16[16,40,3584]{2,1,0:T(8,128)(2,1)} all-to-all(bf16[16,40,3584]{2,1,0:T(8,128)(2,1)S(1)} %bitcast.28), channel_id=1, replica_groups=mesh['z'=8,'p'=16,'c'=2] {'p'}, dimensions={0} | all-to-all | bytes 9175040 | tf_op jit(solution)/shard_map/all_to_all | solution.py:288
  78.4 1.5 collective-permute-start.2
  80.0 1.4 all-gather.2.cloned.1.call-done.w_ref.w_m_ref
  81.4 2.0 slice.34
  83.4 0.8 collective-permute-start.3
  84.1 5.8 %shard_map.161.pre_ref = f32[640,768]{1,0:T(8,128)} custom-call(bf16[640,3584]{1,0:T(8,128)(2,1)} %bitcast.6.x_ref.y_ref.xm_ref.ym_ref, bf16[640,3584]{1,0:T(8,128)(2,1)} %bitcast.6.x_ref.y_ref.xm_ref.ym_ref, bf16[3584,768]{1,0:T(8,128)(2,1)} %all-gather.2.cloned.1.call-done.w_ref.w_m_ref), custom_call_target="tpu_custom_call" | custom-call | flops 1761607680 | bytes 12582912 | tf_op jit(solution)/shard_map/pallas_call | solution.py:77
  90.0 0.0 collective-permute-done.2.x_ref.y_ref.xo_ref.yo_ref
  90.0 6.9 %shard_map.162.deriv_ref.deriv_m_ref = bf16[640,768]{1,0:T(8,128)(2,1)} custom-call(f32[640,768]{1,0:T(8,128)} %shard_map.161.pre_ref, bf16[640,3584]{1,0:T(8,128)(2,1)} %collective-permute-done.2.x_ref.y_ref.xo_ref.yo_ref, bf16[640,3584]{1,0:T(8,128)(2,1)} %collective-permute-done.2.x_ref.y_ref.xo_ref.yo_ref, ...), custom_call_target="tpu_custom_call" | custom-call | flops 1761607680 | bytes 12582912 | tf_op jit(solution)/shard_map/pallas_call | solution.py:114
  96.9 0.0 collective-permute-done.3.w_o_ref
  96.9 0.0 copy-start
  96.9 0.1 collective-permute-start.4
  97.0 11.0 %shard_map.163 = bf16[3584,768]{1,0:T(8,128)(2,1)} custom-call(bf16[640,3584]{1,0:T(8,128)(2,1)} %bitcast.6.x_ref.y_ref.xm_ref.ym_ref, bf16[640,3584]{1,0:T(8,128)(2,1)} %bitcast.6.x_ref.y_ref.xm_ref.ym_ref, bf16[640,3584]{1,0:T(8,128)(2,1)} %collective-permute-done.2.x_ref.y_ref.xo_ref.yo_ref, ...), custom_call_target="tpu_custom_call" | custom-call | flops 3523215360 | bytes 12582912 | tf_op jit(solution)/shard_map/pallas_call | solution.py:154
  107.9 0.0 copy-done
  107.9 0.0 collective-permute-done.4.deriv_o_ref
  107.9 0.0 reduce-scatter.2.cloned.1.call-update
  108.0 10.0 %shard_map.164 = bf16[640,3584]{1,0:T(8,128)(2,1)} custom-call(bf16[640,768]{1,0:T(8,128)(2,1)} %shard_map.162.deriv_ref.deriv_m_ref, bf16[640,768]{1,0:T(8,128)(2,1)} %collective-permute-done.4.deriv_o_ref, bf16[3584,768]{1,0:T(8,128)(2,1)} %all-gather.2.cloned.1.call-done.w_ref.w_m_ref, bf16[1792,768]{1,0:T(8,128)(2,1)} %copy-done), custom_call_target="tpu_custom_call" | custom-call | flops 3523215360 | bytes 12582912 | tf_op jit(solution)/shard_map/pallas_call | solution.py:190
  118.0 6.6 %all-to-all-start.1 = ((bf16[16,40,3584]{2,1,0:T(8,128)(2,1)}), bf16[16,40,3584]{2,1,0:T(8,128)(2,1)}, u32[]{:S(2)}, u32[]{:S(2)}) async-start(bf16[16,40,3584]{2,1,0:T(8,128)(2,1)} %bitcast.27), calls=%async_computation.1 | async-start | bytes 9175040 | tf_op jit(solution)/shard_map/all_to_all | solution.py:304
  124.6 0.8 copy.29.gate_ref
  125.4 0.8 compare_convert_fusion.pick_ref
  126.2 67.9 %all-to-all-done.1 = bf16[16,40,3584]{2,1,0:T(8,128)(2,1)} async-done(((bf16[16,40,3584]{2,1,0:T(8,128)(2,1)}), bf16[16,40,3584]{2,1,0:T(8,128)(2,1)}, u32[]{:S(2)}, u32[]{:S(2)}) %all-to-all-start.1) | async-done | bytes 4587552 | tf_op jit(solution)/shard_map/all_to_all | solution.py:304
  194.1 4.4 %shard_map.165 = (bf16[128,3584]{1,0:T(8,128)(2,1)}, bf16[128,3584]{1,0:T(8,128)(2,1)}) custom-call(bf16[256,640]{1,0:T(8,128)(2,1)} %compare_convert_fusion.pick_ref, f32[256,1]{1,0:T(8,128)} %copy.29.gate_ref, bf16[640,3584]{1,0:T(8,128)(2,1)} %bitcast.11.back_ref), custom_call_target="tpu_custom_call" | custom-call | flops 1174405120 | bytes 12582912 | tf_op jit(solution)/shard_map/pallas_call | solution.py:213
  198.5 0.0 copy-start.1
  198.5 0.0 copy-start.5
  198.5 1.2 collective-permute-start.5
  199.7 1.2 convert_element_type.71
  200.9 0.1 slice_bitcast_fusion.1
  200.9 0.0 copy-done.1
  200.9 0.0 copy-done.5
  200.9 0.0 copy-done.6
  201.0 0.0 copy-start.7
  201.0 0.0 copy-start.8
  201.0 0.0 copy-start.9
  201.0 1.9 subtract_convert_fusion
  202.9 0.0 collective-permute-done.5.far_ref
  202.9 0.0 copy-done.7
  202.9 0.0 copy-done.8
  203.0 0.0 copy-done.9
  203.0 1.3 subtract_convert_fusion.1
  204.2 0.0 copy-done.3
  204.2 2.7 %shard_map.166 = (bf16[128,3584]{1,0:T(8,128)(2,1)}, bf16[128,3584]{1,0:T(8,128)(2,1)}) custom-call(s32[1]{0:T(128)} %bitcast.core_ref, bf16[128,3584]{1,0:T(8,128)(2,1)} %get-tuple-element.21.near_ref, bf16[128,3584]{1,0:T(8,128)(2,1)} %copy-done.3), custom_call_target="tpu_custom_call" | custom-call | flops 458752 | bytes 12582912 | tf_op jit(solution)/shard_map/pallas_call | solution.py:239
  (8 shorter events, 0.0 us)
Async XLA Ops:
  7.2 3.2 %copy-start.10 = (f32[128,1]{0,1:T(1,128)S(1)}, f32[128,1]{0,1:T(1,128)}, u32[]{:S(2)}) copy-start(f32[128,1]{0,1:T(1,128)} %param.13) | copy-start | bytes 1540
  7.2 3.2 %copy-start.2 = (bf16[128,3584]{1,0:T(8,128)(2,1)S(1)}, bf16[128,3584]{1,0:T(8,128)(2,1)}, u32[]{:S(2)}) copy-start(bf16[128,3584]{1,0:T(8,128)(2,1)} %param.11) | copy-start | bytes 2752516
  7.2 74.2 %all-gather.2.cloned.1.call-start = ((), (), s32[]{:S(2)}) async-start(), calls=%async_computation.3 | async-start | bytes 6193152 | tf_op jit(solution)/shard_map/all_gather | solution.py:265
  8.4 2.2 %copy-start.4 = (bf16[128,3584]{1,0:T(8,128)(2,1)S(1)}, bf16[128,3584]{1,0:T(8,128)(2,1)}, u32[]{:S(2)}) copy-start(bf16[128,3584]{1,0:T(8,128)(2,1)} %param.10) | copy-start | bytes 2752516
  10.3 189.3 %reduce-scatter.2.cloned.1.call-start = ((), (), s32[]{:S(2)}) async-start(), calls=%async_computation.4 | async-start | bytes 6193152 | tf_op jit(solution)/shard_map/reduce_scatter | solution.py:299
  10.8 3.4 %copy-start.11 = (s32[128,1]{0,1:T(1,128)S(1)}, s32[128,1]{0,1:T(1,128)}, u32[]{:S(2)}) copy-start(s32[128,1]{0,1:T(1,128)} %param.12) | copy-start | bytes 1540
  10.9 5.6 %collective-permute-start.1 = (bf16[128,3584]{1,0:T(8,128)(2,1)S(1)}, bf16[128,3584]{1,0:T(8,128)(2,1)}, u32[]{:S(2)}, u32[]{:S(2)}) collective-permute-start(bf16[128,3584]{1,0:T(8,128)(2,1)S(1)} %pad_maximum_fusion), channel_id=1, source_target_pairs={{0,1},{1,0},{2,3},{3,2},{4,5},{5,4},{6,7},{7,6},{8,9},{9,8},{10,11... | collective-permute-start | bytes 2752520 | tf_op jit(solution)/shard_map/ppermute | solution.py:281
  14.4 1.9 collective-permute-start
  78.4 11.6 %collective-permute-start.2 = (bf16[640,3584]{1,0:T(8,128)(2,1)}, bf16[640,3584]{1,0:T(8,128)(2,1)}, u32[]{:S(2)}, u32[]{:S(2)}) collective-permute-start(bf16[640,3584]{1,0:T(8,128)(2,1)} %bitcast.6.x_ref.y_ref.xm_ref.ym_ref), channel_id=1, source_target_pairs={{0,1},{1,0},{2,3},{3,2},{4,5},{5,4},{6,7},{7,6},{8,9},{9,8},{10,11... | collective-permute-start | bytes 13762568 | tf_op jit(solution)/shard_map/ppermute | solution.py:290
  83.4 13.5 %collective-permute-start.3 = (bf16[1792,768]{1,0:T(8,128)(2,1)S(1)}, bf16[1792,768]{1,0:T(8,128)(2,1)S(1)}, u32[]{:S(2)}, u32[]{:S(2)}) collective-permute-start(bf16[1792,768]{1,0:T(8,128)(2,1)S(1)} %slice.34), channel_id=1, source_target_pairs={{0,1},{1,0},{2,3},{3,2},{4,5},{5,4},{6,7},{7,6},{8,9},{9,8},{10,11... | collective-permute-start | bytes 8257544 | tf_op jit(solution)/shard_map/ppermute | solution.py:292
  96.9 11.1 %copy-start = (bf16[1792,768]{1,0:T(8,128)(2,1)}, bf16[1792,768]{1,0:T(8,128)(2,1)S(1)}, u32[]{:S(2)}) copy-start(bf16[1792,768]{1,0:T(8,128)(2,1)S(1)} %collective-permute-done.3.w_o_ref) | copy-start | bytes 8257540
  96.9 11.1 %collective-permute-start.4 = (bf16[640,768]{1,0:T(8,128)(2,1)}, bf16[640,768]{1,0:T(8,128)(2,1)}, u32[]{:S(2)}, u32[]{:S(2)}) collective-permute-start(bf16[640,768]{1,0:T(8,128)(2,1)} %shard_map.162.deriv_ref.deriv_m_ref), channel_id=1, source_target_pairs={{0,1},{1,0},{2,3},{3,2},{4,5},{5,4},{6,7},{7,6},{8,9},{9,8},{10,11... | collective-permute-start | bytes 2949128 | tf_op jit(solution)/shard_map/ppermute | solution.py:296
  118.0 76.1 %all-to-all-start.1 = ((bf16[16,40,3584]{2,1,0:T(8,128)(2,1)}), bf16[16,40,3584]{2,1,0:T(8,128)(2,1)}, u32[]{:S(2)}, u32[]{:S(2)}) async-start(bf16[16,40,3584]{2,1,0:T(8,128)(2,1)} %bitcast.27), calls=%async_computation.1 | async-start | bytes 9175040 | tf_op jit(solution)/shard_map/all_to_all | solution.py:304
  198.5 2.4 %copy-start.1 = (bf16[2,448,256]{2,1,0:T(8,128)(2,1)S(1)}, bf16[2,448,256]{2,1,0:T(8,128)(2,1)}, u32[]{:S(2)}) copy-start(bf16[2,448,256]{2,1,0:T(8,128)(2,1)} %param.14) | copy-start | bytes 1376260
  198.5 2.5 %copy-start.5 = (f32[2,448,256]{2,1,0:T(8,128)S(1)}, f32[2,448,256]{2,1,0:T(8,128)}, u32[]{:S(2)}) copy-start(f32[2,448,256]{2,1,0:T(8,128)} %param.17) | copy-start | bytes 2752516
  198.5 2.5 %copy-start.6 = (f32[2,448,256]{2,1,0:T(8,128)S(1)}, f32[2,448,256]{2,1,0:T(8,128)}, u32[]{:S(2)}) copy-start(f32[2,448,256]{2,1,0:T(8,128)} %param.16) | copy-start | bytes 2752516
  198.5 4.4 %collective-permute-start.5 = (bf16[128,3584]{1,0:T(8,128)(2,1)}, bf16[128,3584]{1,0:T(8,128)(2,1)S(1)}, u32[]{:S(2)}, u32[]{:S(2)}) collective-permute-start(bf16[128,3584]{1,0:T(8,128)(2,1)} %get-tuple-element.22), channel_id=1, source_target_pairs={{0,1},{1,0},{2,3},{3,2},{4,5},{5,4},{6,7},{7,6},{8,9},{9,8},{10,11... | collective-permute-start | bytes 2752520 | tf_op jit(solution)/shard_map/ppermute | solution.py:309
  201.0 2.0 copy-start.7
  201.0 2.0 copy-start.8
  201.0 2.0 copy-start.9
  202.9 1.3 copy-start.3
Sparse Core Ops, SparseCore 0:
  10.5 70.8 all-gather.1
  108.1 65.8 reduce-scatter.1

commit v4 on v3

--- a/solution.py
+++ b/solution.py
@@ -46,7 +46,10 @@
 
 
 MIB = 1 << 20
-VMEM = 57
+VMEM = 56
+BACK_VMEM = 40
+GRAD_VMEM = 56
+LANES = 128
 
 
 def call(body, grid, in_specs, out_specs, out_shape, flops, scratch=(), vmem=VMEM):
@@ -88,15 +91,22 @@
     )(rows, rows, weights)
 
 
-def mid_body(hid, blocks, pre_ref, x_ref, y_ref, w_ref, deriv_ref, acc_ref):
+def write_grads(hid, x, y, deriv_ref, grad_ref):
+    grad_ref[:, : 2 * hid] = dot(x, deriv_ref[:, : 2 * hid], ((0,), (0,))).astype(jnp.bfloat16)
+    grad_ref[:, 2 * hid :] = dot(y, deriv_ref[:, 2 * hid :], ((0,), (0,))).astype(jnp.bfloat16)
+
+
+def mid_body(hid, blocks, pre_ref, x_ref, y_ref, w_ref, deriv_ref, grad_ref, acc_ref):
     step = pl.program_id(0)
 
     @pl.when(step == 0)
     def _():
         acc_ref[...] = pre_ref[...]
 
-    acc_ref[:, : 2 * hid] += dot(x_ref[...], w_ref[:, : 2 * hid])
-    acc_ref[:, 2 * hid :] += dot(y_ref[...], w_ref[:, 2 * hid :])
+    @pl.when(step < blocks)
+    def _():
+        acc_ref[:, : 2 * hid] += dot(x_ref[...], w_ref[:, : 2 * hid])
+        acc_ref[:, 2 * hid :] += dot(y_ref[...], w_ref[:, 2 * hid :])
 
     @pl.when(step == blocks - 1)
     def _():
@@ -107,77 +117,75 @@
         deriv_ref[:, hid : 2 * hid] = (d_hidden * gated).astype(jnp.bfloat16)
         deriv_ref[:, 2 * hid :] = (gated * linear).astype(jnp.bfloat16)
 
+    @pl.when(step >= blocks)
+    def _():
+        write_grads(hid, x_ref[...], y_ref[...], deriv_ref, grad_ref)
+
 
 def second_half(pre, rows, weights, hid, blocks):
     n, width = rows.shape
     cols = width // 2 // blocks
+
+    def at(i):
+        return jnp.minimum(i, 2 * blocks - 1 - i)
+
     return call(
         functools.partial(mid_body, hid, blocks),
-        blocks,
+        2 * blocks,
         [
             pl.BlockSpec((n, 3 * hid), lambda i: (0, 0)),
+            pl.BlockSpec((n, cols), lambda i: (0, at(i))),
+            pl.BlockSpec((n, cols), lambda i: (0, blocks + at(i))),
+            pl.BlockSpec((cols, 3 * hid), lambda i: (blocks + jnp.minimum(i, blocks - 1), 0)),
+        ],
+        [
+            pl.BlockSpec((n, 3 * hid), lambda i: (0, 0)),
+            pl.BlockSpec((cols, 3 * hid), lambda i: (blocks + jnp.minimum(blocks - 1, 2 * blocks - 1 - i), 0)),
+        ],
+        [
+            jax.ShapeDtypeStruct((n, 3 * hid), jnp.bfloat16),
+            jax.ShapeDtypeStruct((width, 3 * hid), jnp.bfloat16),
+        ],
+        flops=6 * n * width * hid,
+        scratch=[pltpu.VMEM((n, 3 * hid), jnp.float32)],
+    )(pre, rows, rows, weights)
+
+
+def grad_body(hid, x_ref, y_ref, deriv_ref, _, grad_ref):
+    write_grads(hid, x_ref[...], y_ref[...], deriv_ref, grad_ref)
+
+
+def first_grads(rows, deriv, grad, hid, blocks):
+    n, width = rows.shape
+    cols = width // 2 // blocks
+    return pl.pallas_call(
+        functools.partial(grad_body, hid),
+        grid=(blocks,),
+        in_specs=[
             pl.BlockSpec((n, cols), lambda i: (0, i)),
             pl.BlockSpec((n, cols), lambda i: (0, blocks + i)),
-            pl.BlockSpec((cols, 3 * hid), lambda i: (blocks + i, 0)),
-        ],
-        pl.BlockSpec((n, 3 * hid), lambda i: (0, 0)),
-        jax.ShapeDtypeStruct((n, 3 * hid), jnp.bfloat16),
-        flops=3 * n * width * hid,
-        scratch=[pltpu.VMEM((n, 3 * hid), jnp.float32)],
-    )(pre, rows, rows, weights)
-
-
-def grad_body(hid, blocks, xm_ref, ym_ref, xo_ref, yo_ref, deriv_ref, grad_ref):
-    def write(x, y):
-        grad_ref[:, : 2 * hid] = dot(x, deriv_ref[:, : 2 * hid], ((0,), (0,))).astype(jnp.bfloat16)
-        grad_ref[:, 2 * hid :] = dot(y, deriv_ref[:, 2 * hid :], ((0,), (0,))).astype(jnp.bfloat16)
-
-    @pl.when(pl.program_id(0) < blocks)
-    def _():
-        write(xm_ref[...], ym_ref[...])
-
-    @pl.when(pl.program_id(0) >= blocks)
-    def _():
-        write(xo_ref[...], yo_ref[...])
-
-
-def weight_grads(mine, other, deriv, hid, blocks):
-    n, width = mine.shape
-    cols = width // 2 // blocks
-
-    def early(i):
-        return jnp.minimum(i, blocks - 1)
-
-    def late(i):
-        return jnp.maximum(i - blocks, 0)
-
-    return call(
-        functools.partial(grad_body, hid, blocks),
-        2 * blocks,
-        [
-            pl.BlockSpec((n, cols), lambda i: (0, early(i))),
-            pl.BlockSpec((n, cols), lambda i: (0, blocks + early(i))),
-            pl.BlockSpec((n, cols), lambda i: (0, late(i))),
-            pl.BlockSpec((n, cols), lambda i: (0, blocks + late(i))),
             pl.BlockSpec((n, 3 * hid), lambda i: (0, 0)),
-        ],
-        pl.BlockSpec((cols, 3 * hid), lambda i: (i, 0)),
-        jax.ShapeDtypeStruct((width, 3 * hid), jnp.bfloat16),
-        flops=6 * n * width * hid,
-    )(mine, mine, other, other, deriv)
-
-
-def back_body(hid, blocks, deriv_m_ref, deriv_o_ref, w_m_ref, w_o_ref, back_ref):
+            pl.BlockSpec(memory_space=pl.ANY),
+        ],
+        out_specs=pl.BlockSpec((cols, 3 * hid), lambda i: (i, 0)),
+        out_shape=jax.ShapeDtypeStruct((width, 3 * hid), jnp.bfloat16),
+        input_output_aliases={3: 0},
+        compiler_params=pltpu.CompilerParams(vmem_limit_bytes=GRAD_VMEM * MIB),
+        cost_estimate=pl.CostEstimate(flops=3 * n * width * hid, bytes_accessed=12 * MIB, transcendentals=0),
+    )(rows, rows, deriv, grad)
+
+
+def back_body(hid, deriv_m_ref, deriv_o_ref, w_m_ref, w_o_ref, back_ref):
     def write(cols):
         mine = dot(deriv_m_ref[:, cols], w_m_ref[:, cols], ((1,), (1,)))
         other = dot(deriv_o_ref[:, cols], w_o_ref[:, cols], ((1,), (1,)))
         back_ref[...] = (mine + other).astype(jnp.bfloat16)
 
-    @pl.when(pl.program_id(0) < blocks)
+    @pl.when(lax.rem(pl.program_id(0), 2) == 0)
     def _():
         write(slice(2 * hid, 3 * hid))
 
-    @pl.when(pl.program_id(0) >= blocks)
+    @pl.when(lax.rem(pl.program_id(0), 2) == 1)
     def _():
         write(slice(0, 2 * hid))
 
@@ -186,21 +194,22 @@
     n = deriv_m.shape[0]
     cols = w_o.shape[0] // blocks
     deriv = pl.BlockSpec((n, 3 * hid), lambda i: (0, 0))
-    weight = pl.BlockSpec((cols, 3 * hid), lambda i: (lax.rem(i, blocks), 0))
-    return call(
-        functools.partial(back_body, hid, blocks),
+    weight = pl.BlockSpec((cols, 3 * hid), lambda i: (lax.div(i, 2), 0))
+    return call(
+        functools.partial(back_body, hid),
         2 * blocks,
         [deriv, deriv, weight, weight],
-        pl.BlockSpec((n, cols), lambda i: (0, i)),
+        pl.BlockSpec((n, cols), lambda i: (0, lax.div(i, 2) + blocks * lax.rem(i, 2))),
         jax.ShapeDtypeStruct((n, 2 * w_o.shape[0]), jnp.bfloat16),
         flops=12 * n * w_o.shape[0] * hid,
+        vmem=BACK_VMEM,
     )(deriv_m, deriv_o, w_m, w_o)
 
 
 def unpack_body(pick_ref, gate_ref, back_ref, near_ref, far_ref):
     n = near_ref.shape[0]
     picked = dot(pick_ref[...], back_ref[...])
-    picked = picked * jnp.where(pl.program_id(0) == 0, gate_ref[...], 1.0)
+    picked = picked * jnp.where(pl.program_id(0) == 0, gate_ref[:, :1], 1.0)
     near_ref[...] = picked[:n].astype(jnp.bfloat16)
     far_ref[...] = picked[n:].astype(jnp.bfloat16)
 
@@ -215,12 +224,13 @@
         2,
         [
             pl.BlockSpec((tokens, rows), lambda i: (0, 0)),
-            pl.BlockSpec((tokens, 1), lambda i: (0, 0)),
+            pl.BlockSpec((tokens, LANES), lambda i: (0, 0)),
             pl.BlockSpec((rows, half), lambda i: (0, i)),
         ],
         [result, result],
         [shape, shape],
         flops=4 * tokens * rows * half,
+        vmem=20,
     )(pick, gate, back)
 
 
@@ -243,6 +253,7 @@
         [whole, whole],
         [shape, shape],
         flops=near.size,
+        vmem=20,
     )(core.reshape(1), near, far)
 
 
@@ -261,9 +272,6 @@
         for k in range(n_core)
     ]
 
-    owned = jnp.concatenate([w_gate_up[0], w_gate_up[1], w_down.T], axis=1)
-    weights = lax.all_gather(owned, ("z", "c"), axis=0, tiled=True, axis_index_groups=orders)
-
     flat = routes.reshape(-1)
     place = flat * block + c * CAPACITY + slots_of(flat)
     info = jnp.concatenate([place.astype(jnp.float32)[:, None], gates], axis=1)
@@ -278,7 +286,10 @@
     def both_of(k):
         return jnp.concatenate([half_of(tokens, k), half_of(cot, k)], axis=1)
 
-    rows2 = jnp.concatenate([both_of(c), lax.ppermute(both_of(1 - c), "c", SWAP)], axis=0)
+    sent, w_up, w_dn = lax.optimization_barrier((both_of(1 - c), w_gate_up, w_down))
+    owned = jnp.concatenate([w_up[0], w_up[1], w_dn.T], axis=1)
+    weights = lax.all_gather(owned, ("z", "c"), axis=0, tiled=True, axis_index_groups=orders)
+    rows2 = jnp.concatenate([both_of(c), lax.ppermute(sent, "c", SWAP)], axis=0)
     row_id = lax.broadcasted_iota(jnp.int32, (EXPERTS, pair, block), 0) * block + (
         lax.broadcasted_iota(jnp.int32, (EXPERTS, pair, block), 2)
     )
@@ -286,15 +297,19 @@
     pick = (row_id[:, None] == place2[None, :]).astype(jnp.bfloat16)
     packed = dot(pick, rows2).astype(jnp.bfloat16).reshape(n_chip, block, width)
     got = lax.all_to_all(packed, "p", split_axis=0, concat_axis=0, tiled=True)
+    got, place2, gate2 = lax.optimization_barrier((got, place2, gate2))
     mine = got.reshape(n_chip * block, width)
+    unpick = (place2[:, None] == row_id[None, :]).astype(jnp.bfloat16)
+    gate2 = jnp.broadcast_to(gate2, (gate2.shape[0], LANES))
     other = lax.ppermute(mine, "c", SWAP)
 
     weights_o = lax.ppermute(weights[half:], "c", SWAP)
-    pre = first_half(mine, weights, hid, BLOCKS)
-    deriv = second_half(pre, other, weights, hid, BLOCKS)
+    ready, unpick, gate2 = lax.optimization_barrier((mine, unpick, gate2))
+    pre = first_half(ready, weights, hid, BLOCKS)
+    deriv, grad = second_half(pre, other, weights, hid, BLOCKS)
     deriv, weights_o = lax.optimization_barrier((deriv, weights_o))
     deriv_o = lax.ppermute(deriv, "c", SWAP)
-    grad = weight_grads(mine, other, deriv, hid, BLOCKS)
+    grad = first_grads(mine, deriv, grad, hid, BLOCKS)
     grad, deriv_o = lax.optimization_barrier((grad, deriv_o))
     grad = lax.psum_scatter(
         grad, ("z", "c"), scatter_dimension=0, tiled=True, axis_index_groups=orders
@@ -304,7 +319,6 @@
     back = lax.all_to_all(
         back.reshape(n_chip, block, width), "p", split_axis=0, concat_axis=0, tiled=True
     ).reshape(n_chip * block, width)
-    unpick = (place2[:, None] == row_id[None, :]).astype(jnp.bfloat16)
     near, far = unpacked(unpick, gate2, back)
     far = lax.ppermute(far, "c", SWAP)
     scale = (tok_rows * n_data * n_chip * n_core * routes.shape[1] / EXPERTS) ** (-0.5)

time: 214 us -> 196 us (0.916)
  waiting for transfers between devices: 70.6 us -> 3.71 us
  blocking collectives: 59.4 us -> 120 us
  Pallas kernels: 40.8 us -> 32.1 us
  starting transfers between devices: 14.1 us -> 7.53 us
  local copies, waits for them, and re-layouts: 4.25 us -> 8.06 us
    all_to_all x1 -> x0, waiting for transfers between devices: 67.9 us -> none  [shards(): lax.all_to_all(back.reshape(n_chip, block, width), 'p', split_axis=0, con...]
    all_to_all x0 -> x1, blocking collectives: none -> 60.7 us  [shards(): lax.all_to_all(back.reshape(n_chip, block, width), 'p', split_axis=0, con...]
    all_to_all x1 -> x0, starting transfers between devices: 6.58 us -> none  [shards(): lax.all_to_all(back.reshape(n_chip, block, width), 'p', split_axis=0, con...]
    pallas_call x3, Pallas kernels: 27.9 us -> 22.7 us  [the longest x1 10.3 us: second_half(): call(functools.partial(mid_body, hid, blocks), 2 * blocks, [pl.BlockSpec(...]
    unnamed x25 -> x26, local copies, waits for them, and re-layouts: 0.86 us -> 5.71 us
    pallas_call x1, Pallas kernels: 4.4 us -> 2.23 us  [unpacked(): call(unpack_body, 2, [pl.BlockSpec((tokens, rows), lambda i: (0, 0)), pl....]
  transfers between devices with their start and end apart: 9 -> 8, of which waited for: 4 -> 3; matrix products, arithmetic and copies ran while one was open for 5% -> 4% of each run, Pallas kernels for 18% -> 16%
where the time goes in v4:
time: 196 us
  blocking collectives  120 us (61%)
  Pallas kernels  32.1 us (16%)
  between operations  14.2 us (7%)
  local copies, waits for them, and re-layouts  8.06 us (4%)
  starting transfers between devices  7.53 us (4%)
  other arithmetic  7.11 us (4%)
  waiting for transfers between devices  3.71 us (2%)
  matrix products  2.72 us (1%)
    all_to_all x1, blocking collectives, shards(): lax.all_to_all(back.reshape(n_chip, block, width), 'p', split_axis=0, con...  60.7 us
    all_to_all x1, blocking collectives, shards(): got = lax.all_to_all(packed, 'p', split_axis=0, concat_axis=0, tiled=True)  59.4 us
    pallas_call x1, Pallas kernels, second_half(): call(functools.partial(mid_body, hid, blocks), 2 * blocks, [pl.BlockSpec(...  10.3 us
    pallas_call x1, Pallas kernels, sent_back(): call(functools.partial(back_body, hid), 2 * blocks, [deriv, deriv, weight...  6.7 us
    pallas_call x1, Pallas kernels, first_half(): call(functools.partial(pre_body, hid), blocks, [pl.BlockSpec((n, cols), l...  5.89 us
    unnamed x26, local copies, waits for them, and re-layouts  5.71 us
    pallas_call x1, Pallas kernels, first_grads(): pl.pallas_call(functools.partial(grad_body, hid), grid=(blocks,), in_spec...  5.64 us
  transfers between devices with their start and end apart: 8, of which 3 were waited for; matrix products, arithmetic and copies ran while one was open for 4% of the time, Pallas kernels for 16%

profile of v4, /device:TPU:1, one launch (start us, length us, event | category | flops | bytes accessed | tf_op | source)
XLA Modules:
  0.0 195.7 jit_solution(10617533477280223733)
XLA Ops:
  7.2 0.0 copy-start.5
  7.2 0.0 all-gather.2.cloned.1.call-start
  7.2 1.5 multiply_convert_fusion
  8.7 0.0 copy-done.5
  8.7 0.1 constant_dynamic-slice_fusion.2
  8.8 0.0 copy-start.3
  8.9 0.0 copy-start.8
  8.9 0.1 pad_maximum_fusion
  8.9 0.9 copy-done.3
  9.9 0.0 copy-start.12
  9.9 0.0 copy-start.11
  9.9 0.0 copy-done.8
  9.9 0.9 pad_maximum_fusion.2
  10.8 0.0 all-gather.2.cloned.1.call-update
  10.8 0.0 reduce-scatter.2.cloned.1.call-start
  10.9 3.3 %collective-permute-start.1 = (bf16[128,3584]{1,0:T(8,128)(2,1)S(1)}, bf16[128,3584]{1,0:T(8,128)(2,1)}, u32[]{:S(2)}, u32[]{:S(2)}) collective-permute-start(bf16[128,3584]{1,0:T(8,128)(2,1)S(1)} %pad_maximum_fusion), channel_id=1, source_target_pairs={{0,1},{1,0},{2,3},{3,2},{4,5},{5,4},{6,7},{7,6},{8,9},{9,8},{10,11... | collective-permute-start | bytes 2752520 | tf_op jit(solution)/shard_map/ppermute | solution.py:292
  14.2 0.0 copy-done.12
  14.2 0.1 fusion.5
  14.4 0.0 copy-done.11
  14.4 0.1 collective-permute-start
  14.5 0.1 iota_add_fusion
  14.6 0.1 add.64
  14.7 1.6 collective-permute-done
  16.3 0.1 collective-permute-done.1
  16.5 2.6 %convolution_convert_fusion = bf16[640,3584]{1,0:T(8,128)(2,1)S(1)} fusion(bf16[128,3584]{1,0:T(8,128)(2,1)} %collective-permute-done.1, bf16[128,1792]{1,0:T(8,128)(2,1)S(1)} %get-tuple-element.60, bf16[128,1792]{1,0:T(8,128)(2,1)S(1)} %get-tuple-element.67, s32[256]{0:T(256)S(1)} %bitcast.34, s32[640]{0:T(1024)S(1)} %add.64), kind=kOutput, calls=%fused_computation | convolution fusion | flops 1182367744 | bytes 6426112 | tf_op jit(solution)/shard_map/dot_general | solution.py:45
  19.0 59.4 %all_to_all.10 = bf16[16,40,3584]{2,1,0:T(8,128)(2,1)} all-to-all(bf16[16,40,3584]{2,1,0:T(8,128)(2,1)S(1)} %bitcast.30), channel_id=1, replica_groups=mesh['z'=8,'p'=16,'c'=2] {'p'}, dimensions={0} | all-to-all | bytes 9175040 | tf_op jit(solution)/shard_map/all_to_all | solution.py:299
  78.4 1.5 collective-permute-start.2
  80.0 1.9 all-gather.2.cloned.1.call-done.w_ref.w_m_ref
  81.9 2.0 slice.34
  83.9 0.8 collective-permute-start.3
  84.6 0.1 compare_convert_fusion.pick_ref
  84.8 0.1 broadcast_in_dim.5.gate_ref
  84.9 5.9 %shard_map.161.pre_ref = f32[640,768]{1,0:T(8,128)} custom-call(bf16[640,3584]{1,0:T(8,128)(2,1)} %bitcast.6.x_ref.y_ref, bf16[640,3584]{1,0:T(8,128)(2,1)} %bitcast.6.x_ref.y_ref, bf16[3584,768]{1,0:T(8,128)(2,1)} %all-gather.2.cloned.1.call-done.w_ref.w_m_ref), custom_call_target="tpu_custom_call" | custom-call | flops 1761607680 | bytes 12582912 | tf_op jit(solution)/shard_map/pallas_call | solution.py:80
  90.7 0.0 collective-permute-done.2.x_ref.y_ref
  90.7 10.3 %shard_map.162 = (bf16[640,768]{1,0:T(8,128)(2,1)}, bf16[3584,768]{1,0:T(8,128)(2,1)}) custom-call(f32[640,768]{1,0:T(8,128)} %shard_map.161.pre_ref, bf16[640,3584]{1,0:T(8,128)(2,1)} %collective-permute-done.2.x_ref.y_ref, bf16[640,3584]{1,0:T(8,128)(2,1)} %collective-permute-done.2.x_ref.y_ref, bf16[3584,768]{1,0:T(8,128)(2,1)} %all-gather.2.cloned.1.call-done.w_ref.w_m_ref), custom_call_target="tpu_custom_call" | custom-call | flops 3523215360 | bytes 12582912 | tf_op jit(solution)/shard_map/pallas_call | solution.py:132
  101.1 0.0 collective-permute-done.3.w_o_ref
  101.1 0.0 copy-start.1
  101.1 1.5 copy-done.1
  102.6 0.0 collective-permute-start.4
  102.6 5.6 %shard_map.163 = bf16[3584,768]{1,0:T(8,128)(2,1)} custom-call(bf16[640,3584]{1,0:T(8,128)(2,1)} %bitcast.6.x_ref.y_ref, bf16[640,3584]{1,0:T(8,128)(2,1)} %bitcast.6.x_ref.y_ref, bf16[640,768]{1,0:T(8,128)(2,1)} %get-tuple-element.39.deriv_ref.deriv_m_ref, bf16[3584,768]{1,0:T(8,128)(2,1)} %get-tuple-element.40._), custom_call_target="tpu_custom_call", output_to_operand_aliasing={{}: (3, {})} | custom-call | flops 1761607680 | bytes 12582912 | tf_op jit(solution)/shard_map/pallas_call | solution.py:161
  108.3 0.0 copy-start
  108.3 0.0 collective-permute-done.4.deriv_o_ref
  108.3 0.0 reduce-scatter.2.cloned.1.call-update
  108.3 1.2 copy-done
  109.5 0.0 copy-start.2
  109.5 1.8 copy-done.2
  111.3 6.7 %shard_map.164 = bf16[640,3584]{1,0:T(8,128)(2,1)S(1)} custom-call(bf16[640,768]{1,0:T(8,128)(2,1)S(1)} %copy-done, bf16[640,768]{1,0:T(8,128)(2,1)S(1)} %collective-permute-done.4.deriv_o_ref, bf16[3584,768]{1,0:T(8,128)(2,1)} %all-gather.2.cloned.1.call-done.w_ref.w_m_ref, bf16[1792,768]{1,0:T(8,128)(2,1)S(1)} %copy-done.2), custom_call_target="tpu_custom_call" | custom-call | flops 3523215360 | bytes 12582912 | tf_op jit(solution)/shard_map/pallas_call | solution.py:198
  118.0 60.7 %all_to_all.11 = bf16[16,40,3584]{2,1,0:T(8,128)(2,1)S(1)} all-to-all(bf16[16,40,3584]{2,1,0:T(8,128)(2,1)S(1)} %bitcast.28), channel_id=1, replica_groups=mesh['z'=8,'p'=16,'c'=2] {'p'}, dimensions={0} | all-to-all | bytes 9175040 | tf_op jit(solution)/shard_map/all_to_all | solution.py:319
  178.7 2.2 %shard_map.165 = (bf16[128,3584]{1,0:T(8,128)(2,1)S(1)}, bf16[128,3584]{1,0:T(8,128)(2,1)S(1)}) custom-call(bf16[256,640]{1,0:T(8,128)(2,1)S(1)} %compare_convert_fusion.pick_ref, f32[256,128]{1,0:T(8,128)S(1)} %broadcast_in_dim.5.gate_ref, bf16[640,3584]{1,0:T(8,128)(2,1)S(1)} %bitcast.29), custom_call_target="tpu_custom_call" | custom-call | flops 1174405120 | bytes 12582912 | tf_op jit(solution)/shard_map/pallas_call | solution.py:222
  180.9 0.0 copy-start.4
  181.0 1.7 collective-permute-start.5
  182.7 0.0 reduce-scatter.2.cloned.1.call-done
  182.7 0.0 copy-start.6
  182.7 1.3 convert_element_type.73
  184.0 0.1 slice_bitcast_fusion.1
  184.1 0.0 copy-done.4
  184.1 0.0 copy-done.6
  184.1 0.2 copy-done.7
  184.3 1.9 subtract_convert_fusion
  186.2 0.0 collective-permute-done.5.far_ref
  186.2 0.0 copy-done.9
  186.2 0.0 copy-done.10
  186.2 1.2 subtract_convert_fusion.1
  187.5 1.3 shard_map.166
  (9 shorter events, 0.1 us)
Async XLA Ops:
  7.2 1.5 copy-start.5
  7.2 74.7 %all-gather.2.cloned.1.call-start = ((), (), s32[]{:S(2)}) async-start(), calls=%async_computation.3 | async-start | bytes 6193152 | tf_op jit(solution)/shard_map/all_gather | solution.py:291
  8.8 1.0 copy-start.3
  8.9 1.1 copy-start.8
  9.9 4.4 %copy-start.12 = (s32[128,1]{0,1:T(1,128)S(1)}, s32[128,1]{0,1:T(1,128)}, u32[]{:S(2)}) copy-start(s32[128,1]{0,1:T(1,128)} %param.12) | copy-start | bytes 1540
  9.9 4.5 %copy-start.11 = (f32[128,1]{0,1:T(1,128)S(1)}, f32[128,1]{0,1:T(1,128)}, u32[]{:S(2)}) copy-start(f32[128,1]{0,1:T(1,128)} %param.13) | copy-start | bytes 1540
  10.8 171.8 %reduce-scatter.2.cloned.1.call-start = ((), (), s32[]{:S(2)}) async-start(), calls=%async_computation.4 | async-start | bytes 6193152 | tf_op jit(solution)/shard_map/reduce_scatter | solution.py:314
  10.9 5.6 %collective-permute-start.1 = (bf16[128,3584]{1,0:T(8,128)(2,1)S(1)}, bf16[128,3584]{1,0:T(8,128)(2,1)}, u32[]{:S(2)}, u32[]{:S(2)}) collective-permute-start(bf16[128,3584]{1,0:T(8,128)(2,1)S(1)} %pad_maximum_fusion), channel_id=1, source_target_pairs={{0,1},{1,0},{2,3},{3,2},{4,5},{5,4},{6,7},{7,6},{8,9},{9,8},{10,11... | collective-permute-start | bytes 2752520 | tf_op jit(solution)/shard_map/ppermute | solution.py:292
  14.4 1.9 collective-permute-start
  78.4 12.3 %collective-permute-start.2 = (bf16[640,3584]{1,0:T(8,128)(2,1)}, bf16[640,3584]{1,0:T(8,128)(2,1)}, u32[]{:S(2)}, u32[]{:S(2)}) collective-permute-start(bf16[640,3584]{1,0:T(8,128)(2,1)} %bitcast.6.x_ref.y_ref), channel_id=1, source_target_pairs={{0,1},{1,0},{2,3},{3,2},{4,5},{5,4},{6,7},{7,6},{8,9},{9,8},{10,11... | collective-permute-start | bytes 13762568 | tf_op jit(solution)/shard_map/ppermute | solution.py:304
  83.9 17.2 %collective-permute-start.3 = (bf16[1792,768]{1,0:T(8,128)(2,1)S(1)}, bf16[1792,768]{1,0:T(8,128)(2,1)S(1)}, u32[]{:S(2)}, u32[]{:S(2)}) collective-permute-start(bf16[1792,768]{1,0:T(8,128)(2,1)S(1)} %slice.34), channel_id=1, source_target_pairs={{0,1},{1,0},{2,3},{3,2},{4,5},{5,4},{6,7},{7,6},{8,9},{9,8},{10,11... | collective-permute-start | bytes 8257544 | tf_op jit(solution)/shard_map/ppermute | solution.py:306
  101.1 1.5 copy-start.1
  102.6 5.7 %collective-permute-start.4 = (bf16[640,768]{1,0:T(8,128)(2,1)}, bf16[640,768]{1,0:T(8,128)(2,1)S(1)}, u32[]{:S(2)}, u32[]{:S(2)}) collective-permute-start(bf16[640,768]{1,0:T(8,128)(2,1)} %get-tuple-element.39.deriv_ref.deriv_m_ref), channel_id=1, source_target_pairs={{0,1},{1,0},{2,3},{3,2},{4,5},{5,4},{6,7},{7,6},{8,9},{9,8},{10,11... | collective-permute-start | bytes 2949128 | tf_op jit(solution)/shard_map/ppermute | solution.py:311
  108.3 1.2 copy-start
  109.5 1.8 copy-start.2
  180.9 3.1 %copy-start.4 = (bf16[2,448,256]{2,1,0:T(8,128)(2,1)S(1)}, bf16[2,448,256]{2,1,0:T(8,128)(2,1)}, u32[]{:S(2)}) copy-start(bf16[2,448,256]{2,1,0:T(8,128)(2,1)} %param.14) | copy-start | bytes 1376260
  181.0 5.3 %collective-permute-start.5 = (bf16[128,3584]{1,0:T(8,128)(2,1)S(1)}, bf16[128,3584]{1,0:T(8,128)(2,1)S(1)}, u32[]{:S(2)}, u32[]{:S(2)}) collective-permute-start(bf16[128,3584]{1,0:T(8,128)(2,1)S(1)} %get-tuple-element.44), channel_id=1, source_target_pairs={{0,1},{1,0},{2,3},{3,2},{4,5},{5,4},{6,7},{7,6},{8,9},{9,8},{10,11... | collective-permute-start | bytes 2752520 | tf_op jit(solution)/shard_map/ppermute | solution.py:323
  182.7 1.4 copy-start.6
  182.7 1.7 copy-start.7
  184.3 1.9 copy-start.9
  184.3 1.9 copy-start.10
Sparse Core Ops, SparseCore 0:
  11.0 70.8 all-gather.1
  108.4 66.1 reduce-scatter.1

commit v5 on v4

--- a/solution.py
+++ b/solution.py
@@ -47,8 +47,7 @@
 
 MIB = 1 << 20
 VMEM = 56
-BACK_VMEM = 40
-GRAD_VMEM = 56
+BACK_VMEM = 50
 LANES = 128
 
 
@@ -96,7 +95,7 @@
     grad_ref[:, 2 * hid :] = dot(y, deriv_ref[:, 2 * hid :], ((0,), (0,))).astype(jnp.bfloat16)
 
 
-def mid_body(hid, blocks, pre_ref, x_ref, y_ref, w_ref, deriv_ref, grad_ref, acc_ref):
+def mid_body(hid, blocks, pre_ref, xm_ref, ym_ref, xo_ref, yo_ref, w_ref, deriv_ref, grad_ref, acc_ref):
     step = pl.program_id(0)
 
     @pl.when(step == 0)
@@ -105,8 +104,8 @@
 
     @pl.when(step < blocks)
     def _():
-        acc_ref[:, : 2 * hid] += dot(x_ref[...], w_ref[:, : 2 * hid])
-        acc_ref[:, 2 * hid :] += dot(y_ref[...], w_ref[:, 2 * hid :])
+        acc_ref[:, : 2 * hid] += dot(xo_ref[...], w_ref[:, : 2 * hid])
+        acc_ref[:, 2 * hid :] += dot(yo_ref[...], w_ref[:, 2 * hid :])
 
     @pl.when(step == blocks - 1)
     def _():
@@ -117,62 +116,50 @@
         deriv_ref[:, hid : 2 * hid] = (d_hidden * gated).astype(jnp.bfloat16)
         deriv_ref[:, 2 * hid :] = (gated * linear).astype(jnp.bfloat16)
 
-    @pl.when(step >= blocks)
-    def _():
-        write_grads(hid, x_ref[...], y_ref[...], deriv_ref, grad_ref)
-
-
-def second_half(pre, rows, weights, hid, blocks):
-    n, width = rows.shape
+    @pl.when((step >= blocks) & (step < 2 * blocks))
+    def _():
+        write_grads(hid, xo_ref[...], yo_ref[...], deriv_ref, grad_ref)
+
+    @pl.when(step >= 2 * blocks)
+    def _():
+        write_grads(hid, xm_ref[...], ym_ref[...], deriv_ref, grad_ref)
+
+
+def second_half(pre, mine, other, weights, hid, blocks):
+    n, width = mine.shape
     cols = width // 2 // blocks
 
     def at(i):
-        return jnp.minimum(i, 2 * blocks - 1 - i)
+        return jnp.clip(jnp.minimum(i, 2 * blocks - 1 - i), 0, blocks - 1)
+
+    def late(i):
+        return jnp.maximum(i - 2 * blocks, 0)
+
+    def grad_at(i):
+        return jnp.where(i < blocks, 2 * blocks - 1, jnp.where(i < 2 * blocks, blocks + at(i), late(i)))
 
     return call(
         functools.partial(mid_body, hid, blocks),
-        2 * blocks,
+        3 * blocks,
         [
             pl.BlockSpec((n, 3 * hid), lambda i: (0, 0)),
+            pl.BlockSpec((n, cols), lambda i: (0, late(i))),
+            pl.BlockSpec((n, cols), lambda i: (0, blocks + late(i))),
             pl.BlockSpec((n, cols), lambda i: (0, at(i))),
             pl.BlockSpec((n, cols), lambda i: (0, blocks + at(i))),
             pl.BlockSpec((cols, 3 * hid), lambda i: (blocks + jnp.minimum(i, blocks - 1), 0)),
         ],
         [
             pl.BlockSpec((n, 3 * hid), lambda i: (0, 0)),
-            pl.BlockSpec((cols, 3 * hid), lambda i: (blocks + jnp.minimum(blocks - 1, 2 * blocks - 1 - i), 0)),
+            pl.BlockSpec((cols, 3 * hid), lambda i: (grad_at(i), 0)),
         ],
         [
             jax.ShapeDtypeStruct((n, 3 * hid), jnp.bfloat16),
             jax.ShapeDtypeStruct((width, 3 * hid), jnp.bfloat16),
         ],
-        flops=6 * n * width * hid,
+        flops=9 * n * width * hid,
         scratch=[pltpu.VMEM((n, 3 * hid), jnp.float32)],
-    )(pre, rows, rows, weights)
-
-
-def grad_body(hid, x_ref, y_ref, deriv_ref, _, grad_ref):
-    write_grads(hid, x_ref[...], y_ref[...], deriv_ref, grad_ref)
-
-
-def first_grads(rows, deriv, grad, hid, blocks):
-    n, width = rows.shape
-    cols = width // 2 // blocks
-    return pl.pallas_call(
-        functools.partial(grad_body, hid),
-        grid=(blocks,),
-        in_specs=[
-            pl.BlockSpec((n, cols), lambda i: (0, i)),
-            pl.BlockSpec((n, cols), lambda i: (0, blocks + i)),
-            pl.BlockSpec((n, 3 * hid), lambda i: (0, 0)),
-            pl.BlockSpec(memory_space=pl.ANY),
-        ],
-        out_specs=pl.BlockSpec((cols, 3 * hid), lambda i: (i, 0)),
-        out_shape=jax.ShapeDtypeStruct((width, 3 * hid), jnp.bfloat16),
-        input_output_aliases={3: 0},
-        compiler_params=pltpu.CompilerParams(vmem_limit_bytes=GRAD_VMEM * MIB),
-        cost_estimate=pl.CostEstimate(flops=3 * n * width * hid, bytes_accessed=12 * MIB, transcendentals=0),
-    )(rows, rows, deriv, grad)
+    )(pre, mine, mine, other, other, weights)
 
 
 def back_body(hid, deriv_m_ref, deriv_o_ref, w_m_ref, w_o_ref, back_ref):
@@ -191,17 +178,21 @@
 
 
 def sent_back(deriv_m, deriv_o, w_m, w_o, hid, blocks):
-    n = deriv_m.shape[0]
-    cols = w_o.shape[0] // blocks
+    n, width = deriv_m.shape[0], w_m.shape[0]
+    cols = width // 2 // blocks
     deriv = pl.BlockSpec((n, 3 * hid), lambda i: (0, 0))
-    weight = pl.BlockSpec((cols, 3 * hid), lambda i: (lax.div(i, 2), 0))
     return call(
         functools.partial(back_body, hid),
         2 * blocks,
-        [deriv, deriv, weight, weight],
+        [
+            deriv,
+            deriv,
+            pl.BlockSpec((cols, 3 * hid), lambda i: (lax.div(i, 2), 0)),
+            pl.BlockSpec((cols, 3 * hid), lambda i: (blocks + lax.div(i, 2), 0)),
+        ],
         pl.BlockSpec((n, cols), lambda i: (0, lax.div(i, 2) + blocks * lax.rem(i, 2))),
-        jax.ShapeDtypeStruct((n, 2 * w_o.shape[0]), jnp.bfloat16),
-        flops=12 * n * w_o.shape[0] * hid,
+        jax.ShapeDtypeStruct((n, width), jnp.bfloat16),
+        flops=6 * n * width * hid,
         vmem=BACK_VMEM,
     )(deriv_m, deriv_o, w_m, w_o)
 
@@ -272,6 +263,9 @@
         for k in range(n_core)
     ]
 
+    owned = jnp.concatenate([w_gate_up[0], w_gate_up[1], w_down.T], axis=1)
+    weights = lax.all_gather(owned, ("z", "c"), axis=0, tiled=True, axis_index_groups=orders)
+
     flat = routes.reshape(-1)
     place = flat * block + c * CAPACITY + slots_of(flat)
     info = jnp.concatenate([place.astype(jnp.float32)[:, None], gates], axis=1)
@@ -286,10 +280,7 @@
     def both_of(k):
         return jnp.concatenate([half_of(tokens, k), half_of(cot, k)], axis=1)
 
-    sent, w_up, w_dn = lax.optimization_barrier((both_of(1 - c), w_gate_up, w_down))
-    owned = jnp.concatenate([w_up[0], w_up[1], w_dn.T], axis=1)
-    weights = lax.all_gather(owned, ("z", "c"), axis=0, tiled=True, axis_index_groups=orders)
-    rows2 = jnp.concatenate([both_of(c), lax.ppermute(sent, "c", SWAP)], axis=0)
+    rows2 = jnp.concatenate([both_of(c), lax.ppermute(both_of(1 - c), "c", SWAP)], axis=0)
     row_id = lax.broadcasted_iota(jnp.int32, (EXPERTS, pair, block), 0) * block + (
         lax.broadcasted_iota(jnp.int32, (EXPERTS, pair, block), 2)
     )
@@ -303,14 +294,13 @@
     gate2 = jnp.broadcast_to(gate2, (gate2.shape[0], LANES))
     other = lax.ppermute(mine, "c", SWAP)
 
-    weights_o = lax.ppermute(weights[half:], "c", SWAP)
     ready, unpick, gate2 = lax.optimization_barrier((mine, unpick, gate2))
     pre = first_half(ready, weights, hid, BLOCKS)
-    deriv, grad = second_half(pre, other, weights, hid, BLOCKS)
+    pre, sent = lax.optimization_barrier((pre, weights))
+    weights_o = lax.ppermute(sent, "c", SWAP)
+    deriv, grad = second_half(pre, mine, other, weights, hid, BLOCKS)
     deriv, weights_o = lax.optimization_barrier((deriv, weights_o))
     deriv_o = lax.ppermute(deriv, "c", SWAP)
-    grad = first_grads(mine, deriv, grad, hid, BLOCKS)
-    grad, deriv_o = lax.optimization_barrier((grad, deriv_o))
     grad = lax.psum_scatter(
         grad, ("z", "c"), scatter_dimension=0, tiled=True, axis_index_groups=orders
     ).astype(jnp.float32)

time: 196 us -> 196 us (level)
  local copies, waits for them, and re-layouts: 8.06 us -> 3.2 us
  waiting for transfers between devices: 3.71 us -> 7.41 us
    ppermute x2, starting transfers between devices: 4.09 us -> 0.77 us  [the longest x1 0.67 us: shards(): weights_o = lax.ppermute(sent, 'c', SWAP)]
    ppermute x1, starting transfers between devices: 0.11 us -> 3.24 us  [shards(): info2 = jnp.concatenate([info, lax.ppermute(info, 'c', SWAP)], axis=0)]
    unnamed x26 -> x20, local copies, waits for them, and re-layouts: 5.71 us -> 2.8 us
    ppermute x1, waiting for transfers between devices: 0.01 us -> 2.55 us  [shards(): deriv_o = lax.ppermute(deriv, 'c', SWAP)]
    all_gather x1, waiting for transfers between devices: 1.93 us -> 4.43 us  [shards(): lax.all_gather(owned, ('z', 'c'), axis=0, tiled=True, axis_index_groups=o...]
    pallas_call x3 -> x2, Pallas kernels: 22.7 us -> 22.8 us  [the longest x1 14.5 us: second_half(): call(functools.partial(mid_body, hid, blocks), 3 * blocks, [pl.BlockSpec(...]
where the time goes in v5:
time: 196 us
  blocking collectives  121 us (62%)
  Pallas kernels  32.2 us (16%)
  between operations  14.3 us (7%)
  other arithmetic  8.27 us (4%)
  waiting for transfers between devices  7.41 us (4%)
  starting transfers between devices  7.32 us (4%)
  local copies, waits for them, and re-layouts  3.2 us (2%)
  matrix products  2.28 us (1%)
    all_to_all x1, blocking collectives, shards(): lax.all_to_all(back.reshape(n_chip, block, width), 'p', split_axis=0, con...  61.3 us
    all_to_all x1, blocking collectives, shards(): got = lax.all_to_all(packed, 'p', split_axis=0, concat_axis=0, tiled=True)  59.7 us
    pallas_call x1, Pallas kernels, second_half(): call(functools.partial(mid_body, hid, blocks), 3 * blocks, [pl.BlockSpec(...  14.5 us
    pallas_call x1, Pallas kernels, sent_back(): call(functools.partial(back_body, hid), 2 * blocks, [deriv, deriv, pl.Blo...  8.31 us
    pallas_call x1, Pallas kernels, first_half(): call(functools.partial(pre_body, hid), blocks, [pl.BlockSpec((n, cols), l...  5.83 us
    all_gather x1, waiting for transfers between devices, shards(): lax.all_gather(owned, ('z', 'c'), axis=0, tiled=True, axis_index_groups=o...  4.43 us
  transfers between devices with their start and end apart: 8, of which 3 were waited for; matrix products, arithmetic and copies ran while one was open for 4% of the time, Pallas kernels for 16%

profile of v5, /device:TPU:1, one launch (start us, length us, event | category | flops | bytes accessed | tf_op | source)
XLA Modules:
  0.0 196.0 jit_solution(4086176437994698829)
XLA Ops:
  7.2 0.0 copy-start.3
  7.2 0.0 all-gather.2.cloned.1.call-start
  7.2 0.9 fusion.5
  8.1 0.7 fusion.11
  8.8 0.7 pad_maximum_fusion.4
  9.5 3.2 %collective-permute-start = (f32[128,2]{0,1:T(2,128)S(1)}, f32[128,2]{0,1:T(2,128)S(1)}, u32[]{:S(2)}, u32[]{:S(2)}) collective-permute-start(f32[128,2]{0,1:T(2,128)S(1)} %pad_maximum_fusion.4), channel_id=1, source_target_pairs={{0,1},{1,0},{2,3},{3,2},{4,5},{5,4},{6,7},{7,6},{8,9},{9,8},{10,11... | collective-permute-start | bytes 3080 | tf_op jit(solution)/shard_map/ppermute | solution.py:272
  12.7 1.4 multiply_convert_fusion
  14.1 0.0 copy-done.3
  14.1 0.1 constant_dynamic-slice_fusion.2
  14.2 0.0 copy-start.1
  14.3 0.0 copy-start.6
  14.3 0.1 pad_maximum_fusion
  14.3 0.0 copy-start.9
  14.4 0.1 collective-permute-start.1
  14.5 0.8 copy-done.1
  15.3 0.0 copy-done.6
  15.3 0.9 pad_maximum_fusion.2
  16.2 0.0 all-gather.2.cloned.1.call-update
  16.2 0.0 reduce-scatter.2.cloned.1.call-start
  16.3 0.1 iota_add_fusion
  16.4 0.1 add.64
  16.5 0.0 collective-permute-done
  16.5 0.0 copy-done.9
  16.5 0.4 collective-permute-done.1
  16.9 1.4 convolution_convert_fusion
  18.3 59.7 %all_to_all.10 = bf16[16,40,3584]{2,1,0:T(8,128)(2,1)} all-to-all(bf16[16,40,3584]{2,1,0:T(8,128)(2,1)S(1)} %bitcast.30), channel_id=1, replica_groups=mesh['z'=8,'p'=16,'c'=2] {'p'}, dimensions={0} | all-to-all | bytes 9175040 | tf_op jit(solution)/shard_map/all_to_all | solution.py:290
  78.0 1.6 collective-permute-start.2
  79.6 0.1 compare_convert_fusion.pick_ref
  79.7 0.1 broadcast_in_dim.5.gate_ref
  79.8 4.4 %all-gather.2.cloned.1.call-done.w_ref.w_m_ref = bf16[3584,768]{1,0:T(8,128)(2,1)} async-done(((bf16[448,768]{1,0:T(8,128)(2,1)}), bf16[3584,768]{1,0:T(8,128)(2,1)}) %all-gather.2.cloned.1.call-update) | async-done | bytes 5505040 | tf_op jit(solution)/shard_map/all_gather | solution.py:267
  84.2 5.8 %shard_map.161.pre_ref = f32[640,768]{1,0:T(8,128)} custom-call(bf16[640,3584]{1,0:T(8,128)(2,1)} %bitcast.6.x_ref.y_ref.xm_ref.ym_ref, bf16[640,3584]{1,0:T(8,128)(2,1)} %bitcast.6.x_ref.y_ref.xm_ref.ym_ref, bf16[3584,768]{1,0:T(8,128)(2,1)} %all-gather.2.cloned.1.call-done.w_ref.w_m_ref), custom_call_target="tpu_custom_call" | custom-call | flops 1761607680 | bytes 12582912 | tf_op jit(solution)/shard_map/pallas_call | solution.py:79
  90.1 0.7 collective-permute-start.3
  90.7 0.0 collective-permute-done.2.xo_ref.yo_ref
  90.7 14.5 %shard_map.162 = (bf16[640,768]{1,0:T(8,128)(2,1)}, bf16[3584,768]{1,0:T(8,128)(2,1)}) custom-call(f32[640,768]{1,0:T(8,128)} %shard_map.161.pre_ref, bf16[640,3584]{1,0:T(8,128)(2,1)} %bitcast.6.x_ref.y_ref.xm_ref.ym_ref, bf16[640,3584]{1,0:T(8,128)(2,1)} %bitcast.6.x_ref.y_ref.xm_ref.ym_ref, bf16[640,3584]{1,0:T(8,128)(2,1)} %collective-permute-done.2.xo_ref.yo_ref, ...), custom_call_target="tpu_custom_call" | custom-call | flops 5284823040 | bytes 12582912 | tf_op jit(solution)/shard_map/pallas_call | solution.py:141
  105.2 0.0 copy-start
  105.2 0.0 reduce-scatter.2.cloned.1.call-update
  105.3 0.0 collective-permute-done.3.w_o_ref
  105.3 1.2 copy-done
  106.4 0.0 collective-permute-start.4
  106.5 2.5 %collective-permute-done.4.deriv_o_ref = bf16[640,768]{1,0:T(8,128)(2,1)S(1)} collective-permute-done((bf16[640,768]{1,0:T(8,128)(2,1)S(1)}, bf16[640,768]{1,0:T(8,128)(2,1)S(1)}, u32[]{:S(2)}, u32[]{:S(2)}) %collective-permute-start.4) | collective-permute-done | bytes 983072 | tf_op jit(solution)/shard_map/ppermute | solution.py:303
  109.0 8.3 %shard_map.163 = bf16[640,3584]{1,0:T(8,128)(2,1)} custom-call(bf16[640,768]{1,0:T(8,128)(2,1)S(1)} %copy-done, bf16[640,768]{1,0:T(8,128)(2,1)S(1)} %collective-permute-done.4.deriv_o_ref, bf16[3584,768]{1,0:T(8,128)(2,1)} %all-gather.2.cloned.1.call-done.w_ref.w_m_ref, bf16[3584,768]{1,0:T(8,128)(2,1)} %collective-permute-done.3.w_o_ref), custom_call_target="tpu_custom_call" | custom-call | flops 3523215360 | bytes 12582912 | tf_op jit(solution)/shard_map/pallas_call | solution.py:184
  117.3 61.3 %all_to_all.11 = bf16[16,40,3584]{2,1,0:T(8,128)(2,1)S(1)} all-to-all(bf16[16,40,3584]{2,1,0:T(8,128)(2,1)} %bitcast.29), channel_id=1, replica_groups=mesh['z'=8,'p'=16,'c'=2] {'p'}, dimensions={0} | all-to-all | bytes 9175040 | tf_op jit(solution)/shard_map/all_to_all | solution.py:309
  178.6 2.2 %shard_map.164 = (bf16[128,3584]{1,0:T(8,128)(2,1)S(1)}, bf16[128,3584]{1,0:T(8,128)(2,1)S(1)}) custom-call(bf16[256,640]{1,0:T(8,128)(2,1)S(1)} %compare_convert_fusion.pick_ref, f32[256,128]{1,0:T(8,128)S(1)} %broadcast_in_dim.5.gate_ref, bf16[640,3584]{1,0:T(8,128)(2,1)S(1)} %bitcast.28), custom_call_target="tpu_custom_call" | custom-call | flops 1174405120 | bytes 12582912 | tf_op jit(solution)/shard_map/pallas_call | solution.py:213
  180.8 0.0 copy-start.7
  180.9 1.7 collective-permute-start.5
  182.5 0.0 reduce-scatter.2.cloned.1.call-done
  182.5 0.0 copy-start.8
  182.5 1.2 convert_element_type.73
  183.8 0.1 slice_bitcast_fusion.1
  183.8 0.0 copy-done.7
  183.8 0.0 copy-done.8
  183.9 0.0 copy-start.2
  183.9 0.0 copy-start.4
  183.9 0.0 copy-start.5
  183.9 1.2 subtract_convert_fusion.1
  185.1 0.0 copy-done.2
  185.1 0.5 copy-done.4
  185.6 0.3 copy-done.5
  185.9 1.9 subtract_convert_fusion
  187.8 0.0 collective-permute-done.5.far_ref
  187.8 1.3 shard_map.165
  (4 shorter events, 0.0 us)
Async XLA Ops:
  7.2 6.9 %copy-start.3 = (bf16[128,3584]{1,0:T(8,128)(2,1)S(1)}, bf16[128,3584]{1,0:T(8,128)(2,1)}, u32[]{:S(2)}) copy-start(bf16[128,3584]{1,0:T(8,128)(2,1)} %param.10) | copy-start | bytes 2752516
  7.2 77.0 %all-gather.2.cloned.1.call-start = ((), (), s32[]{:S(2)}) async-start(), calls=%async_computation.3 | async-start | bytes 6193152 | tf_op jit(solution)/shard_map/all_gather | solution.py:267
  9.5 7.0 %collective-permute-start = (f32[128,2]{0,1:T(2,128)S(1)}, f32[128,2]{0,1:T(2,128)S(1)}, u32[]{:S(2)}, u32[]{:S(2)}) collective-permute-start(f32[128,2]{0,1:T(2,128)S(1)} %pad_maximum_fusion.4), channel_id=1, source_target_pairs={{0,1},{1,0},{2,3},{3,2},{4,5},{5,4},{6,7},{7,6},{8,9},{9,8},{10,11... | collective-permute-start | bytes 3080 | tf_op jit(solution)/shard_map/ppermute | solution.py:272
  14.2 1.0 copy-start.1
  14.3 1.1 copy-start.6
  14.3 2.1 %copy-start.9 = (f32[128,1]{0,1:T(1,128)S(1)}, f32[128,1]{0,1:T(1,128)}, u32[]{:S(2)}) copy-start(f32[128,1]{0,1:T(1,128)} %param.13) | copy-start | bytes 1540
  14.4 2.6 %collective-permute-start.1 = (bf16[128,3584]{1,0:T(8,128)(2,1)S(1)}, bf16[128,3584]{1,0:T(8,128)(2,1)S(1)}, u32[]{:S(2)}, u32[]{:S(2)}) collective-permute-start(bf16[128,3584]{1,0:T(8,128)(2,1)S(1)} %pad_maximum_fusion), channel_id=1, source_target_pairs={{0,1},{1,0},{2,3},{3,2},{4,5},{5,4},{6,7},{7,6},{8,9},{9,8},{10,11... | collective-permute-start | bytes 2752520 | tf_op jit(solution)/shard_map/ppermute | solution.py:283
  16.2 166.3 %reduce-scatter.2.cloned.1.call-start = ((), (), s32[]{:S(2)}) async-start(), calls=%async_computation.4 | async-start | bytes 6193152 | tf_op jit(solution)/shard_map/reduce_scatter | solution.py:304
  78.0 12.7 %collective-permute-start.2 = (bf16[640,3584]{1,0:T(8,128)(2,1)}, bf16[640,3584]{1,0:T(8,128)(2,1)}, u32[]{:S(2)}, u32[]{:S(2)}) collective-permute-start(bf16[640,3584]{1,0:T(8,128)(2,1)} %bitcast.6.x_ref.y_ref.xm_ref.ym_ref), channel_id=1, source_target_pairs={{0,1},{1,0},{2,3},{3,2},{4,5},{5,4},{6,7},{7,6},{8,9},{9,8},{10,11... | collective-permute-start | bytes 13762568 | tf_op jit(solution)/shard_map/ppermute | solution.py:295
  90.1 15.2 %collective-permute-start.3 = (bf16[3584,768]{1,0:T(8,128)(2,1)}, bf16[3584,768]{1,0:T(8,128)(2,1)}, u32[]{:S(2)}, u32[]{:S(2)}) collective-permute-start(bf16[3584,768]{1,0:T(8,128)(2,1)} %all-gather.2.cloned.1.call-done.w_ref.w_m_ref), channel_id=1, source_target_pairs={{0,1},{1,0},{2,3},{3,2},{4,5},{5,4},{6,7},{7,6},{8,9},{9,8},{10,11... | collective-permute-start | bytes 16515080 | tf_op jit(solution)/shard_map/ppermute | solution.py:300
  105.2 1.2 copy-start
  106.4 2.6 %collective-permute-start.4 = (bf16[640,768]{1,0:T(8,128)(2,1)S(1)}, bf16[640,768]{1,0:T(8,128)(2,1)S(1)}, u32[]{:S(2)}, u32[]{:S(2)}) collective-permute-start(bf16[640,768]{1,0:T(8,128)(2,1)S(1)} %copy-done), channel_id=1, source_target_pairs={{0,1},{1,0},{2,3},{3,2},{4,5},{5,4},{6,7},{7,6},{8,9},{9,8},{10,11... | collective-permute-start | bytes 2949128 | tf_op jit(solution)/shard_map/ppermute | solution.py:303
  180.8 3.0 %copy-start.7 = (f32[256,448]{0,1:T(8,128)S(1)}, f32[256,448]{0,1:T(8,128)}, u32[]{:S(2)}) copy-start(f32[256,448]{0,1:T(8,128)} %param.18) | copy-start | bytes 1376260
  180.9 6.9 %collective-permute-start.5 = (bf16[128,3584]{1,0:T(8,128)(2,1)S(1)}, bf16[128,3584]{1,0:T(8,128)(2,1)S(1)}, u32[]{:S(2)}, u32[]{:S(2)}) collective-permute-start(bf16[128,3584]{1,0:T(8,128)(2,1)S(1)} %get-tuple-element.38), channel_id=1, source_target_pairs={{0,1},{1,0},{2,3},{3,2},{4,5},{5,4},{6,7},{7,6},{8,9},{9,8},{10,11... | collective-permute-start | bytes 2752520 | tf_op jit(solution)/shard_map/ppermute | solution.py:313
  182.5 1.3 copy-start.8
  183.9 1.3 copy-start.2
  183.9 1.7 copy-start.4
  183.9 2.0 %copy-start.5 = (f32[2,448,256]{2,1,0:T(8,128)S(1)}, f32[2,448,256]{2,1,0:T(8,128)}, u32[]{:S(2)}) copy-start(f32[2,448,256]{2,1,0:T(8,128)} %param.16) | copy-start | bytes 2752516
Sparse Core Ops, SparseCore 0:
  16.4 67.8 all-gather.1
  105.4 65.8 reduce-scatter.1

commit v6 on v4

--- a/solution.py
+++ b/solution.py
@@ -46,13 +46,13 @@
 
 
 MIB = 1 << 20
+FIRST_VMEM = 56
 VMEM = 56
-BACK_VMEM = 40
-GRAD_VMEM = 56
+BACK_VMEM = 50
 LANES = 128
 
 
-def call(body, grid, in_specs, out_specs, out_shape, flops, scratch=(), vmem=VMEM):
+def call(body, grid, in_specs, out_specs, out_shape, flops, scratch=(), vmem=VMEM, size=12 * MIB):
     return pl.pallas_call(
         body,
         grid=(grid,),
@@ -61,8 +61,31 @@
         out_shape=out_shape,
         scratch_shapes=list(scratch),
         compiler_params=pltpu.CompilerParams(vmem_limit_bytes=vmem * MIB),
-        cost_estimate=pl.CostEstimate(flops=flops, bytes_accessed=12 * MIB, transcendentals=0),
+        cost_estimate=pl.CostEstimate(flops=flops, bytes_accessed=size, transcendentals=0),
     )
+
+
+def lay_body(up_ref, down_ref, out_ref):
+    hid = down_ref.shape[1]
+    out_ref[:, :hid] = up_ref[0]
+    out_ref[:, hid : 2 * hid] = up_ref[1]
+    out_ref[:, 2 * hid :] = down_ref[...]
+
+
+def laid(up, down):
+    rows, hid = down.shape
+    return call(
+        lay_body,
+        1,
+        [
+            pl.BlockSpec((2, rows, hid), lambda i: (0, 0, 0)),
+            pl.BlockSpec((rows, hid), lambda i: (0, 0)),
+        ],
+        pl.BlockSpec((rows, 3 * hid), lambda i: (0, 0)),
+        jax.ShapeDtypeStruct((rows, 3 * hid), up.dtype),
+        flops=up.size,
+        vmem=8,
+    )(up, down)
 
 
 def pre_body(hid, x_ref, y_ref, w_ref, acc_ref):
@@ -87,7 +110,9 @@
         ],
         pl.BlockSpec((n, 3 * hid), lambda i: (0, 0)),
         jax.ShapeDtypeStruct((n, 3 * hid), jnp.float32),
-        flops=3 * n * width * hid,
+        flops=n * hid,
+        vmem=FIRST_VMEM,
+        size=MIB >> 4,
     )(rows, rows, weights)
 
 
@@ -170,7 +195,7 @@
         out_specs=pl.BlockSpec((cols, 3 * hid), lambda i: (i, 0)),
         out_shape=jax.ShapeDtypeStruct((width, 3 * hid), jnp.bfloat16),
         input_output_aliases={3: 0},
-        compiler_params=pltpu.CompilerParams(vmem_limit_bytes=GRAD_VMEM * MIB),
+        compiler_params=pltpu.CompilerParams(vmem_limit_bytes=VMEM * MIB),
         cost_estimate=pl.CostEstimate(flops=3 * n * width * hid, bytes_accessed=12 * MIB, transcendentals=0),
     )(rows, rows, deriv, grad)
 
@@ -191,17 +216,21 @@
 
 
 def sent_back(deriv_m, deriv_o, w_m, w_o, hid, blocks):
-    n = deriv_m.shape[0]
-    cols = w_o.shape[0] // blocks
+    n, width = deriv_m.shape[0], w_m.shape[0]
+    cols = width // 2 // blocks
     deriv = pl.BlockSpec((n, 3 * hid), lambda i: (0, 0))
-    weight = pl.BlockSpec((cols, 3 * hid), lambda i: (lax.div(i, 2), 0))
     return call(
         functools.partial(back_body, hid),
         2 * blocks,
-        [deriv, deriv, weight, weight],
+        [
+            deriv,
+            deriv,
+            pl.BlockSpec((cols, 3 * hid), lambda i: (lax.div(i, 2), 0)),
+            pl.BlockSpec((cols, 3 * hid), lambda i: (blocks + lax.div(i, 2), 0)),
+        ],
         pl.BlockSpec((n, cols), lambda i: (0, lax.div(i, 2) + blocks * lax.rem(i, 2))),
-        jax.ShapeDtypeStruct((n, 2 * w_o.shape[0]), jnp.bfloat16),
-        flops=12 * n * w_o.shape[0] * hid,
+        jax.ShapeDtypeStruct((n, width), jnp.bfloat16),
+        flops=6 * n * width * hid,
         vmem=BACK_VMEM,
     )(deriv_m, deriv_o, w_m, w_o)
 
@@ -272,24 +301,25 @@
         for k in range(n_core)
     ]
 
+    owned = laid(w_gate_up, w_down.T)
+    weights = lax.all_gather(owned, ("z", "c"), axis=0, tiled=True, axis_index_groups=orders)
+
+    cot = (gates * cotangent.astype(jnp.float32)).astype(jnp.bfloat16)
+
+    def half_of(array, k):
+        return lax.dynamic_slice_in_dim(array, k * half, half, axis=1)
+
+    def both_of(k):
+        return jnp.concatenate([half_of(tokens, k), half_of(cot, k)], axis=1)
+
+    sent, routes, gates = lax.optimization_barrier((both_of(1 - c), routes, gates))
+    rows2 = jnp.concatenate([both_of(c), lax.ppermute(sent, "c", SWAP)], axis=0)
     flat = routes.reshape(-1)
     place = flat * block + c * CAPACITY + slots_of(flat)
     info = jnp.concatenate([place.astype(jnp.float32)[:, None], gates], axis=1)
     info2 = jnp.concatenate([info, lax.ppermute(info, "c", SWAP)], axis=0)
     place2 = info2[:, 0].astype(jnp.int32)
     gate2 = info2[:, 1:2]
-    cot = (gates * cotangent.astype(jnp.float32)).astype(jnp.bfloat16)
-
-    def half_of(array, k):
-        return lax.dynamic_slice_in_dim(array, k * half, half, axis=1)
-
-    def both_of(k):
-        return jnp.concatenate([half_of(tokens, k), half_of(cot, k)], axis=1)
-
-    sent, w_up, w_dn = lax.optimization_barrier((both_of(1 - c), w_gate_up, w_down))
-    owned = jnp.concatenate([w_up[0], w_up[1], w_dn.T], axis=1)
-    weights = lax.all_gather(owned, ("z", "c"), axis=0, tiled=True, axis_index_groups=orders)
-    rows2 = jnp.concatenate([both_of(c), lax.ppermute(sent, "c", SWAP)], axis=0)
     row_id = lax.broadcasted_iota(jnp.int32, (EXPERTS, pair, block), 0) * block + (
         lax.broadcasted_iota(jnp.int32, (EXPERTS, pair, block), 2)
     )
@@ -303,9 +333,10 @@
     gate2 = jnp.broadcast_to(gate2, (gate2.shape[0], LANES))
     other = lax.ppermute(mine, "c", SWAP)
 
-    weights_o = lax.ppermute(weights[half:], "c", SWAP)
     ready, unpick, gate2 = lax.optimization_barrier((mine, unpick, gate2))
     pre = first_half(ready, weights, hid, BLOCKS)
+    pre, other, sent = lax.optimization_barrier((pre, other, weights))
+    weights_o = lax.ppermute(sent, "c", SWAP)
     deriv, grad = second_half(pre, other, weights, hid, BLOCKS)
     deriv, weights_o = lax.optimization_barrier((deriv, weights_o))
     deriv_o = lax.ppermute(deriv, "c", SWAP)

time: 196 us -> 194 us (0.990)
  local copies, waits for them, and re-layouts: 8.06 us -> 3.54 us
  Pallas kernels: 32.1 us -> 36 us
    unnamed x26 -> x22, local copies, waits for them, and re-layouts: 5.71 us -> 3.16 us
    pallas_call x1 -> x2, Pallas kernels: 6.7 us -> 9.21 us  [the longest x1 8.31 us: sent_back(): call(functools.partial(back_body, hid), 2 * blocks, [deriv, deriv, pl.Blo...]
  transfers between devices with their start and end apart: 8 -> 8, of which waited for: 3 -> 2; matrix products, arithmetic and copies ran while one was open for 4% -> 4% of each run, Pallas kernels for 16% -> 17%
where the time goes in v6:
time: 194 us
  blocking collectives  120 us (62%)
  Pallas kernels  36 us (19%)
  between operations  14.2 us (7%)
  other arithmetic  7.59 us (4%)
  starting transfers between devices  7.45 us (4%)
  local copies, waits for them, and re-layouts  3.54 us (2%)
  waiting for transfers between devices  3.14 us (2%)
    all_to_all x1, blocking collectives, shards(): lax.all_to_all(back.reshape(n_chip, block, width), 'p', split_axis=0, con...  61 us
    all_to_all x1, blocking collectives, shards(): got = lax.all_to_all(packed, 'p', split_axis=0, concat_axis=0, tiled=True)  59.4 us
    pallas_call x1, Pallas kernels, second_half(): call(functools.partial(mid_body, hid, blocks), 2 * blocks, [pl.BlockSpec(...  10.3 us
    pallas_call x1, Pallas kernels, sent_back(): call(functools.partial(back_body, hid), 2 * blocks, [deriv, deriv, pl.Blo...  8.31 us
    pallas_call x1, Pallas kernels, first_half(): call(functools.partial(pre_body, hid), blocks, [pl.BlockSpec((n, cols), l...  6.59 us
    pallas_call x1, Pallas kernels, first_grads(): pl.pallas_call(functools.partial(grad_body, hid), grid=(blocks,), in_spec...  5.63 us
    convert_element_type x2, other arithmetic, adam_update(): (weight.astype(jnp.float32) - learn_rate * update).astype(jnp.bfloat16)  4.7 us
  transfers between devices with their start and end apart: 8, of which 2 were waited for; matrix products, arithmetic and copies ran while one was open for 4% of the time, Pallas kernels for 17%

profile of v6, /device:TPU:1, one launch (start us, length us, event | category | flops | bytes accessed | tf_op | source)
XLA Modules:
  0.0 193.9 jit_solution(12898995204293606987)
XLA Ops:
  7.2 0.0 all-gather.2.cloned.1.call-start
  7.2 0.0 copy-start.1
  7.2 1.0 copy-done.1
  8.2 0.0 copy-start.3
  8.2 0.9 copy-done.3
  9.2 0.0 copy-start.6
  9.2 0.9 shard_map.161
  10.1 0.0 all-gather.2.cloned.1.call-update
  10.1 0.0 reduce-scatter.2.cloned.1.call-start
  10.1 0.0 copy-start.10
  10.2 0.0 copy-start.9
  10.2 1.4 multiply_convert_fusion
  11.6 0.0 copy-done.6
  11.6 0.1 constant_dynamic-slice_fusion
  11.7 0.1 pad_maximum_fusion
  11.8 3.3 %collective-permute-start.1 = (bf16[128,3584]{1,0:T(8,128)(2,1)S(1)}, bf16[128,3584]{1,0:T(8,128)(2,1)S(1)}, u32[]{:S(2)}, u32[]{:S(2)}) collective-permute-start(bf16[128,3584]{1,0:T(8,128)(2,1)S(1)} %pad_maximum_fusion), channel_id=1, source_target_pairs={{0,1},{1,0},{2,3},{3,2},{4,5},{5,4},{6,7},{7,6},{8,9},{9,8},{10,11... | collective-permute-start | bytes 2752520 | tf_op jit(solution)/shard_map/ppermute | solution.py:316
  15.1 0.0 copy-done.10
  15.1 0.1 fusion.5
  15.3 0.0 copy-done.9
  15.3 0.1 collective-permute-start
  15.4 0.1 iota_add_fusion
  15.5 0.1 add.64
  15.6 1.6 collective-permute-done
  17.2 0.0 collective-permute-done.1
  17.3 1.4 convolution_convert_fusion
  18.6 59.4 %all_to_all.10 = bf16[16,40,3584]{2,1,0:T(8,128)(2,1)} all-to-all(bf16[16,40,3584]{2,1,0:T(8,128)(2,1)S(1)} %bitcast.27), channel_id=1, replica_groups=mesh['z'=8,'p'=16,'c'=2] {'p'}, dimensions={0} | all-to-all | bytes 9175040 | tf_op jit(solution)/shard_map/all_to_all | solution.py:329
  78.1 1.5 collective-permute-start.2
  79.6 0.1 compare_convert_fusion.pick_ref
  79.7 0.1 broadcast_in_dim.5.gate_ref
  79.8 1.5 all-gather.2.cloned.1.call-done.w_ref.w_m_ref
  81.3 0.0 copy-start.5
  81.3 6.6 %shard_map.162.pre_ref = f32[640,768]{1,0:T(8,128)} custom-call(bf16[640,3584]{1,0:T(8,128)(2,1)} %bitcast.6.x_ref.y_ref, bf16[640,3584]{1,0:T(8,128)(2,1)} %bitcast.6.x_ref.y_ref, bf16[3584,768]{1,0:T(8,128)(2,1)} %all-gather.2.cloned.1.call-done.w_ref.w_m_ref), custom_call_target="tpu_custom_call" | custom-call | flops 163840 | bytes 65536 | tf_op jit(solution)/shard_map/pallas_call | solution.py:103
  87.9 0.0 collective-permute-done.2.x_ref.y_ref
  87.9 0.0 copy-done.5
  87.9 0.8 collective-permute-start.3
  88.7 10.3 %shard_map.163 = (bf16[640,768]{1,0:T(8,128)(2,1)}, bf16[3584,768]{1,0:T(8,128)(2,1)}) custom-call(f32[640,768]{1,0:T(8,128)} %shard_map.162.pre_ref, bf16[640,3584]{1,0:T(8,128)(2,1)} %collective-permute-done.2.x_ref.y_ref, bf16[640,3584]{1,0:T(8,128)(2,1)} %collective-permute-done.2.x_ref.y_ref, bf16[3584,768]{1,0:T(8,128)(2,1)} %all-gather.2.cloned.1.call-done.w_ref.w_m_ref), custom_call_target="tpu_custom_call" | custom-call | flops 3523215360 | bytes 12582912 | tf_op jit(solution)/shard_map/pallas_call | solution.py:157
  99.0 0.0 collective-permute-done.3.w_o_ref
  99.0 0.1 collective-permute-start.4
  99.0 5.6 %shard_map.164 = bf16[3584,768]{1,0:T(8,128)(2,1)} custom-call(bf16[640,3584]{1,0:T(8,128)(2,1)} %bitcast.6.x_ref.y_ref, bf16[640,3584]{1,0:T(8,128)(2,1)} %bitcast.6.x_ref.y_ref, bf16[640,768]{1,0:T(8,128)(2,1)} %get-tuple-element.45.deriv_ref.deriv_m_ref, bf16[3584,768]{1,0:T(8,128)(2,1)} %get-tuple-element.46._), custom_call_target="tpu_custom_call", output_to_operand_aliasing={{}: (3, {})} | custom-call | flops 1761607680 | bytes 12582912 | tf_op jit(solution)/shard_map/pallas_call | solution.py:186
  104.7 0.0 copy-start
  104.7 0.0 collective-permute-done.4.deriv_o_ref
  104.7 0.0 reduce-scatter.2.cloned.1.call-update
  104.7 1.2 copy-done
  105.9 8.3 %shard_map.165 = bf16[640,3584]{1,0:T(8,128)(2,1)} custom-call(bf16[640,768]{1,0:T(8,128)(2,1)S(1)} %copy-done, bf16[640,768]{1,0:T(8,128)(2,1)S(1)} %collective-permute-done.4.deriv_o_ref, bf16[3584,768]{1,0:T(8,128)(2,1)} %all-gather.2.cloned.1.call-done.w_ref.w_m_ref, bf16[3584,768]{1,0:T(8,128)(2,1)} %collective-permute-done.3.w_o_ref), custom_call_target="tpu_custom_call" | custom-call | flops 3523215360 | bytes 12582912 | tf_op jit(solution)/shard_map/pallas_call | solution.py:222
  114.2 61.0 %all_to_all.11 = bf16[16,40,3584]{2,1,0:T(8,128)(2,1)S(1)} all-to-all(bf16[16,40,3584]{2,1,0:T(8,128)(2,1)} %bitcast.26), channel_id=1, replica_groups=mesh['z'=8,'p'=16,'c'=2] {'p'}, dimensions={0} | all-to-all | bytes 9175040 | tf_op jit(solution)/shard_map/all_to_all | solution.py:350
  175.1 0.0 copy-start.2
  175.1 2.9 %shard_map.166 = (bf16[128,3584]{1,0:T(8,128)(2,1)S(1)}, bf16[128,3584]{1,0:T(8,128)(2,1)}) custom-call(bf16[256,640]{1,0:T(8,128)(2,1)S(1)} %compare_convert_fusion.pick_ref, f32[256,128]{1,0:T(8,128)S(1)} %broadcast_in_dim.5.gate_ref, bf16[640,3584]{1,0:T(8,128)(2,1)S(1)} %bitcast.24), custom_call_target="tpu_custom_call" | custom-call | flops 1174405120 | bytes 12582912 | tf_op jit(solution)/shard_map/pallas_call | solution.py:251
  178.1 1.6 collective-permute-start.5
  179.6 0.0 reduce-scatter.2.cloned.1.call-done
  179.6 1.2 convert_element_type.73
  180.8 0.0 copy-start.4
  180.9 0.0 copy-start.7
  180.9 0.0 copy-start.8
  180.9 0.1 slice_bitcast_fusion.1
  180.9 0.0 copy-done.2
  181.0 3.5 %subtract_convert_fusion = (bf16[2,448,256]{2,1,0:T(8,128)(2,1)}, f32[2,448,256]{2,1,0:T(8,128)}, f32[2,448,256]{2,1,0:T(8,128)}) fusion(bf16[2,448,256]{2,1,0:T(8,128)(2,1)S(1)} %copy-done.2, f32[1,448,256]{2,1,0:T(8,128)S(1)} %get-tuple-element.63, f32[1,448,256]{2,1,0:T(8,128)S(1)} %get-tuple-element.62, f32[2,448,256]{2,1,0:T(8,128)} %param.17, ...), kind=kLoop, calls=%fused_computation.11 | loop fusion | flops 3899392 | bytes 5505024 | tf_op jit(solution)/shard_map/convert_element_type | solution.py:40
  184.4 0.0 collective-permute-done.5.far_ref
  184.4 0.0 copy-done.4
  184.4 0.0 copy-done.7
  184.4 0.0 copy-done.8
  184.4 1.2 subtract_convert_fusion.1
  185.7 1.3 shard_map.167
  (5 shorter events, 0.0 us)
Async XLA Ops:
  7.2 74.1 %all-gather.2.cloned.1.call-start = ((), (), s32[]{:S(2)}) async-start(), calls=%async_computation.3 | async-start | bytes 6193152 | tf_op jit(solution)/shard_map/all_gather | solution.py:305
  7.2 1.0 copy-start.1
  8.2 0.9 copy-start.3
  9.2 2.4 %copy-start.6 = (bf16[128,3584]{1,0:T(8,128)(2,1)S(1)}, bf16[128,3584]{1,0:T(8,128)(2,1)}, u32[]{:S(2)}) copy-start(bf16[128,3584]{1,0:T(8,128)(2,1)} %param.10) | copy-start | bytes 2752516
  10.1 169.6 %reduce-scatter.2.cloned.1.call-start = ((), (), s32[]{:S(2)}) async-start(), calls=%async_computation.4 | async-start | bytes 6193152 | tf_op jit(solution)/shard_map/reduce_scatter | solution.py:345
  10.1 5.0 %copy-start.10 = (s32[128,1]{0,1:T(1,128)S(1)}, s32[128,1]{0,1:T(1,128)}, u32[]{:S(2)}) copy-start(s32[128,1]{0,1:T(1,128)} %param.12) | copy-start | bytes 1540
  10.2 5.1 %copy-start.9 = (f32[128,1]{0,1:T(1,128)S(1)}, f32[128,1]{0,1:T(1,128)}, u32[]{:S(2)}) copy-start(f32[128,1]{0,1:T(1,128)} %param.13) | copy-start | bytes 1540
  11.8 5.4 %collective-permute-start.1 = (bf16[128,3584]{1,0:T(8,128)(2,1)S(1)}, bf16[128,3584]{1,0:T(8,128)(2,1)S(1)}, u32[]{:S(2)}, u32[]{:S(2)}) collective-permute-start(bf16[128,3584]{1,0:T(8,128)(2,1)S(1)} %pad_maximum_fusion), channel_id=1, source_target_pairs={{0,1},{1,0},{2,3},{3,2},{4,5},{5,4},{6,7},{7,6},{8,9},{9,8},{10,11... | collective-permute-start | bytes 2752520 | tf_op jit(solution)/shard_map/ppermute | solution.py:316
  15.3 1.9 collective-permute-start
  78.1 9.8 %collective-permute-start.2 = (bf16[640,3584]{1,0:T(8,128)(2,1)}, bf16[640,3584]{1,0:T(8,128)(2,1)}, u32[]{:S(2)}, u32[]{:S(2)}) collective-permute-start(bf16[640,3584]{1,0:T(8,128)(2,1)} %bitcast.6.x_ref.y_ref), channel_id=1, source_target_pairs={{0,1},{1,0},{2,3},{3,2},{4,5},{5,4},{6,7},{7,6},{8,9},{9,8},{10,11... | collective-permute-start | bytes 13762568 | tf_op jit(solution)/shard_map/ppermute | solution.py:334
  81.3 6.6 %copy-start.5 = (bf16[3584,768]{1,0:T(8,128)(2,1)S(1)}, bf16[3584,768]{1,0:T(8,128)(2,1)}, u32[]{:S(2)}) copy-start(bf16[3584,768]{1,0:T(8,128)(2,1)} %all-gather.2.cloned.1.call-done.w_ref.w_m_ref) | copy-start | bytes 16515076
  87.9 11.1 %collective-permute-start.3 = (bf16[3584,768]{1,0:T(8,128)(2,1)S(1)}, bf16[3584,768]{1,0:T(8,128)(2,1)}, u32[]{:S(2)}, u32[]{:S(2)}) collective-permute-start(bf16[3584,768]{1,0:T(8,128)(2,1)S(1)} %copy-done.5), channel_id=1, source_target_pairs={{0,1},{1,0},{2,3},{3,2},{4,5},{5,4},{6,7},{7,6},{8,9},{9,8},{10,11... | collective-permute-start | bytes 16515080 | tf_op jit(solution)/shard_map/ppermute | solution.py:339
  99.0 5.7 %collective-permute-start.4 = (bf16[640,768]{1,0:T(8,128)(2,1)}, bf16[640,768]{1,0:T(8,128)(2,1)S(1)}, u32[]{:S(2)}, u32[]{:S(2)}) collective-permute-start(bf16[640,768]{1,0:T(8,128)(2,1)} %get-tuple-element.45.deriv_ref.deriv_m_ref), channel_id=1, source_target_pairs={{0,1},{1,0},{2,3},{3,2},{4,5},{5,4},{6,7},{7,6},{8,9},{9,8},{10,11... | collective-permute-start | bytes 2949128 | tf_op jit(solution)/shard_map/ppermute | solution.py:342
  104.7 1.2 copy-start
  175.1 5.8 %copy-start.2 = (bf16[2,448,256]{2,1,0:T(8,128)(2,1)S(1)}, bf16[2,448,256]{2,1,0:T(8,128)(2,1)}, u32[]{:S(2)}) copy-start(bf16[2,448,256]{2,1,0:T(8,128)(2,1)} %up_ref.1) | copy-start | bytes 1376260
  178.1 6.3 %collective-permute-start.5 = (bf16[128,3584]{1,0:T(8,128)(2,1)}, bf16[128,3584]{1,0:T(8,128)(2,1)S(1)}, u32[]{:S(2)}, u32[]{:S(2)}) collective-permute-start(bf16[128,3584]{1,0:T(8,128)(2,1)} %get-tuple-element.50), channel_id=1, source_target_pairs={{0,1},{1,0},{2,3},{3,2},{4,5},{5,4},{6,7},{7,6},{8,9},{9,8},{10,11... | collective-permute-start | bytes 2752520 | tf_op jit(solution)/shard_map/ppermute | solution.py:354
  180.8 3.6 %copy-start.4 = (bf16[256,448]{0,1:T(8,128)(2,1)S(1)}, bf16[256,448]{0,1:T(8,128)(2,1)}, u32[]{:S(2)}) copy-start(bf16[256,448]{0,1:T(8,128)(2,1)} %param.15) | copy-start | bytes 688132
  180.9 3.6 %copy-start.7 = (f32[256,448]{0,1:T(8,128)S(1)}, f32[256,448]{0,1:T(8,128)}, u32[]{:S(2)}) copy-start(f32[256,448]{0,1:T(8,128)} %param.18) | copy-start | bytes 1376260
  180.9 3.6 %copy-start.8 = (f32[256,448]{0,1:T(8,128)S(1)}, f32[256,448]{0,1:T(8,128)}, u32[]{:S(2)}) copy-start(f32[256,448]{0,1:T(8,128)} %param.19) | copy-start | bytes 1376260
Sparse Core Ops, SparseCore 0:
  10.4 70.9 all-gather.1
  104.8 66.0 reduce-scatter.1

commit v7 on v6

--- a/solution.py
+++ b/solution.py
@@ -46,10 +46,19 @@
 
 
 MIB = 1 << 20
+UPDATE_BLOCKS = 4
 FIRST_VMEM = 56
 VMEM = 56
-BACK_VMEM = 50
+BACK_VMEM = 28
 LANES = 128
+
+
+def in_hbm(array):
+    return pltpu.with_memory_space_constraint(array, pltpu.HBM)
+
+
+def in_vmem(array):
+    return pltpu.with_memory_space_constraint(array, pltpu.VMEM)
 
 
 def call(body, grid, in_specs, out_specs, out_shape, flops, scratch=(), vmem=VMEM, size=12 * MIB):
@@ -84,7 +93,7 @@
         pl.BlockSpec((rows, 3 * hid), lambda i: (0, 0)),
         jax.ShapeDtypeStruct((rows, 3 * hid), up.dtype),
         flops=up.size,
-        vmem=8,
+        vmem=56,
     )(up, down)
 
 
@@ -109,11 +118,11 @@
             pl.BlockSpec((cols, 3 * hid), lambda i: (i, 0)),
         ],
         pl.BlockSpec((n, 3 * hid), lambda i: (0, 0)),
-        jax.ShapeDtypeStruct((n, 3 * hid), jnp.float32),
+        pltpu.VMEM((n, 3 * hid), jnp.float32),
         flops=n * hid,
         vmem=FIRST_VMEM,
         size=MIB >> 4,
-    )(rows, rows, weights)
+    )(in_hbm(rows), in_hbm(rows), in_hbm(weights))
 
 
 def write_grads(hid, x, y, deriv_ref, grad_ref):
@@ -168,12 +177,12 @@
             pl.BlockSpec((cols, 3 * hid), lambda i: (blocks + jnp.minimum(blocks - 1, 2 * blocks - 1 - i), 0)),
         ],
         [
-            jax.ShapeDtypeStruct((n, 3 * hid), jnp.bfloat16),
-            jax.ShapeDtypeStruct((width, 3 * hid), jnp.bfloat16),
+            pltpu.VMEM((n, 3 * hid), jnp.bfloat16),
+            pltpu.HBM((width, 3 * hid), jnp.bfloat16),
         ],
         flops=6 * n * width * hid,
         scratch=[pltpu.VMEM((n, 3 * hid), jnp.float32)],
-    )(pre, rows, rows, weights)
+    )(in_vmem(pre), in_hbm(rows), in_hbm(rows), in_hbm(weights))
 
 
 def grad_body(hid, x_ref, y_ref, deriv_ref, _, grad_ref):
@@ -193,11 +202,11 @@
             pl.BlockSpec(memory_space=pl.ANY),
         ],
         out_specs=pl.BlockSpec((cols, 3 * hid), lambda i: (i, 0)),
-        out_shape=jax.ShapeDtypeStruct((width, 3 * hid), jnp.bfloat16),
+        out_shape=pltpu.HBM((width, 3 * hid), jnp.bfloat16),
         input_output_aliases={3: 0},
         compiler_params=pltpu.CompilerParams(vmem_limit_bytes=VMEM * MIB),
         cost_estimate=pl.CostEstimate(flops=3 * n * width * hid, bytes_accessed=12 * MIB, transcendentals=0),
-    )(rows, rows, deriv, grad)
+    )(in_hbm(rows), in_hbm(rows), in_vmem(deriv), in_hbm(grad))
 
 
 def back_body(hid, deriv_m_ref, deriv_o_ref, w_m_ref, w_o_ref, back_ref):
@@ -229,10 +238,10 @@
             pl.BlockSpec((cols, 3 * hid), lambda i: (blocks + lax.div(i, 2), 0)),
         ],
         pl.BlockSpec((n, cols), lambda i: (0, lax.div(i, 2) + blocks * lax.rem(i, 2))),
-        jax.ShapeDtypeStruct((n, width), jnp.bfloat16),
+        pltpu.VMEM((n, width), jnp.bfloat16),
         flops=6 * n * width * hid,
         vmem=BACK_VMEM,
-    )(deriv_m, deriv_o, w_m, w_o)
+    )(in_vmem(deriv_m), in_vmem(deriv_o), in_hbm(w_m), in_hbm(w_o))
 
 
 def unpack_body(pick_ref, gate_ref, back_ref, near_ref, far_ref):
@@ -261,6 +270,32 @@
         flops=4 * tokens * rows * half,
         vmem=20,
     )(pick, gate, back)
+
+
+def update_body(scale, grad_ref, wu_ref, mu_ref, vu_ref, wd_ref, md_ref, vd_ref, *out_refs):
+    hid = wd_ref.shape[1]
+    for k, (w_ref, m_ref, v_ref) in enumerate(((wu_ref, mu_ref, vu_ref),) * 2 + ((wd_ref, md_ref, vd_ref),)):
+        at = (k,) if k < 2 else ()
+        grad = grad_ref[:, k * hid : (k + 1) * hid].astype(jnp.float32)
+        new = adam_update(w_ref[at + (...,)], m_ref[at + (...,)], v_ref[at + (...,)], grad, scale)
+        for ref, value in zip(out_refs[:3] if k < 2 else out_refs[3:], new):
+            ref[at + (...,)] = value
+
+
+def updated(grad, up, down, scale, blocks):
+    rows, hid = down[0].shape
+    step = rows // blocks
+    up_spec = pl.BlockSpec((2, step, hid), lambda i: (0, i, 0))
+    down_spec = pl.BlockSpec((step, hid), lambda i: (i, 0))
+    return call(
+        functools.partial(update_body, scale),
+        blocks,
+        [pl.BlockSpec((step, 3 * hid), lambda i: (i, 0))] + [up_spec] * 3 + [down_spec] * 3,
+        [up_spec] * 3 + [down_spec] * 3,
+        [jax.ShapeDtypeStruct(a.shape, a.dtype) for a in (*up, *down)],
+        flops=60 * rows * hid,
+        vmem=56,
+    )(grad, *up, *down)
 
 
 def join_body(core_ref, near_ref, far_ref, out_ref, grad_ref):
@@ -344,7 +379,7 @@
     grad, deriv_o = lax.optimization_barrier((grad, deriv_o))
     grad = lax.psum_scatter(
         grad, ("z", "c"), scatter_dimension=0, tiled=True, axis_index_groups=orders
-    ).astype(jnp.float32)
+    )
 
     back = sent_back(deriv, deriv_o, weights, weights_o, hid, BLOCKS)
     back = lax.all_to_all(
@@ -353,9 +388,11 @@
     near, far = unpacked(unpick, gate2, back)
     far = lax.ppermute(far, "c", SWAP)
     scale = (tok_rows * n_data * n_chip * n_core * routes.shape[1] / EXPERTS) ** (-0.5)
-    grad_up = jnp.stack([grad[:, :hid], grad[:, hid : 2 * hid]])
-    new_wu, new_mu, new_vu = adam_update(w_gate_up, m_gate_up, v_gate_up, grad_up, scale)
-    new_wd, new_md, new_vd = adam_update(w_down, m_down, v_down, grad[:, 2 * hid :].T, scale)
+    new = updated(
+        grad, (w_gate_up, m_gate_up, v_gate_up), (w_down.T, m_down.T, v_down.T), scale, UPDATE_BLOCKS
+    )
+    new_wu, new_mu, new_vu = new[:3]
+    new_wd, new_md, new_vd = (a.T for a in new[3:])
     far, new_mu = lax.optimization_barrier((far, new_mu))
     outputs, input_grads = joined(c, near, far)
     return (outputs, input_grads, new_wu, new_mu, new_vu, new_wd, new_md, new_vd)

time: 194 us -> 187 us (0.964)
  other arithmetic: 7.59 us -> 1.7 us
  local copies, waits for them, and re-layouts: 3.54 us -> 0.34 us
    convert_element_type x3 -> x0, other arithmetic: 5.89 us -> none  [the longest x2 4.7 us: adam_update(): (weight.astype(jnp.float32) - learn_rate * update).astype(jnp.bfloat16)]
    pallas_call x0 -> x1, Pallas kernels: none -> 5.13 us  [updated(): call(functools.partial(update_body, scale), blocks, [pl.BlockSpec((step,...]
    unnamed x22 -> x6, local copies, waits for them, and re-layouts: 3.16 us -> 0.02 us
    pallas_call x1, Pallas kernels: 6.59 us -> 4.59 us  [first_half(): call(functools.partial(pre_body, hid), blocks, [pl.BlockSpec((n, cols), l...]
  transfers between devices with their start and end apart: 8 -> 8, of which waited for: 2 -> 4; matrix products, arithmetic and copies ran while one was open for 4% -> 2% of each run, Pallas kernels for 17% -> 18%
where the time goes in v7:
time: 187 us
  blocking collectives  120 us (64%)
  Pallas kernels  36.8 us (20%)
  between operations  14.2 us (8%)
  starting transfers between devices  7.44 us (4%)
  waiting for transfers between devices  4.57 us (2%)
    all_to_all x1, blocking collectives, shards(): lax.all_to_all(back.reshape(n_chip, block, width), 'p', split_axis=0, con...  60.9 us
    all_to_all x1, blocking collectives, shards(): got = lax.all_to_all(packed, 'p', split_axis=0, concat_axis=0, tiled=True)  59.4 us
    pallas_call x1, Pallas kernels, second_half(): call(functools.partial(mid_body, hid, blocks), 2 * blocks, [pl.BlockSpec(...  8.95 us
    pallas_call x1, Pallas kernels, sent_back(): call(functools.partial(back_body, hid), 2 * blocks, [deriv, deriv, pl.Blo...  7.21 us
    pallas_call x1, Pallas kernels, first_grads(): pl.pallas_call(functools.partial(grad_body, hid), grid=(blocks,), in_spec...  5.34 us
    pallas_call x1, Pallas kernels, updated(): call(functools.partial(update_body, scale), blocks, [pl.BlockSpec((step,...  5.13 us
    pallas_call x1, Pallas kernels, first_half(): call(functools.partial(pre_body, hid), blocks, [pl.BlockSpec((n, cols), l...  4.59 us
  transfers between devices with their start and end apart: 8, of which 4 were waited for; matrix products, arithmetic and copies ran while one was open for 2% of the time, Pallas kernels for 18%

profile of v7, /device:TPU:1, one launch (start us, length us, event | category | flops | bytes accessed | tf_op | source)
XLA Modules:
  0.0 187.0 jit_solution(17432959890318870540)
XLA Ops:
  7.2 0.0 copy-start
  7.2 0.0 all-gather.2.cloned.1.call-start
  7.2 2.0 %shard_map.161 = bf16[448,768]{1,0:T(8,128)(2,1)} custom-call(bf16[2,448,256]{2,1,0:T(8,128)(2,1)} %wu_ref.1, bf16[448,256]{1,0:T(8,128)(2,1)} %bitcast.22), custom_call_target="tpu_custom_call" | custom-call | flops 229376 | bytes 12582912 | tf_op jit(solution)/shard_map/pallas_call | solution.py:86
  9.3 0.0 all-gather.2.cloned.1.call-update
  9.3 0.0 reduce-scatter.2.cloned.1.call-start
  9.3 0.0 copy-start.2
  9.4 0.0 copy-start.1
  9.4 1.4 multiply_convert_fusion
  10.8 0.0 copy-done
  10.8 0.1 constant_dynamic-slice_fusion
  10.9 0.1 pad_maximum_fusion
  11.0 3.3 %collective-permute-start.1 = (bf16[128,3584]{1,0:T(8,128)(2,1)S(1)}, bf16[128,3584]{1,0:T(8,128)(2,1)S(1)}, u32[]{:S(2)}, u32[]{:S(2)}) collective-permute-start(bf16[128,3584]{1,0:T(8,128)(2,1)S(1)} %pad_maximum_fusion), channel_id=1, source_target_pairs={{0,1},{1,0},{2,3},{3,2},{4,5},{5,4},{6,7},{7,6},{8,9},{9,8},{10,11... | collective-permute-start | bytes 2752520 | tf_op jit(solution)/shard_map/ppermute | solution.py:351
  14.3 0.0 copy-done.2
  14.3 0.1 fusion.5
  14.5 0.0 copy-done.1
  14.5 0.1 collective-permute-start
  14.6 0.1 iota_add_fusion
  14.7 0.1 add.40
  14.8 1.6 collective-permute-done
  16.4 0.0 collective-permute-done.1
  16.4 1.4 convolution_convert_fusion
  17.9 59.4 %all_to_all.10 = bf16[16,40,3584]{2,1,0:T(8,128)(2,1)} all-to-all(bf16[16,40,3584]{2,1,0:T(8,128)(2,1)S(1)} %bitcast.21), channel_id=1, replica_groups=mesh['z'=8,'p'=16,'c'=2] {'p'}, dimensions={0} | all-to-all | bytes 9175040 | tf_op jit(solution)/shard_map/all_to_all | solution.py:364
  77.3 1.5 collective-permute-start.2
  78.8 0.1 compare_convert_fusion.pick_ref
  78.9 0.1 broadcast_in_dim.5.gate_ref
  79.0 2.3 %all-gather.2.cloned.1.call-done.w_ref.w_m_ref = bf16[3584,768]{1,0:T(8,128)(2,1)} async-done(((bf16[448,768]{1,0:T(8,128)(2,1)}), bf16[3584,768]{1,0:T(8,128)(2,1)}) %all-gather.2.cloned.1.call-update) | async-done | bytes 5505040 | tf_op jit(solution)/shard_map/all_gather | solution.py:340
  81.3 4.6 %shard_map.162.pre_ref = f32[640,768]{1,0:T(8,128)S(1)} custom-call(bf16[640,3584]{1,0:T(8,128)(2,1)} %bitcast.6.x_ref.y_ref, bf16[640,3584]{1,0:T(8,128)(2,1)} %bitcast.6.x_ref.y_ref, bf16[3584,768]{1,0:T(8,128)(2,1)} %all-gather.2.cloned.1.call-done.w_ref.w_m_ref), custom_call_target="tpu_custom_call" | custom-call | flops 163840 | bytes 65536 | tf_op jit(solution)/shard_map/pallas_call | solution.py:112
  85.9 0.6 collective-permute-done.2.x_ref.y_ref
  86.5 0.4 collective-permute-start.3
  86.9 8.9 %shard_map.163 = (bf16[640,768]{1,0:T(8,128)(2,1)S(1)}, bf16[3584,768]{1,0:T(8,128)(2,1)}) custom-call(f32[640,768]{1,0:T(8,128)S(1)} %shard_map.162.pre_ref, bf16[640,3584]{1,0:T(8,128)(2,1)} %collective-permute-done.2.x_ref.y_ref, bf16[640,3584]{1,0:T(8,128)(2,1)} %collective-permute-done.2.x_ref.y_ref, ...), custom_call_target="tpu_custom_call" | custom-call | flops 3523215360 | bytes 12582912 | tf_op jit(solution)/shard_map/pallas_call | solution.py:166
  95.8 0.1 collective-permute-done.3.w_o_ref
  95.9 0.4 collective-permute-start.4
  96.2 5.3 %shard_map.164 = bf16[3584,768]{1,0:T(8,128)(2,1)} custom-call(bf16[640,3584]{1,0:T(8,128)(2,1)} %bitcast.6.x_ref.y_ref, bf16[640,3584]{1,0:T(8,128)(2,1)} %bitcast.6.x_ref.y_ref, bf16[640,768]{1,0:T(8,128)(2,1)S(1)} %get-tuple-element.51.deriv_ref.deriv_m_ref, bf16[3584,768]{1,0:T(8,128)(2,1)} %get-tuple-element.52._), custom_call_target="tpu_custom_call", output_to_operand_aliasing={{}: (3, {})} | custom-call | flops 1761607680 | bytes 12582912 | tf_op jit(solution)/shard_map/pallas_call | solution.py:195
  101.6 0.0 collective-permute-done.4.deriv_o_ref
  101.6 0.0 reduce-scatter.2.cloned.1.call-update
  101.6 7.2 %shard_map.165 = bf16[640,3584]{1,0:T(8,128)(2,1)S(1)} custom-call(bf16[640,768]{1,0:T(8,128)(2,1)S(1)} %get-tuple-element.51.deriv_ref.deriv_m_ref, bf16[640,768]{1,0:T(8,128)(2,1)S(1)} %collective-permute-done.4.deriv_o_ref, bf16[3584,768]{1,0:T(8,128)(2,1)} %all-gather.2.cloned.1.call-done.w_ref.w_m_ref, bf16[3584,768]{1,0:T(8,128)(2,1)} %collective-permute-done.3.w_o_ref), custom_call_target="tpu_custom_call" | custom-call | flops 3523215360 | bytes 12582912 | tf_op jit(solution)/shard_map/pallas_call | solution.py:231
  108.8 60.9 %all_to_all.11 = bf16[16,40,3584]{2,1,0:T(8,128)(2,1)S(1)} all-to-all(bf16[16,40,3584]{2,1,0:T(8,128)(2,1)S(1)} %bitcast.19), channel_id=1, replica_groups=mesh['z'=8,'p'=16,'c'=2] {'p'}, dimensions={0} | all-to-all | bytes 9175040 | tf_op jit(solution)/shard_map/all_to_all | solution.py:385
  169.8 2.2 %shard_map.166 = (bf16[128,3584]{1,0:T(8,128)(2,1)S(1)}, bf16[128,3584]{1,0:T(8,128)(2,1)S(1)}) custom-call(bf16[256,640]{1,0:T(8,128)(2,1)S(1)} %compare_convert_fusion.pick_ref, f32[256,128]{1,0:T(8,128)S(1)} %broadcast_in_dim.5.gate_ref, bf16[640,3584]{1,0:T(8,128)(2,1)S(1)} %bitcast.20), custom_call_target="tpu_custom_call" | custom-call | flops 1174405120 | bytes 12582912 | tf_op jit(solution)/shard_map/pallas_call | solution.py:260
  172.0 1.6 collective-permute-start.5
  173.6 0.0 reduce-scatter.2.cloned.1.call-done.grad_ref
  173.6 5.1 %shard_map.167 = (bf16[2,448,256]{2,1,0:T(8,128)(2,1)}, f32[2,448,256]{2,1,0:T(8,128)}, f32[2,448,256]{2,1,0:T(8,128)}, bf16[448,256]{1,0:T(8,128)(2,1)}, f32[448,256]{1,0:T(8,128)}, /*index=5*/f32[448,256]{1,0:T(8,128)}) custom-call(bf16[448,768]{1,0:T(8,128)(2,1)} %reduce-scatter.2.cloned.1.call-done.grad_ref, bf16[2,448,256]{2,1,0:T(8,128)(2,1)} %wu_ref.1, ...), custom_call_target="tpu_custom_call" | custom-call | flops 6881280 | bytes 12582912 | tf_op jit(solution)/shard_map/pallas_call | solution.py:290
  178.8 0.0 collective-permute-done.5.far_ref
  178.8 1.3 shard_map.168
  (5 shorter events, 0.0 us)
Async XLA Ops:
  7.2 3.6 %copy-start = (bf16[128,3584]{1,0:T(8,128)(2,1)S(1)}, bf16[128,3584]{1,0:T(8,128)(2,1)}, u32[]{:S(2)}) copy-start(bf16[128,3584]{1,0:T(8,128)(2,1)} %param.10) | copy-start | bytes 2752516
  7.2 74.1 %all-gather.2.cloned.1.call-start = ((), (), s32[]{:S(2)}) async-start(), calls=%async_computation.3 | async-start | bytes 6193152 | tf_op jit(solution)/shard_map/all_gather | solution.py:340
  9.3 164.4 %reduce-scatter.2.cloned.1.call-start = ((), (), s32[]{:S(2)}) async-start(), calls=%async_computation.4 | async-start | bytes 6193152 | tf_op jit(solution)/shard_map/reduce_scatter | solution.py:380
  9.3 5.0 %copy-start.2 = (s32[128,1]{0,1:T(1,128)S(1)}, s32[128,1]{0,1:T(1,128)}, u32[]{:S(2)}) copy-start(s32[128,1]{0,1:T(1,128)} %param.12) | copy-start | bytes 1540
  9.4 5.1 %copy-start.1 = (f32[128,1]{0,1:T(1,128)S(1)}, f32[128,1]{0,1:T(1,128)}, u32[]{:S(2)}) copy-start(f32[128,1]{0,1:T(1,128)} %param.13) | copy-start | bytes 1540
  11.0 5.4 %collective-permute-start.1 = (bf16[128,3584]{1,0:T(8,128)(2,1)S(1)}, bf16[128,3584]{1,0:T(8,128)(2,1)S(1)}, u32[]{:S(2)}, u32[]{:S(2)}) collective-permute-start(bf16[128,3584]{1,0:T(8,128)(2,1)S(1)} %pad_maximum_fusion), channel_id=1, source_target_pairs={{0,1},{1,0},{2,3},{3,2},{4,5},{5,4},{6,7},{7,6},{8,9},{9,8},{10,11... | collective-permute-start | bytes 2752520 | tf_op jit(solution)/shard_map/ppermute | solution.py:351
  14.5 1.9 %collective-permute-start = (f32[128,2]{0,1:T(2,128)S(1)}, f32[128,2]{0,1:T(2,128)S(1)}, u32[]{:S(2)}, u32[]{:S(2)}) collective-permute-start(f32[128,2]{0,1:T(2,128)S(1)} %pad_maximum_fusion.2), channel_id=1, source_target_pairs={{0,1},{1,0},{2,3},{3,2},{4,5},{5,4},{6,7},{7,6},{8,9},{9,8},{10,11... | collective-permute-start | bytes 3080 | tf_op jit(solution)/shard_map/ppermute | solution.py:355
  77.3 9.2 %collective-permute-start.2 = (bf16[640,3584]{1,0:T(8,128)(2,1)}, bf16[640,3584]{1,0:T(8,128)(2,1)}, u32[]{:S(2)}, u32[]{:S(2)}) collective-permute-start(bf16[640,3584]{1,0:T(8,128)(2,1)} %bitcast.6.x_ref.y_ref), channel_id=1, source_target_pairs={{0,1},{1,0},{2,3},{3,2},{4,5},{5,4},{6,7},{7,6},{8,9},{9,8},{10,11... | collective-permute-start | bytes 13762568 | tf_op jit(solution)/shard_map/ppermute | solution.py:369
  86.5 9.4 %collective-permute-start.3 = (bf16[3584,768]{1,0:T(8,128)(2,1)}, bf16[3584,768]{1,0:T(8,128)(2,1)}, u32[]{:S(2)}, u32[]{:S(2)}) collective-permute-start(bf16[3584,768]{1,0:T(8,128)(2,1)} %all-gather.2.cloned.1.call-done.w_ref.w_m_ref), channel_id=1, source_target_pairs={{0,1},{1,0},{2,3},{3,2},{4,5},{5,4},{6,7},{7,6},{8,9},{9,8},{10,11... | collective-permute-start | bytes 16515080 | tf_op jit(solution)/shard_map/ppermute | solution.py:374
  95.9 5.7 %collective-permute-start.4 = (bf16[640,768]{1,0:T(8,128)(2,1)S(1)}, bf16[640,768]{1,0:T(8,128)(2,1)S(1)}, u32[]{:S(2)}, u32[]{:S(2)}) collective-permute-start(bf16[640,768]{1,0:T(8,128)(2,1)S(1)} %get-tuple-element.51.deriv_ref.deriv_m_ref), channel_id=1, source_target_pairs={{0,1},{1,0},{2,3},{3,2},{4,5},{5,4},{6,7},{7,6},{8,9},{9,8},{10,11... | collective-permute-start | bytes 2949128 | tf_op jit(solution)/shard_map/ppermute | solution.py:377
  172.0 6.8 %collective-permute-start.5 = (bf16[128,3584]{1,0:T(8,128)(2,1)S(1)}, bf16[128,3584]{1,0:T(8,128)(2,1)S(1)}, u32[]{:S(2)}, u32[]{:S(2)}) collective-permute-start(bf16[128,3584]{1,0:T(8,128)(2,1)S(1)} %get-tuple-element.56), channel_id=1, source_target_pairs={{0,1},{1,0},{2,3},{3,2},{4,5},{5,4},{6,7},{7,6},{8,9},{9,8},{10,11... | collective-permute-start | bytes 2752520 | tf_op jit(solution)/shard_map/ppermute | solution.py:389
Sparse Core Ops, SparseCore 0:
  10.4 70.8 all-gather.1
  101.7 66.2 reduce-scatter.1

commit v8 on v7

--- a/solution.py
+++ b/solution.py
@@ -46,7 +46,8 @@
 
 
 MIB = 1 << 20
-UPDATE_BLOCKS = 4
+UPDATE_BLOCKS = 2
+BACK_BLOCKS = 1
 FIRST_VMEM = 56
 VMEM = 56
 BACK_VMEM = 28
@@ -381,7 +382,7 @@
         grad, ("z", "c"), scatter_dimension=0, tiled=True, axis_index_groups=orders
     )
 
-    back = sent_back(deriv, deriv_o, weights, weights_o, hid, BLOCKS)
+    back = sent_back(deriv, deriv_o, weights, weights_o, hid, BACK_BLOCKS)
     back = lax.all_to_all(
         back.reshape(n_chip, block, width), "p", split_axis=0, concat_axis=0, tiled=True
     ).reshape(n_chip * block, width)

time: 187 us -> 186 us (level)
  transfers between devices with their start and end apart: 8 -> 8, of which waited for: 4 -> 4; matrix products, arithmetic and copies ran while one was open for 2% -> 2% of each run, Pallas kernels for 18% -> 17%
where the time goes in v8:
time: 186 us
  blocking collectives  120 us (65%)
  Pallas kernels  35.5 us (19%)
  between operations  14.2 us (8%)
  starting transfers between devices  7.46 us (4%)
  waiting for transfers between devices  4.57 us (2%)
    all_to_all x1, blocking collectives, shards(): lax.all_to_all(back.reshape(n_chip, block, width), 'p', split_axis=0, con...  60.9 us
    all_to_all x1, blocking collectives, shards(): got = lax.all_to_all(packed, 'p', split_axis=0, concat_axis=0, tiled=True)  59.4 us
    pallas_call x1, Pallas kernels, second_half(): call(functools.partial(mid_body, hid, blocks), 2 * blocks, [pl.BlockSpec(...  8.95 us
    pallas_call x1, Pallas kernels, sent_back(): call(functools.partial(back_body, hid), 2 * blocks, [deriv, deriv, pl.Blo...  6.99 us
    pallas_call x1, Pallas kernels, first_grads(): pl.pallas_call(functools.partial(grad_body, hid), grid=(blocks,), in_spec...  5.34 us
    pallas_call x1, Pallas kernels, first_half(): call(functools.partial(pre_body, hid), blocks, [pl.BlockSpec((n, cols), l...  4.59 us
    pallas_call x1, Pallas kernels, updated(): call(functools.partial(update_body, scale), blocks, [pl.BlockSpec((step,...  4 us
  transfers between devices with their start and end apart: 8, of which 4 were waited for; matrix products, arithmetic and copies ran while one was open for 2% of the time, Pallas kernels for 17%

profile of v8, /device:TPU:1, one launch (start us, length us, event | category | flops | bytes accessed | tf_op | source)
XLA Modules:
  0.0 185.6 jit_solution(15172862351330150482)
XLA Ops:
  7.2 0.0 copy-start
  7.2 0.0 all-gather.2.cloned.1.call-start
  7.2 2.0 %shard_map.161 = bf16[448,768]{1,0:T(8,128)(2,1)} custom-call(bf16[2,448,256]{2,1,0:T(8,128)(2,1)} %wu_ref.1, bf16[448,256]{1,0:T(8,128)(2,1)} %bitcast.22), custom_call_target="tpu_custom_call" | custom-call | flops 229376 | bytes 12582912 | tf_op jit(solution)/shard_map/pallas_call | solution.py:87
  9.3 0.0 all-gather.2.cloned.1.call-update
  9.3 0.0 reduce-scatter.2.cloned.1.call-start
  9.3 0.0 copy-start.2
  9.4 0.0 copy-start.1
  9.4 1.4 multiply_convert_fusion
  10.8 0.0 copy-done
  10.8 0.1 constant_dynamic-slice_fusion
  10.9 0.1 pad_maximum_fusion
  11.0 3.3 %collective-permute-start.1 = (bf16[128,3584]{1,0:T(8,128)(2,1)S(1)}, bf16[128,3584]{1,0:T(8,128)(2,1)S(1)}, u32[]{:S(2)}, u32[]{:S(2)}) collective-permute-start(bf16[128,3584]{1,0:T(8,128)(2,1)S(1)} %pad_maximum_fusion), channel_id=1, source_target_pairs={{0,1},{1,0},{2,3},{3,2},{4,5},{5,4},{6,7},{7,6},{8,9},{9,8},{10,11... | collective-permute-start | bytes 2752520 | tf_op jit(solution)/shard_map/ppermute | solution.py:352
  14.3 0.0 copy-done.2
  14.3 0.1 fusion.5
  14.5 0.0 copy-done.1
  14.5 0.1 collective-permute-start
  14.6 0.1 iota_add_fusion
  14.7 0.1 add.40
  14.8 1.6 collective-permute-done
  16.4 0.0 collective-permute-done.1
  16.4 1.4 convolution_convert_fusion
  17.8 59.4 %all_to_all.10 = bf16[16,40,3584]{2,1,0:T(8,128)(2,1)} all-to-all(bf16[16,40,3584]{2,1,0:T(8,128)(2,1)S(1)} %bitcast.21), channel_id=1, replica_groups=mesh['z'=8,'p'=16,'c'=2] {'p'}, dimensions={0} | all-to-all | bytes 9175040 | tf_op jit(solution)/shard_map/all_to_all | solution.py:365
  77.3 1.5 collective-permute-start.2
  78.8 0.1 compare_convert_fusion.pick_ref
  78.9 0.1 broadcast_in_dim.5.gate_ref
  79.0 2.3 %all-gather.2.cloned.1.call-done.w_ref.w_m_ref = bf16[3584,768]{1,0:T(8,128)(2,1)} async-done(((bf16[448,768]{1,0:T(8,128)(2,1)}), bf16[3584,768]{1,0:T(8,128)(2,1)}) %all-gather.2.cloned.1.call-update) | async-done | bytes 5505040 | tf_op jit(solution)/shard_map/all_gather | solution.py:341
  81.3 4.6 %shard_map.162.pre_ref = f32[640,768]{1,0:T(8,128)S(1)} custom-call(bf16[640,3584]{1,0:T(8,128)(2,1)} %bitcast.6.x_ref.y_ref, bf16[640,3584]{1,0:T(8,128)(2,1)} %bitcast.6.x_ref.y_ref, bf16[3584,768]{1,0:T(8,128)(2,1)} %all-gather.2.cloned.1.call-done.w_ref.w_m_ref), custom_call_target="tpu_custom_call" | custom-call | flops 163840 | bytes 65536 | tf_op jit(solution)/shard_map/pallas_call | solution.py:113
  85.9 0.6 collective-permute-done.2.x_ref.y_ref
  86.5 0.4 collective-permute-start.3
  86.9 8.9 %shard_map.163 = (bf16[640,768]{1,0:T(8,128)(2,1)S(1)}, bf16[3584,768]{1,0:T(8,128)(2,1)}) custom-call(f32[640,768]{1,0:T(8,128)S(1)} %shard_map.162.pre_ref, bf16[640,3584]{1,0:T(8,128)(2,1)} %collective-permute-done.2.x_ref.y_ref, bf16[640,3584]{1,0:T(8,128)(2,1)} %collective-permute-done.2.x_ref.y_ref, ...), custom_call_target="tpu_custom_call" | custom-call | flops 3523215360 | bytes 12582912 | tf_op jit(solution)/shard_map/pallas_call | solution.py:167
  95.8 0.1 collective-permute-done.3.w_o_ref
  95.9 0.4 collective-permute-start.4
  96.2 5.3 %shard_map.164 = bf16[3584,768]{1,0:T(8,128)(2,1)} custom-call(bf16[640,3584]{1,0:T(8,128)(2,1)} %bitcast.6.x_ref.y_ref, bf16[640,3584]{1,0:T(8,128)(2,1)} %bitcast.6.x_ref.y_ref, bf16[640,768]{1,0:T(8,128)(2,1)S(1)} %get-tuple-element.51.deriv_ref.deriv_m_ref, bf16[3584,768]{1,0:T(8,128)(2,1)} %get-tuple-element.52._), custom_call_target="tpu_custom_call", output_to_operand_aliasing={{}: (3, {})} | custom-call | flops 1761607680 | bytes 12582912 | tf_op jit(solution)/shard_map/pallas_call | solution.py:196
  101.6 0.0 collective-permute-done.4.deriv_o_ref
  101.6 0.0 reduce-scatter.2.cloned.1.call-update
  101.6 7.0 %shard_map.165 = bf16[640,3584]{1,0:T(8,128)(2,1)S(1)} custom-call(bf16[640,768]{1,0:T(8,128)(2,1)S(1)} %get-tuple-element.51.deriv_ref.deriv_m_ref, bf16[640,768]{1,0:T(8,128)(2,1)S(1)} %collective-permute-done.4.deriv_o_ref, bf16[3584,768]{1,0:T(8,128)(2,1)} %all-gather.2.cloned.1.call-done.w_ref.w_m_ref, bf16[3584,768]{1,0:T(8,128)(2,1)} %collective-permute-done.3.w_o_ref), custom_call_target="tpu_custom_call" | custom-call | flops 3523215360 | bytes 12582912 | tf_op jit(solution)/shard_map/pallas_call | solution.py:232
  108.6 60.9 %all_to_all.11 = bf16[16,40,3584]{2,1,0:T(8,128)(2,1)S(1)} all-to-all(bf16[16,40,3584]{2,1,0:T(8,128)(2,1)S(1)} %bitcast.19), channel_id=1, replica_groups=mesh['z'=8,'p'=16,'c'=2] {'p'}, dimensions={0} | all-to-all | bytes 9175040 | tf_op jit(solution)/shard_map/all_to_all | solution.py:386
  169.5 2.2 %shard_map.166 = (bf16[128,3584]{1,0:T(8,128)(2,1)S(1)}, bf16[128,3584]{1,0:T(8,128)(2,1)S(1)}) custom-call(bf16[256,640]{1,0:T(8,128)(2,1)S(1)} %compare_convert_fusion.pick_ref, f32[256,128]{1,0:T(8,128)S(1)} %broadcast_in_dim.5.gate_ref, bf16[640,3584]{1,0:T(8,128)(2,1)S(1)} %bitcast.20), custom_call_target="tpu_custom_call" | custom-call | flops 1174405120 | bytes 12582912 | tf_op jit(solution)/shard_map/pallas_call | solution.py:261
  171.8 1.7 collective-permute-start.5
  173.4 0.0 reduce-scatter.2.cloned.1.call-done.grad_ref
  173.4 4.0 %shard_map.167 = (bf16[2,448,256]{2,1,0:T(8,128)(2,1)}, f32[2,448,256]{2,1,0:T(8,128)}, f32[2,448,256]{2,1,0:T(8,128)}, bf16[448,256]{1,0:T(8,128)(2,1)}, f32[448,256]{1,0:T(8,128)}, /*index=5*/f32[448,256]{1,0:T(8,128)}) custom-call(bf16[448,768]{1,0:T(8,128)(2,1)} %reduce-scatter.2.cloned.1.call-done.grad_ref, bf16[2,448,256]{2,1,0:T(8,128)(2,1)} %wu_ref.1, ...), custom_call_target="tpu_custom_call" | custom-call | flops 6881280 | bytes 12582912 | tf_op jit(solution)/shard_map/pallas_call | solution.py:291
  177.4 0.0 collective-permute-done.5.far_ref
  177.4 1.3 shard_map.168
  (5 shorter events, 0.0 us)
Async XLA Ops:
  7.2 3.6 %copy-start = (bf16[128,3584]{1,0:T(8,128)(2,1)S(1)}, bf16[128,3584]{1,0:T(8,128)(2,1)}, u32[]{:S(2)}) copy-start(bf16[128,3584]{1,0:T(8,128)(2,1)} %param.10) | copy-start | bytes 2752516
  7.2 74.1 %all-gather.2.cloned.1.call-start = ((), (), s32[]{:S(2)}) async-start(), calls=%async_computation.3 | async-start | bytes 6193152 | tf_op jit(solution)/shard_map/all_gather | solution.py:341
  9.3 164.1 %reduce-scatter.2.cloned.1.call-start = ((), (), s32[]{:S(2)}) async-start(), calls=%async_computation.4 | async-start | bytes 6193152 | tf_op jit(solution)/shard_map/reduce_scatter | solution.py:381
  9.3 5.0 %copy-start.2 = (s32[128,1]{0,1:T(1,128)S(1)}, s32[128,1]{0,1:T(1,128)}, u32[]{:S(2)}) copy-start(s32[128,1]{0,1:T(1,128)} %param.12) | copy-start | bytes 1540
  9.4 5.1 %copy-start.1 = (f32[128,1]{0,1:T(1,128)S(1)}, f32[128,1]{0,1:T(1,128)}, u32[]{:S(2)}) copy-start(f32[128,1]{0,1:T(1,128)} %param.13) | copy-start | bytes 1540
  11.0 5.4 %collective-permute-start.1 = (bf16[128,3584]{1,0:T(8,128)(2,1)S(1)}, bf16[128,3584]{1,0:T(8,128)(2,1)S(1)}, u32[]{:S(2)}, u32[]{:S(2)}) collective-permute-start(bf16[128,3584]{1,0:T(8,128)(2,1)S(1)} %pad_maximum_fusion), channel_id=1, source_target_pairs={{0,1},{1,0},{2,3},{3,2},{4,5},{5,4},{6,7},{7,6},{8,9},{9,8},{10,11... | collective-permute-start | bytes 2752520 | tf_op jit(solution)/shard_map/ppermute | solution.py:352
  14.5 1.9 %collective-permute-start = (f32[128,2]{0,1:T(2,128)S(1)}, f32[128,2]{0,1:T(2,128)S(1)}, u32[]{:S(2)}, u32[]{:S(2)}) collective-permute-start(f32[128,2]{0,1:T(2,128)S(1)} %pad_maximum_fusion.2), channel_id=1, source_target_pairs={{0,1},{1,0},{2,3},{3,2},{4,5},{5,4},{6,7},{7,6},{8,9},{9,8},{10,11... | collective-permute-start | bytes 3080 | tf_op jit(solution)/shard_map/ppermute | solution.py:356
  77.3 9.2 %collective-permute-start.2 = (bf16[640,3584]{1,0:T(8,128)(2,1)}, bf16[640,3584]{1,0:T(8,128)(2,1)}, u32[]{:S(2)}, u32[]{:S(2)}) collective-permute-start(bf16[640,3584]{1,0:T(8,128)(2,1)} %bitcast.6.x_ref.y_ref), channel_id=1, source_target_pairs={{0,1},{1,0},{2,3},{3,2},{4,5},{5,4},{6,7},{7,6},{8,9},{9,8},{10,11... | collective-permute-start | bytes 13762568 | tf_op jit(solution)/shard_map/ppermute | solution.py:370
  86.5 9.4 %collective-permute-start.3 = (bf16[3584,768]{1,0:T(8,128)(2,1)}, bf16[3584,768]{1,0:T(8,128)(2,1)}, u32[]{:S(2)}, u32[]{:S(2)}) collective-permute-start(bf16[3584,768]{1,0:T(8,128)(2,1)} %all-gather.2.cloned.1.call-done.w_ref.w_m_ref), channel_id=1, source_target_pairs={{0,1},{1,0},{2,3},{3,2},{4,5},{5,4},{6,7},{7,6},{8,9},{9,8},{10,11... | collective-permute-start | bytes 16515080 | tf_op jit(solution)/shard_map/ppermute | solution.py:375
  95.9 5.7 %collective-permute-start.4 = (bf16[640,768]{1,0:T(8,128)(2,1)S(1)}, bf16[640,768]{1,0:T(8,128)(2,1)S(1)}, u32[]{:S(2)}, u32[]{:S(2)}) collective-permute-start(bf16[640,768]{1,0:T(8,128)(2,1)S(1)} %get-tuple-element.51.deriv_ref.deriv_m_ref), channel_id=1, source_target_pairs={{0,1},{1,0},{2,3},{3,2},{4,5},{5,4},{6,7},{7,6},{8,9},{9,8},{10,11... | collective-permute-start | bytes 2949128 | tf_op jit(solution)/shard_map/ppermute | solution.py:378
  171.8 5.7 %collective-permute-start.5 = (bf16[128,3584]{1,0:T(8,128)(2,1)S(1)}, bf16[128,3584]{1,0:T(8,128)(2,1)S(1)}, u32[]{:S(2)}, u32[]{:S(2)}) collective-permute-start(bf16[128,3584]{1,0:T(8,128)(2,1)S(1)} %get-tuple-element.56), channel_id=1, source_target_pairs={{0,1},{1,0},{2,3},{3,2},{4,5},{5,4},{6,7},{7,6},{8,9},{9,8},{10,11... | collective-permute-start | bytes 2752520 | tf_op jit(solution)/shard_map/ppermute | solution.py:390
Sparse Core Ops, SparseCore 0:
  10.4 70.8 all-gather.1
  101.7 66.2 reduce-scatter.1

commit v9 on v8

--- a/solution.py
+++ b/solution.py
@@ -309,13 +309,13 @@
 
 
 def joined(core, near, far):
-    whole = pl.BlockSpec(near.shape, lambda i: (0, 0))
+    rows = pl.BlockSpec((near.shape[0] // 2, near.shape[1]), lambda i: (i, 0))
     shape = jax.ShapeDtypeStruct(near.shape, jnp.bfloat16)
     return call(
         join_body,
-        1,
-        [pl.BlockSpec(memory_space=pltpu.SMEM), whole, whole],
-        [whole, whole],
+        2,
+        [pl.BlockSpec(memory_space=pltpu.SMEM), rows, rows],
+        [rows, rows],
         [shape, shape],
         flops=near.size,
         vmem=20,

time: 186 us -> 186 us (level)
  no operation moved by 1% of the time
where the time goes in v9:
time: 186 us
  blocking collectives  120 us (65%)
  Pallas kernels  35.5 us (19%)
  between operations  14.2 us (8%)
  starting transfers between devices  7.46 us (4%)
  waiting for transfers between devices  4.57 us (2%)
    all_to_all x1, blocking collectives, shards(): lax.all_to_all(back.reshape(n_chip, block, width), 'p', split_axis=0, con...  60.9 us
    all_to_all x1, blocking collectives, shards(): got = lax.all_to_all(packed, 'p', split_axis=0, concat_axis=0, tiled=True)  59.4 us
    pallas_call x1, Pallas kernels, second_half(): call(functools.partial(mid_body, hid, blocks), 2 * blocks, [pl.BlockSpec(...  8.95 us
    pallas_call x1, Pallas kernels, sent_back(): call(functools.partial(back_body, hid), 2 * blocks, [deriv, deriv, pl.Blo...  6.99 us
    pallas_call x1, Pallas kernels, first_grads(): pl.pallas_call(functools.partial(grad_body, hid), grid=(blocks,), in_spec...  5.34 us
    pallas_call x1, Pallas kernels, first_half(): call(functools.partial(pre_body, hid), blocks, [pl.BlockSpec((n, cols), l...  4.59 us
    pallas_call x1, Pallas kernels, updated(): call(functools.partial(update_body, scale), blocks, [pl.BlockSpec((step,...  4 us
  transfers between devices with their start and end apart: 8, of which 4 were waited for; matrix products, arithmetic and copies ran while one was open for 2% of the time, Pallas kernels for 17%

profile of v9, /device:TPU:1, one launch (start us, length us, event | category | flops | bytes accessed | tf_op | source)
XLA Modules:
  0.0 185.6 jit_solution(287687856156596520)
XLA Ops:
  7.2 0.0 copy-start
  7.2 0.0 all-gather.2.cloned.1.call-start
  7.2 2.0 %shard_map.161 = bf16[448,768]{1,0:T(8,128)(2,1)} custom-call(bf16[2,448,256]{2,1,0:T(8,128)(2,1)} %wu_ref.1, bf16[448,256]{1,0:T(8,128)(2,1)} %bitcast.22), custom_call_target="tpu_custom_call" | custom-call | flops 229376 | bytes 12582912 | tf_op jit(solution)/shard_map/pallas_call | solution.py:87
  9.3 0.0 all-gather.2.cloned.1.call-update
  9.3 0.0 reduce-scatter.2.cloned.1.call-start
  9.3 0.0 copy-start.2
  9.4 0.0 copy-start.1
  9.4 1.4 multiply_convert_fusion
  10.8 0.0 copy-done
  10.8 0.1 constant_dynamic-slice_fusion
  10.9 0.1 pad_maximum_fusion
  11.0 3.3 %collective-permute-start.1 = (bf16[128,3584]{1,0:T(8,128)(2,1)S(1)}, bf16[128,3584]{1,0:T(8,128)(2,1)S(1)}, u32[]{:S(2)}, u32[]{:S(2)}) collective-permute-start(bf16[128,3584]{1,0:T(8,128)(2,1)S(1)} %pad_maximum_fusion), channel_id=1, source_target_pairs={{0,1},{1,0},{2,3},{3,2},{4,5},{5,4},{6,7},{7,6},{8,9},{9,8},{10,11... | collective-permute-start | bytes 2752520 | tf_op jit(solution)/shard_map/ppermute | solution.py:352
  14.3 0.0 copy-done.2
  14.3 0.1 fusion.5
  14.5 0.0 copy-done.1
  14.5 0.1 collective-permute-start
  14.6 0.1 iota_add_fusion
  14.7 0.1 add.40
  14.8 1.6 collective-permute-done
  16.4 0.0 collective-permute-done.1
  16.4 1.4 convolution_convert_fusion
  17.8 59.4 %all_to_all.10 = bf16[16,40,3584]{2,1,0:T(8,128)(2,1)} all-to-all(bf16[16,40,3584]{2,1,0:T(8,128)(2,1)S(1)} %bitcast.21), channel_id=1, replica_groups=mesh['z'=8,'p'=16,'c'=2] {'p'}, dimensions={0} | all-to-all | bytes 9175040 | tf_op jit(solution)/shard_map/all_to_all | solution.py:365
  77.3 1.5 collective-permute-start.2
  78.8 0.1 compare_convert_fusion.pick_ref
  78.9 0.1 broadcast_in_dim.5.gate_ref
  79.0 2.3 %all-gather.2.cloned.1.call-done.w_ref.w_m_ref = bf16[3584,768]{1,0:T(8,128)(2,1)} async-done(((bf16[448,768]{1,0:T(8,128)(2,1)}), bf16[3584,768]{1,0:T(8,128)(2,1)}) %all-gather.2.cloned.1.call-update) | async-done | bytes 5505040 | tf_op jit(solution)/shard_map/all_gather | solution.py:341
  81.3 4.6 %shard_map.162.pre_ref = f32[640,768]{1,0:T(8,128)S(1)} custom-call(bf16[640,3584]{1,0:T(8,128)(2,1)} %bitcast.6.x_ref.y_ref, bf16[640,3584]{1,0:T(8,128)(2,1)} %bitcast.6.x_ref.y_ref, bf16[3584,768]{1,0:T(8,128)(2,1)} %all-gather.2.cloned.1.call-done.w_ref.w_m_ref), custom_call_target="tpu_custom_call" | custom-call | flops 163840 | bytes 65536 | tf_op jit(solution)/shard_map/pallas_call | solution.py:113
  85.9 0.6 collective-permute-done.2.x_ref.y_ref
  86.5 0.4 collective-permute-start.3
  86.9 8.9 %shard_map.163 = (bf16[640,768]{1,0:T(8,128)(2,1)S(1)}, bf16[3584,768]{1,0:T(8,128)(2,1)}) custom-call(f32[640,768]{1,0:T(8,128)S(1)} %shard_map.162.pre_ref, bf16[640,3584]{1,0:T(8,128)(2,1)} %collective-permute-done.2.x_ref.y_ref, bf16[640,3584]{1,0:T(8,128)(2,1)} %collective-permute-done.2.x_ref.y_ref, ...), custom_call_target="tpu_custom_call" | custom-call | flops 3523215360 | bytes 12582912 | tf_op jit(solution)/shard_map/pallas_call | solution.py:167
  95.8 0.1 collective-permute-done.3.w_o_ref
  95.9 0.4 collective-permute-start.4
  96.2 5.3 %shard_map.164 = bf16[3584,768]{1,0:T(8,128)(2,1)} custom-call(bf16[640,3584]{1,0:T(8,128)(2,1)} %bitcast.6.x_ref.y_ref, bf16[640,3584]{1,0:T(8,128)(2,1)} %bitcast.6.x_ref.y_ref, bf16[640,768]{1,0:T(8,128)(2,1)S(1)} %get-tuple-element.51.deriv_ref.deriv_m_ref, bf16[3584,768]{1,0:T(8,128)(2,1)} %get-tuple-element.52._), custom_call_target="tpu_custom_call", output_to_operand_aliasing={{}: (3, {})} | custom-call | flops 1761607680 | bytes 12582912 | tf_op jit(solution)/shard_map/pallas_call | solution.py:196
  101.6 0.0 collective-permute-done.4.deriv_o_ref
  101.6 0.0 reduce-scatter.2.cloned.1.call-update
  101.6 7.0 %shard_map.165 = bf16[640,3584]{1,0:T(8,128)(2,1)S(1)} custom-call(bf16[640,768]{1,0:T(8,128)(2,1)S(1)} %get-tuple-element.51.deriv_ref.deriv_m_ref, bf16[640,768]{1,0:T(8,128)(2,1)S(1)} %collective-permute-done.4.deriv_o_ref, bf16[3584,768]{1,0:T(8,128)(2,1)} %all-gather.2.cloned.1.call-done.w_ref.w_m_ref, bf16[3584,768]{1,0:T(8,128)(2,1)} %collective-permute-done.3.w_o_ref), custom_call_target="tpu_custom_call" | custom-call | flops 3523215360 | bytes 12582912 | tf_op jit(solution)/shard_map/pallas_call | solution.py:232
  108.6 60.9 %all_to_all.11 = bf16[16,40,3584]{2,1,0:T(8,128)(2,1)S(1)} all-to-all(bf16[16,40,3584]{2,1,0:T(8,128)(2,1)S(1)} %bitcast.19), channel_id=1, replica_groups=mesh['z'=8,'p'=16,'c'=2] {'p'}, dimensions={0} | all-to-all | bytes 9175040 | tf_op jit(solution)/shard_map/all_to_all | solution.py:386
  169.5 2.2 %shard_map.166 = (bf16[128,3584]{1,0:T(8,128)(2,1)S(1)}, bf16[128,3584]{1,0:T(8,128)(2,1)S(1)}) custom-call(bf16[256,640]{1,0:T(8,128)(2,1)S(1)} %compare_convert_fusion.pick_ref, f32[256,128]{1,0:T(8,128)S(1)} %broadcast_in_dim.5.gate_ref, bf16[640,3584]{1,0:T(8,128)(2,1)S(1)} %bitcast.20), custom_call_target="tpu_custom_call" | custom-call | flops 1174405120 | bytes 12582912 | tf_op jit(solution)/shard_map/pallas_call | solution.py:261
  171.8 1.7 collective-permute-start.5
  173.4 0.0 reduce-scatter.2.cloned.1.call-done.grad_ref
  173.4 4.0 %shard_map.167 = (bf16[2,448,256]{2,1,0:T(8,128)(2,1)}, f32[2,448,256]{2,1,0:T(8,128)}, f32[2,448,256]{2,1,0:T(8,128)}, bf16[448,256]{1,0:T(8,128)(2,1)}, f32[448,256]{1,0:T(8,128)}, /*index=5*/f32[448,256]{1,0:T(8,128)}) custom-call(bf16[448,768]{1,0:T(8,128)(2,1)} %reduce-scatter.2.cloned.1.call-done.grad_ref, bf16[2,448,256]{2,1,0:T(8,128)(2,1)} %wu_ref.1, ...), custom_call_target="tpu_custom_call" | custom-call | flops 6881280 | bytes 12582912 | tf_op jit(solution)/shard_map/pallas_call | solution.py:291
  177.4 0.0 collective-permute-done.5.far_ref
  177.4 1.3 shard_map.168
  (5 shorter events, 0.0 us)
Async XLA Ops:
  7.2 3.6 %copy-start = (bf16[128,3584]{1,0:T(8,128)(2,1)S(1)}, bf16[128,3584]{1,0:T(8,128)(2,1)}, u32[]{:S(2)}) copy-start(bf16[128,3584]{1,0:T(8,128)(2,1)} %param.10) | copy-start | bytes 2752516
  7.2 74.1 %all-gather.2.cloned.1.call-start = ((), (), s32[]{:S(2)}) async-start(), calls=%async_computation.3 | async-start | bytes 6193152 | tf_op jit(solution)/shard_map/all_gather | solution.py:341
  9.3 164.1 %reduce-scatter.2.cloned.1.call-start = ((), (), s32[]{:S(2)}) async-start(), calls=%async_computation.4 | async-start | bytes 6193152 | tf_op jit(solution)/shard_map/reduce_scatter | solution.py:381
  9.3 5.0 %copy-start.2 = (s32[128,1]{0,1:T(1,128)S(1)}, s32[128,1]{0,1:T(1,128)}, u32[]{:S(2)}) copy-start(s32[128,1]{0,1:T(1,128)} %param.12) | copy-start | bytes 1540
  9.4 5.1 %copy-start.1 = (f32[128,1]{0,1:T(1,128)S(1)}, f32[128,1]{0,1:T(1,128)}, u32[]{:S(2)}) copy-start(f32[128,1]{0,1:T(1,128)} %param.13) | copy-start | bytes 1540
  11.0 5.4 %collective-permute-start.1 = (bf16[128,3584]{1,0:T(8,128)(2,1)S(1)}, bf16[128,3584]{1,0:T(8,128)(2,1)S(1)}, u32[]{:S(2)}, u32[]{:S(2)}) collective-permute-start(bf16[128,3584]{1,0:T(8,128)(2,1)S(1)} %pad_maximum_fusion), channel_id=1, source_target_pairs={{0,1},{1,0},{2,3},{3,2},{4,5},{5,4},{6,7},{7,6},{8,9},{9,8},{10,11... | collective-permute-start | bytes 2752520 | tf_op jit(solution)/shard_map/ppermute | solution.py:352
  14.5 1.9 %collective-permute-start = (f32[128,2]{0,1:T(2,128)S(1)}, f32[128,2]{0,1:T(2,128)S(1)}, u32[]{:S(2)}, u32[]{:S(2)}) collective-permute-start(f32[128,2]{0,1:T(2,128)S(1)} %pad_maximum_fusion.2), channel_id=1, source_target_pairs={{0,1},{1,0},{2,3},{3,2},{4,5},{5,4},{6,7},{7,6},{8,9},{9,8},{10,11... | collective-permute-start | bytes 3080 | tf_op jit(solution)/shard_map/ppermute | solution.py:356
  77.3 9.2 %collective-permute-start.2 = (bf16[640,3584]{1,0:T(8,128)(2,1)}, bf16[640,3584]{1,0:T(8,128)(2,1)}, u32[]{:S(2)}, u32[]{:S(2)}) collective-permute-start(bf16[640,3584]{1,0:T(8,128)(2,1)} %bitcast.6.x_ref.y_ref), channel_id=1, source_target_pairs={{0,1},{1,0},{2,3},{3,2},{4,5},{5,4},{6,7},{7,6},{8,9},{9,8},{10,11... | collective-permute-start | bytes 13762568 | tf_op jit(solution)/shard_map/ppermute | solution.py:370
  86.5 9.4 %collective-permute-start.3 = (bf16[3584,768]{1,0:T(8,128)(2,1)}, bf16[3584,768]{1,0:T(8,128)(2,1)}, u32[]{:S(2)}, u32[]{:S(2)}) collective-permute-start(bf16[3584,768]{1,0:T(8,128)(2,1)} %all-gather.2.cloned.1.call-done.w_ref.w_m_ref), channel_id=1, source_target_pairs={{0,1},{1,0},{2,3},{3,2},{4,5},{5,4},{6,7},{7,6},{8,9},{9,8},{10,11... | collective-permute-start | bytes 16515080 | tf_op jit(solution)/shard_map/ppermute | solution.py:375
  95.9 5.7 %collective-permute-start.4 = (bf16[640,768]{1,0:T(8,128)(2,1)S(1)}, bf16[640,768]{1,0:T(8,128)(2,1)S(1)}, u32[]{:S(2)}, u32[]{:S(2)}) collective-permute-start(bf16[640,768]{1,0:T(8,128)(2,1)S(1)} %get-tuple-element.51.deriv_ref.deriv_m_ref), channel_id=1, source_target_pairs={{0,1},{1,0},{2,3},{3,2},{4,5},{5,4},{6,7},{7,6},{8,9},{9,8},{10,11... | collective-permute-start | bytes 2949128 | tf_op jit(solution)/shard_map/ppermute | solution.py:378
  171.8 5.7 %collective-permute-start.5 = (bf16[128,3584]{1,0:T(8,128)(2,1)S(1)}, bf16[128,3584]{1,0:T(8,128)(2,1)S(1)}, u32[]{:S(2)}, u32[]{:S(2)}) collective-permute-start(bf16[128,3584]{1,0:T(8,128)(2,1)S(1)} %get-tuple-element.56), channel_id=1, source_target_pairs={{0,1},{1,0},{2,3},{3,2},{4,5},{5,4},{6,7},{7,6},{8,9},{9,8},{10,11... | collective-permute-start | bytes 2752520 | tf_op jit(solution)/shard_map/ppermute | solution.py:390
Sparse Core Ops, SparseCore 0:
  10.4 70.8 all-gather.1
  101.7 66.2 reduce-scatter.1
